TPU v7x, 512 devices: a whole 4x4x16 slice. The times are simulated.
512 devices in a mesh: height: 16 (over x, y_lo, core), width: 16 (over z), head: 2 (over y_hi).
Axes of the slice: x: 4, y: 4 (y_hi: 2, y_lo: 2; y = y_hi * 2 + y_lo), z: 16, core: 2. Of those that a mesh axis runs over, the one named last changes fastest.
Arguments:
- tokens: bfloat16 [16, 32, 144, 1536], P('height', 'width'), may hold values from -6 to 6
- grad_out: bfloat16 [16, 32, 144, 1536], P('height', 'width'), may hold values from -6 to 6
- qkv_weight: bfloat16 [1536, 3, 768], P(('height', 'width'), None, 'head'), may hold values from -0.15625 to 0.15625
- out_weight: bfloat16 [1536, 768], P(('height', 'width'), 'head'), may hold values from -0.5 to 0.5
- q_gain: float32 [768], P('head'), may hold values from 0.5 to 2
- k_gain: float32 [768], P('head'), may hold values from 0.5 to 2
- key_valid: int32 [16, 32, 144], P('height', 'width'), may hold values from 0 to 1, as said below
Outputs:
- mixed: bfloat16 [16, 32, 144, 1536], P('height', 'width', None, 'head')
- grad_in: bfloat16 [16, 32, 144, 1536], P('height', 'width', None, 'head')
Inputs may be any that keep to these rules, and one draw needn't show every extreme that they name: key_valid is 0 only in the last row of tiles and in the last column of tiles. In a tile of the last row, each frame and column within the tile has its own count of valid rows, 1 to 5, and the rows from that count on are 0. In a tile of the last column, each frame and row within the tile has its own count of valid columns, 1 to 8, and the columns from that count on are 0. The first token of every tile is valid.
All inputs are finite; a program needn't handle non-finite values.
Results may differ from a plain program's by a relative error of at most 0.015.
Values may be sent and summed in bfloat16 or wider, within the bound.
No kernel may reach another device: no remote copies, remote signals or barrier semaphores. Data moves between devices by JAX's collectives and lax.ppermute only.
A program may use at most 128 MiB of HBM per device.

v0:
```python
import jax
import jax.numpy as jnp
from jax import lax
from jax.sharding import PartitionSpec as P

HEAD_DIM = 128


epsilon = 1e-06


def padded(x, sides, width):
    for axis, dim in sides:
        count, length = (lax.axis_size(axis), x.shape[dim])
        up = [(i, (i + 1) % count) for i in range(count - 1)]
        down = [(j, i) for i, j in up]
        last = lax.slice_in_dim(x, length - width, length, axis=dim)
        first = lax.slice_in_dim(x, 0, width, axis=dim)
        before = lax.ppermute(last, axis, up)
        after = lax.ppermute(first, axis, down)
        x = jnp.concatenate([before, x, after], axis=dim)
    return x


def norm_scale(raw_values, gain_vec):
    inverse = lax.rsqrt(jnp.mean(raw_values * raw_values, axis=-1, keepdims=True) + epsilon)
    return (raw_values * inverse * gain_vec, inverse)


def norm_backward(raw_values, inverse, gain_vec, upstream):
    weighted = gain_vec * upstream
    inner_mean = jnp.mean(weighted * raw_values, axis=-1, keepdims=True)
    return inverse * weighted - raw_values * inverse**3 * inner_mean


def windows(extended, tile_rows, tile_cols):
    return jnp.stack(
        [
            extended[row_step : row_step + tile_rows, col_step : col_step + tile_cols]
            for row_step in range(3)
            for col_step in range(3)
        ],
        axis=2,
    )


def fold_windows(windowed, tile_rows, tile_cols):
    total = jnp.zeros((tile_rows + 2, tile_cols + 2) + windowed.shape[3:], jnp.float32)
    for position in range(9):
        row_step, col_step = divmod(position, 3)
        total = total.at[row_step : row_step + tile_rows, col_step : col_step + tile_cols].add(
            windowed[:, :, position]
        )
    return total


def fold_along(values, along, length):
    middle = lax.slice_in_dim(values, 2, length + 2, axis=along)
    first_rim = lax.slice_in_dim(values, 0, 1, axis=along)
    last_rim = lax.slice_in_dim(values, length + 3, length + 4, axis=along)
    before = [(0, 0)] * values.ndim
    before[along] = (0, length - 1)
    behind = [(0, 0)] * values.ndim
    behind[along] = (length - 1, 0)
    return middle + jnp.pad(first_rim, before) + jnp.pad(last_rim, behind)


def attend(queries, win_keys, win_values, win_valid, upstream):
    factor = HEAD_DIM ** (-0.5)
    scores = (
        jnp.einsum("bqhe,bkhe->bhqk", queries, win_keys, preferred_element_type=jnp.float32)
        * factor
    )
    weights = jnp.exp(scores) * win_valid[:, None, None, :]
    attn_probs = weights / jnp.sum(weights, axis=-1, keepdims=True)
    attn_weights = attn_probs.astype(jnp.bfloat16)
    attended = jnp.einsum(
        "bhqk,bkhe->bqhe", attn_weights, win_values, preferred_element_type=jnp.float32
    ).astype(jnp.bfloat16)
    grad_probs = jnp.einsum(
        "bqhe,bkhe->bhqk", upstream, win_values, preferred_element_type=jnp.float32
    )
    grad_scores = attn_probs * (
        grad_probs - jnp.sum(attn_probs * grad_probs, axis=-1, keepdims=True)
    )
    grad_scores = grad_scores.astype(jnp.bfloat16)
    grad_values = jnp.einsum(
        "bhqk,bqhe->bkhe", attn_weights, upstream, preferred_element_type=jnp.float32
    )
    grad_keys = (
        jnp.einsum("bhqk,bqhe->bkhe", grad_scores, queries, preferred_element_type=jnp.float32)
        * factor
    )
    grad_queries = (
        jnp.einsum("bhqk,bkhe->bqhe", grad_scores, win_keys, preferred_element_type=jnp.float32)
        * factor
    )
    return (attended, grad_queries, grad_keys, grad_values)


def on_device(tokens, grad_out, qkv_weight, out_weight, q_gain, k_gain, key_valid):
    tile_rows, tile_cols, tile_tokens, model_width = tokens.shape
    head_count = q_gain.shape[0] // HEAD_DIM
    inner_width = head_count * HEAD_DIM
    token_count = tile_rows * tile_cols * tile_tokens
    tile_count = tile_rows * tile_cols
    whole_qkv, whole_out = (
        lax.all_gather(qkv_weight, ("height", "width"), axis=0, tiled=True),
        lax.all_gather(out_weight, ("height", "width"), axis=0, tiled=True),
    )
    projected = jnp.dot(
        tokens.reshape(token_count, model_width),
        whole_qkv.reshape(model_width, 3 * inner_width),
        preferred_element_type=jnp.float32,
    ).reshape(token_count, 3, head_count, HEAD_DIM)
    q_gains = q_gain.reshape(head_count, HEAD_DIM)
    k_gains = k_gain.reshape(head_count, HEAD_DIM)
    q_normed, q_inverse = norm_scale(projected[:, 0], q_gains)
    k_normed, k_inverse = norm_scale(projected[:, 1], k_gains)
    shape_tiles = (tile_rows, tile_cols, tile_tokens, head_count, HEAD_DIM)
    queries = q_normed.astype(jnp.bfloat16).reshape(tile_count, tile_tokens, head_count, HEAD_DIM)
    keys_tiled = k_normed.astype(jnp.bfloat16).reshape(shape_tiles)
    values_tiled = projected[:, 2].astype(jnp.bfloat16).reshape(shape_tiles)
    keys_ext, values_ext, valid_ext = (
        padded(keys_tiled, (("height", 0), ("width", 1)), 1),
        padded(values_tiled, (("height", 0), ("width", 1)), 1),
        padded(key_valid.astype(jnp.bfloat16), (("height", 0), ("width", 1)), 1),
    )
    win_keys = windows(keys_ext, tile_rows, tile_cols).reshape(
        tile_count, 9 * tile_tokens, head_count, HEAD_DIM
    )
    win_values = windows(values_ext, tile_rows, tile_cols).reshape(
        tile_count, 9 * tile_tokens, head_count, HEAD_DIM
    )
    win_valid = (
        windows(valid_ext, tile_rows, tile_cols)
        .reshape(tile_count, 9 * tile_tokens)
        .astype(jnp.float32)
    )
    grad_attended = jnp.dot(
        grad_out.reshape(token_count, model_width), whole_out, preferred_element_type=jnp.float32
    )
    grad_attended = grad_attended.astype(jnp.bfloat16).reshape(
        tile_count, tile_tokens, head_count, HEAD_DIM
    )
    attended, grad_queries, grad_keys_win, grad_values_win = attend(
        queries, win_keys, win_values, win_valid, grad_attended
    )
    win_shape = (tile_rows, tile_cols, 9, tile_tokens, head_count, HEAD_DIM)
    keys_back = fold_windows(grad_keys_win.reshape(win_shape), tile_rows, tile_cols)
    values_back = fold_windows(grad_values_win.reshape(win_shape), tile_rows, tile_cols)
    keys_recv, values_recv = (
        padded(keys_back.astype(jnp.bfloat16), (("height", 0), ("width", 1)), 1).astype(
            keys_back.dtype
        ),
        padded(values_back.astype(jnp.bfloat16), (("height", 0), ("width", 1)), 1).astype(
            values_back.dtype
        ),
    )
    grad_keys = fold_along(fold_along(keys_recv, 0, tile_rows), 1, tile_cols)
    grad_values = fold_along(fold_along(values_recv, 0, tile_rows), 1, tile_cols)
    grad_q_raw = norm_backward(
        projected[:, 0], q_inverse, q_gains, grad_queries.reshape(token_count, head_count, HEAD_DIM)
    )
    grad_k_raw = norm_backward(
        projected[:, 1], k_inverse, k_gains, grad_keys.reshape(token_count, head_count, HEAD_DIM)
    )
    grad_qkv = jnp.stack(
        [grad_q_raw, grad_k_raw, grad_values.reshape(token_count, head_count, HEAD_DIM)], axis=1
    )
    grad_qkv = grad_qkv.reshape(token_count, 3, inner_width).astype(jnp.bfloat16)
    attended_rows = attended.reshape(token_count, inner_width)
    mixed_part = jnp.dot(attended_rows, whole_out.T, preferred_element_type=jnp.float32)
    mixed = lax.psum_scatter(
        mixed_part.astype(jnp.bfloat16), "head", scatter_dimension=1, tiled=True
    )
    grad_part = jnp.dot(
        grad_qkv.reshape(token_count, 3 * inner_width),
        whole_qkv.reshape(model_width, 3 * inner_width).T,
        preferred_element_type=jnp.float32,
    )
    grad_in = lax.psum_scatter(
        grad_part.astype(jnp.bfloat16), "head", scatter_dimension=1, tiled=True
    )
    out_shape = (tile_rows, tile_cols, tile_tokens, -1)
    return (mixed.reshape(out_shape), grad_in.reshape(out_shape))


def solution(mesh):
    placed = (
        P("height", "width", None, None),
        P("height", "width", None, None),
        P(("height", "width"), None, "head"),
        P(("height", "width"), "head"),
        P("head"),
        P("head"),
        P("height", "width", None),
    )
    return jax.shard_map(
        on_device,
        mesh=mesh,
        in_specs=placed,
        out_specs=(P("height", "width", None, "head"), P("height", "width", None, "head")),
        check_vma=False,
    )
```

profile of v0, /device:TPU:6, one launch (start us, length us, event | category | flops | bytes accessed | tf_op | source)
XLA Modules:
  0.0 1612.9 jit_solution(8500159153226415645)
XLA Ops:
  7.2 0.7 all-gather.6.cloned.1.call-update
  8.0 0.7 all-gather.4.cloned.1.call-update
  8.7 0.7 convert_element_type.105
  9.4 3.2 collective-permute-start.9
  12.6 1.9 collective-permute-start.8
  14.5 1.4 and_reduce_fusion
  15.9 0.7 fusion.101
  16.6 1.8 collective-permute-done.8
  18.4 3.8 collective-permute-start.10
  22.8 1.3 collective-permute-start.11
  24.2 4.1 collective-permute-done.11
  28.3 0.7 constant_dynamic-update-slice_fusion.4
  29.2 672.8 %all-gather.6.cloned.1.call-done = bf16[256,6,384]{2,1,0:T(8,128)(2,1)} async-done(((bf16[1,6,384]{2,1,0:T(8,128)(2,1)}), bf16[256,6,384]{2,1,0:T(8,128)(2,1)}) %all-gather.6.cloned.1.call-update) | async-done | bytes 1179664 | tf_op jit(solution)/shard_map/all_gather | solution.py:109
  702.0 3.3 reshape.1061
  705.3 715.7 %all-gather.4.cloned.1.call-done = bf16[1536,3,384]{2,1,0:T(4,128)(2,1)} async-done(((bf16[6,3,384]{2,1,0:T(4,128)(2,1)}), bf16[1536,3,384]{2,1,0:T(4,128)(2,1)}) %all-gather.4.cloned.1.call-update) | async-done | bytes 3538960 | tf_op jit(solution)/shard_map/all_gather | solution.py:108
  1421.0 8.0 copy.71
  1429.0 3.3 fusion.105
  1432.7 0.8 fusion.97
  1433.5 0.6 multiply_multiply_fusion
  1434.4 1.9 collective-permute-start.5
  1436.3 2.4 collective-permute-start.4
  1438.8 2.2 convolution_convert_fusion.1
  1441.0 4.1 collective-permute-start.1
  1445.1 1.9 collective-permute-start
  1447.3 1.3 collective-permute-start.6
  1448.6 4.7 collective-permute-done
  1453.4 1.3 collective-permute-start.3
  1454.7 4.6 collective-permute-start.2
  1459.3 1.5 collective-permute-start.7
  1460.8 13.0 collective-permute-done.7
  1474.3 1.4 copy.75
  1476.2 3.1 fusion.88
  1479.3 7.1 multiply_reduce_fusion
  1486.4 3.4 fusion.13
  1490.2 1.5 fusion.5
  1492.3 1.7 convolution_multiply_fusion
  1494.2 1.3 fusion.24
  1495.6 2.0 fusion.21
  1498.5 2.1 collective-permute-start.12
  1500.6 4.3 collective-permute-start.13
  1505.1 1.3 fusion.26
  1506.5 2.0 fusion.22
  1509.5 2.1 collective-permute-start.16
  1511.6 4.8 collective-permute-start.17
  1516.4 1.6 fusion.9
  1518.0 1.2 pad_maximum_fusion.15
  1519.2 6.5 collective-permute-start.14
  1525.7 1.3 collective-permute-start.15
  1527.0 1.2 pad_maximum_fusion.12
  1528.3 5.3 collective-permute-start.18
  1533.6 1.3 collective-permute-start.19
  1534.9 1.6 convolution_convert_fusion
  1536.5 1.0 copy.79
  1537.6 1.5 bitcast_multiply_fusion.1
  1539.1 4.3 collective-permute-done.15
  1543.4 1.7 fusion.4
  1545.2 1.7 collective-permute-done.18
  1546.9 4.9 collective-permute-done.19
  1551.8 1.6 fusion.3
  1554.1 0.7 copy-done.4
  1555.3 0.9 fusion.61
  1556.9 2.3 fusion
  1559.2 14.2 reduce-scatter.3.cloned.1.call-done
  1573.4 33.0 %reduce-scatter.5.cloned.1.call-done = bf16[288,768]{1,0:T(8,128)(2,1)} async-done(((bf16[288,1536]{1,0:T(8,128)(2,1)}), bf16[288,768]{1,0:T(8,128)(2,1)}) %reduce-scatter.5.cloned.1.call-update) | async-done | bytes 442384 | tf_op jit(solution)/shard_map/reduce_scatter | solution.py:182
  (145 shorter events, 8.0 us)
Async XLA Ops:
  7.2 1421.8 %copy-start = (bf16[1,2,144,1536]{3,2,1,0:T(8,128)(2,1)S(1)}, bf16[1,2,144,1536]{3,2,1,0:T(8,128)(2,1)}, u32[]{:S(2)}) copy-start(bf16[1,2,144,1536]{3,2,1,0:T(8,128)(2,1)} %param.43) | copy-start | bytes 2654212
  7.2 694.8 %all-gather.6.cloned.1.call-start = ((), (), s32[]{:S(2)}) async-start(), calls=%async_computation.5 | async-start | bytes 1579008 | tf_op jit(solution)/shard_map/all_gather | solution.py:109
  7.9 1413.1 %all-gather.4.cloned.1.call-start = ((), (), s32[]{:S(2)}) async-start(), calls=%async_computation.2 | async-start | bytes 4737024 | tf_op jit(solution)/shard_map/all_gather | solution.py:108
  8.7 1564.7 %reduce-scatter.3.cloned.1.call-start = ((), (), s32[]{:S(2)}) async-start(), calls=%async_computation.3 | async-start | bytes 1327104 | tf_op jit(solution)/shard_map/reduce_scatter | solution.py:174
  9.4 7.2 collective-permute-start.9
  12.6 5.8 collective-permute-start.8
  18.4 5.7 collective-permute-start.10
  22.8 5.5 collective-permute-start.11
  1432.3 8.7 copy-start.3
  1432.3 1.9 copy-start.17
  1434.4 12.7 collective-permute-start.5
  1436.3 10.8 collective-permute-start.4
  1441.0 7.6 collective-permute-start.1
  1445.1 8.2 collective-permute-start
  1447.3 13.5 collective-permute-start.6
  1453.4 22.3 %collective-permute-start.3 = (bf16[3,1,144,3,128]{4,2,1,3,0:T(8,128)(2,1)S(1)}, bf16[3,1,144,3,128]{4,2,1,3,0:T(8,128)(2,1)S(1)}, u32[]{:S(2)}, u32[]{:S(2)}) collective-permute-start(bf16[3,1,144,3,128]{4,2,1,3,0:T(8,128)(2,1)S(1)} %get-tuple-element.236), channel_id=1, source_target_pairs={{2,0},{4,2},{6,4},{8,6},{10,8},{12,10},{14,12},{16,14},{18,16},{20... | collective-permute-start | bytes 995336 | tf_op jit(solution)/shard_map/ppermute | solution.py:20
  1454.7 21.0 %collective-permute-start.2 = (bf16[3,1,144,3,128]{4,2,1,3,0:T(8,128)(2,1)S(1)}, bf16[3,1,144,3,128]{4,2,1,3,0:T(8,128)(2,1)S(1)}, u32[]{:S(2)}, u32[]{:S(2)}) collective-permute-start(bf16[3,1,144,3,128]{4,2,1,3,0:T(8,128)(2,1)S(1)} %get-tuple-element.237), channel_id=1, source_target_pairs={{0,2},{2,4},{4,6},{6,8},{8,10},{10,12},{12,14},{14,16},{16,18},{18... | collective-permute-start | bytes 995336 | tf_op jit(solution)/shard_map/ppermute | solution.py:19
  1459.3 14.5 collective-permute-start.7
  1476.1 3.1 copy-start.8
  1476.2 3.1 copy-start.15
  1486.4 3.8 copy-start.2
  1486.4 5.4 slice-start
  1490.2 1.6 slice-start.1
  1498.5 19.5 %collective-permute-start.12 = (bf16[1,4,144,3,128]{4,2,3,1,0:T(8,128)(2,1)S(1)}, bf16[1,4,144,3,128]{4,2,3,1,0:T(8,128)(2,1)S(1)}, u32[]{:S(2)}, u32[]{:S(2)}) collective-permute-start(bf16[1,4,144,3,128]{4,2,3,1,0:T(8,128)(2,1)S(1)} %get-tuple-element.228), channel_id=1, source_target_pairs={{0,32},{32,64},{64,96},{96,128},{128,160},{160,192},{192,224},{224... | collective-permute-start | bytes 1327112 | tf_op jit(solution)/shard_map/ppermute | solution.py:19
  1500.6 17.4 %collective-permute-start.13 = (bf16[1,4,144,3,128]{4,2,3,1,0:T(8,128)(2,1)S(1)}, bf16[1,4,144,3,128]{4,2,3,1,0:T(8,128)(2,1)S(1)}, u32[]{:S(2)}, u32[]{:S(2)}) collective-permute-start(bf16[1,4,144,3,128]{4,2,3,1,0:T(8,128)(2,1)S(1)} %get-tuple-element.229), channel_id=1, source_target_pairs={{32,0},{64,32},{96,64},{128,96},{160,128},{192,160},{224,192},{256... | collective-permute-start | bytes 1327112 | tf_op jit(solution)/shard_map/ppermute | solution.py:20
  1509.2 7.2 copy-start.5
  1509.5 17.5 %collective-permute-start.16 = (bf16[1,4,144,3,128]{4,2,3,1,0:T(8,128)(2,1)S(1)}, bf16[1,4,144,3,128]{4,2,3,1,0:T(8,128)(2,1)S(1)}, u32[]{:S(2)}, u32[]{:S(2)}) collective-permute-start(bf16[1,4,144,3,128]{4,2,3,1,0:T(8,128)(2,1)S(1)} %get-tuple-element.230), channel_id=1, source_target_pairs={{0,32},{32,64},{64,96},{96,128},{128,160},{160,192},{192,224},{224... | collective-permute-start | bytes 1327112 | tf_op jit(solution)/shard_map/ppermute | solution.py:19
  1511.6 15.4 collective-permute-start.17
  1518.0 10.3 copy-start.9
  1519.2 15.7 copy-start.6
  1519.2 19.9 %collective-permute-start.14 = (bf16[5,1,144,3,128]{4,2,3,1,0:T(8,128)(2,1)}, bf16[5,1,144,3,128]{4,2,3,1,0:T(8,128)(2,1)}, u32[]{:S(2)}, u32[]{:S(2)}) collective-permute-start(bf16[5,1,144,3,128]{4,2,3,1,0:T(8,128)(2,1)} %get-tuple-element.222), channel_id=1, source_target_pairs={{0,2},{2,4},{4,6},{6,8},{8,10},{10,12},{12,14},{14,16},{16,18},{18... | collective-permute-start | bytes 1658888 | tf_op jit(solution)/shard_map/ppermute | solution.py:19
  1525.7 17.7 %collective-permute-start.15 = (bf16[5,1,144,3,128]{4,2,3,1,0:T(8,128)(2,1)}, bf16[5,1,144,3,128]{4,2,3,1,0:T(8,128)(2,1)}, u32[]{:S(2)}, u32[]{:S(2)}) collective-permute-start(bf16[5,1,144,3,128]{4,2,3,1,0:T(8,128)(2,1)} %get-tuple-element.223), channel_id=1, source_target_pairs={{2,0},{4,2},{6,4},{8,6},{10,8},{12,10},{14,12},{16,14},{18,16},{20... | collective-permute-start | bytes 1658888 | tf_op jit(solution)/shard_map/ppermute | solution.py:20
  1527.0 9.5 copy-start.10
  1527.0 1.3 copy-start.12
  1528.3 18.6 %collective-permute-start.18 = (bf16[5,1,144,3,128]{4,2,3,1,0:T(8,128)(2,1)}, bf16[5,1,144,3,128]{4,2,3,1,0:T(8,128)(2,1)}, u32[]{:S(2)}, u32[]{:S(2)}) collective-permute-start(bf16[5,1,144,3,128]{4,2,3,1,0:T(8,128)(2,1)} %get-tuple-element.224), channel_id=1, source_target_pairs={{0,2},{2,4},{4,6},{6,8},{8,10},{10,12},{12,14},{14,16},{16,18},{18... | collective-permute-start | bytes 1658888 | tf_op jit(solution)/shard_map/ppermute | solution.py:19
  1533.6 18.2 %collective-permute-start.19 = (bf16[5,1,144,3,128]{4,2,3,1,0:T(8,128)(2,1)}, bf16[5,1,144,3,128]{4,2,3,1,0:T(8,128)(2,1)}, u32[]{:S(2)}, u32[]{:S(2)}) collective-permute-start(bf16[5,1,144,3,128]{4,2,3,1,0:T(8,128)(2,1)} %get-tuple-element.225), channel_id=1, source_target_pairs={{2,0},{4,2},{6,4},{8,6},{10,8},{12,10},{14,12},{16,14},{18,16},{20... | collective-permute-start | bytes 1658888 | tf_op jit(solution)/shard_map/ppermute | solution.py:20
  1537.6 68.8 %reduce-scatter.5.cloned.1.call-start = ((), (), s32[]{:S(2)}) async-start(), calls=%async_computation.4 | async-start | bytes 1327104 | tf_op jit(solution)/shard_map/reduce_scatter | solution.py:182
  1539.1 12.7 copy-start.11
  1539.1 12.7 copy-start.13
  1545.2 8.3 copy-start.21
  1553.5 1.3 copy-start.4
  1553.5 1.4 copy-start.14
  1553.5 1.4 copy-start.18
  1553.7 1.6 copy-start.16
  1553.7 1.6 copy-start.19
  1553.7 1.6 copy-start.20
  1554.9 2.0 copy-start.7
  1556.2 50.1 %copy-start.1 = (bf16[1,2,144,1536]{3,2,1,0:T(8,128)(2,1)S(1)}, bf16[1,2,144,1536]{3,2,1,0:T(8,128)(2,1)}, u32[]{:S(2)}) copy-start(bf16[1,2,144,1536]{3,2,1,0:T(8,128)(2,1)} %param.43) | copy-start | bytes 2654212
Sparse Core Ops, SparseCore 0:
  10.2 691.7 all-gather.5
  704.2 716.7 all-gather.3
  1537.7 35.6 reduce-scatter.2
  1576.6 29.6 reduce-scatter.4
where the time goes:
time: 1620 us; the launch traced here: 1610 us
  waiting for transfers between devices  1470 us (91%)
  starting transfers between devices  57 us (4%)
  matrix products  27.7 us (2%)
  other arithmetic  22.2 us (1%)
  local copies, waits for them, and re-layouts  19.6 us (1%)
    all_gather x1, waiting for transfers between devices, on_device(): lax.all_gather(qkv_weight, ('height', 'width'), axis=0, tiled=True)  716 us
    all_gather x1, waiting for transfers between devices, on_device(): lax.all_gather(out_weight, ('height', 'width'), axis=0, tiled=True)  673 us
    reduce_scatter x1, waiting for transfers between devices, on_device(): lax.psum_scatter(grad_part.astype(jnp.bfloat16), 'head', scatter_dimensio...  33 us
  transfers between devices with their start and end apart: 24, of which 11 were waited for; matrix products, arithmetic and copies ran while one was open for 2% of the time, Pallas kernels for 0%

commit v1 on v0

--- a/solution.py
+++ b/solution.py
@@ -104,10 +104,12 @@
     inner_width = head_count * HEAD_DIM
     token_count = tile_rows * tile_cols * tile_tokens
     tile_count = tile_rows * tile_cols
-    whole_qkv, whole_out = (
-        lax.all_gather(qkv_weight, ("height", "width"), axis=0, tiled=True),
-        lax.all_gather(out_weight, ("height", "width"), axis=0, tiled=True),
-    )
+    fan = 3 * inner_width
+    shard_rows = qkv_weight.shape[0]
+    joined = jnp.concatenate([qkv_weight.reshape(shard_rows, fan), out_weight], axis=1)
+    along_width = lax.all_gather(joined, "width", axis=0, tiled=True)
+    whole = lax.all_gather(along_width, "height", axis=0, tiled=True)
+    whole_qkv, whole_out = whole[:, :fan], whole[:, fan:]
     projected = jnp.dot(
         tokens.reshape(token_count, model_width),
         whole_qkv.reshape(model_width, 3 * inner_width),

time: 1620 us -> 278 us (0.17)
  waiting for transfers between devices: 1470 us -> 89.4 us
  blocking collectives: 0 us -> 37.7 us
    all_gather x2 -> x1, waiting for transfers between devices: 1390 us -> 24 us  [on_device(): whole = lax.all_gather(along_width, 'height', axis=0, tiled=True)]
    all_gather x0 -> x1, blocking collectives: none -> 37.7 us  [on_device(): along_width = lax.all_gather(joined, 'width', axis=0, tiled=True)]
  transfers between devices with their start and end apart: 24 -> 23, of which waited for: 11 -> 10; matrix products, arithmetic and copies ran while one was open for 2% -> 16% of each run, Pallas kernels for 0% -> 0%
where the time goes in v1:
time: 278 us; the launch traced here: 275 us
  waiting for transfers between devices  89.4 us (32%)
  starting transfers between devices  55.6 us (20%)
  blocking collectives  37.7 us (14%)
  matrix products  31 us (11%)
  other arithmetic  27.4 us (10%)
  local copies, waits for them, and re-layouts  19.6 us (7%)
  between operations  14.7 us (5%)
    all_gather x1, blocking collectives, on_device(): along_width = lax.all_gather(joined, 'width', axis=0, tiled=True)  37.7 us
    reduce_scatter x1, waiting for transfers between devices, on_device(): lax.psum_scatter(grad_part.astype(jnp.bfloat16), 'head', scatter_dimensio...  33.2 us
    ppermute x10, starting transfers between devices, padded(): before = lax.ppermute(last, axis, up)  29.7 us
    ppermute x10, starting transfers between devices, padded(): after = lax.ppermute(first, axis, down)  25.7 us
    all_gather x1, waiting for transfers between devices, on_device(): whole = lax.all_gather(along_width, 'height', axis=0, tiled=True)  24 us
    ppermute x10, waiting for transfers between devices, padded(): after = lax.ppermute(first, axis, down)  17.2 us
    ppermute x10, waiting for transfers between devices, padded(): before = lax.ppermute(last, axis, up)  8.7 us
    scatter-add x16, other arithmetic, fold_windows(): total.at[row_step:row_step + tile_rows, col_step:col_step + tile_cols]  7.59 us
  transfers between devices with their start and end apart: 23, of which 10 were waited for; matrix products, arithmetic and copies ran while one was open for 16% of the time, Pallas kernels for 0%

profile of v1, /device:TPU:6, one launch (start us, length us, event | category | flops | bytes accessed | tf_op | source)
XLA Modules:
  0.0 275.4 jit_solution(580131072214794566)
XLA Ops:
  8.7 37.7 %all-gather = bf16[16,6,1536]{2,1,0:T(8,128)(2,1)S(1)} all-gather(bf16[1,6,1536]{2,1,0:T(8,128)(2,1)S(1)} %maximum_bitcast_fusion.9), channel_id=1, replica_groups=mesh['height'=16,'width'=16,'head'=2] {'width'}, dimensions={0}, use_global_device_ids=true | all-gather | bytes 313344 | tf_op jit(solution)/shard_map/all_gather | solution.py:110
  46.4 0.8 reshape.1064
  48.0 1.9 collective-permute-start.9
  49.9 2.4 collective-permute-start.8
  52.3 1.4 and_reduce_fusion
  54.4 1.3 collective-permute-done.8
  55.7 1.5 collective-permute-start.10
  57.8 1.3 collective-permute-start.11
  59.2 4.1 %collective-permute-done.11 = bf16[3,1,144]{2,1,0:T(2,128)(2,1)S(1)} collective-permute-done((bf16[3,1,144]{2,1,0:T(2,128)(2,1)S(1)}, bf16[3,1,144]{2,1,0:T(2,128)(2,1)S(1)}, u32[]{:S(2)}, u32[]{:S(2)}) %collective-permute-start.11) | collective-permute-done | bytes 896 | tf_op jit(solution)/shard_map/ppermute | solution.py:20
  64.2 24.0 %all-gather.3.cloned.1.call-done = bf16[1536,1536]{1,0:T(8,128)(2,1)} async-done(((bf16[96,1536]{1,0:T(8,128)(2,1)}), bf16[1536,1536]{1,0:T(8,128)(2,1)}) %all-gather.3.cloned.1.call-update) | async-done | bytes 4718608 | tf_op jit(solution)/shard_map/all_gather | solution.py:111
  88.2 3.3 %fusion.4 = f32[288,1152]{1,0:T(8,128)S(1)} fusion(bf16[288,1536]{1,0:T(8,128)(2,1)S(1)} %bitcast.315, bf16[1536,1536]{1,0:T(8,128)(2,1)} %all-gather.3.cloned.1.call-done), kind=kOutput, calls=%fused_computation.8 | convolution fusion | flops 1019215872 | bytes 5750784 | tf_op jit(solution)/shard_map/dot_general | solution.py:113
  93.0 3.4 %collective-permute-start.1 = (bf16[1,2,144,3,128]{4,2,3,1,0:T(8,128)(2,1)}, bf16[1,2,144,3,128]{4,2,3,1,0:T(8,128)(2,1)}, u32[]{:S(2)}, u32[]{:S(2)}) collective-permute-start(bf16[1,2,144,3,128]{4,2,3,1,0:T(8,128)(2,1)} %copy.110), channel_id=1, source_target_pairs={{32,0},{64,32},{96,64},{128,96},{160,128},{192,160},{224,192},{256... | collective-permute-start | bytes 663560 | tf_op jit(solution)/shard_map/ppermute | solution.py:20
  96.3 1.9 collective-permute-start
  99.0 1.0 fusion.100
  101.6 4.5 %collective-permute-start.5 = (bf16[1,2,144,3,128]{4,2,3,1,0:T(8,128)(2,1)S(1)}, bf16[1,2,144,3,128]{4,2,3,1,0:T(8,128)(2,1)S(1)}, u32[]{:S(2)}, u32[]{:S(2)}) collective-permute-start(bf16[1,2,144,3,128]{4,2,3,1,0:T(8,128)(2,1)S(1)} %fusion.73), channel_id=1, source_target_pairs={{32,0},{64,32},{96,64},{128,96},{160,128},{192,160},{224,192},{256... | collective-permute-start | bytes 663560 | tf_op jit(solution)/shard_map/ppermute | solution.py:20
  106.1 1.9 collective-permute-start.4
  108.1 2.8 %fusion.25 = bf16[288,384]{1,0:T(8,128)(2,1)} fusion(bf16[288,1536]{1,0:T(8,128)(2,1)} %bitcast.364, bf16[1536,1536]{1,0:T(8,128)(2,1)} %all-gather.3.cloned.1.call-done), kind=kOutput, calls=%fused_computation.26 | convolution fusion | flops 339849216 | bytes 2285568 | tf_op jit(solution)/shard_map/dot_general | solution.py:142
  110.9 1.7 reshape.1034
  112.7 1.9 copy.121
  114.8 3.5 %collective-permute-start.6 = (bf16[3,1,144,3,128]{4,2,3,1,0:T(8,128)(2,1)S(1)}, bf16[3,1,144,3,128]{4,2,3,1,0:T(8,128)(2,1)S(1)}, u32[]{:S(2)}, u32[]{:S(2)}) collective-permute-start(bf16[3,1,144,3,128]{4,2,3,1,0:T(8,128)(2,1)S(1)} %get-tuple-element.235), channel_id=1, source_target_pairs={{0,2},{2,4},{4,6},{6,8},{8,10},{10,12},{12,14},{14,16},{16,18},{18... | collective-permute-start | bytes 995336 | tf_op jit(solution)/shard_map/ppermute | solution.py:19
  118.3 1.0 constant_dynamic-update-slice_fusion.11
  119.3 1.0 constant_dynamic-update-slice_fusion.9
  120.3 1.3 collective-permute-start.3
  121.6 4.6 %collective-permute-start.2 = (bf16[3,1,144,3,128]{4,2,3,1,0:T(8,128)(2,1)S(1)}, bf16[3,1,144,3,128]{4,2,3,1,0:T(8,128)(2,1)S(1)}, u32[]{:S(2)}, u32[]{:S(2)}) collective-permute-start(bf16[3,1,144,3,128]{4,2,3,1,0:T(8,128)(2,1)S(1)} %get-tuple-element.237), channel_id=1, source_target_pairs={{0,2},{2,4},{4,6},{6,8},{8,10},{10,12},{12,14},{14,16},{16,18},{18... | collective-permute-start | bytes 995336 | tf_op jit(solution)/shard_map/ppermute | solution.py:19
  126.2 1.5 collective-permute-start.7
  127.7 4.8 %collective-permute-done.2 = bf16[3,1,144,3,128]{4,2,3,1,0:T(8,128)(2,1)S(1)} collective-permute-done((bf16[3,1,144,3,128]{4,2,3,1,0:T(8,128)(2,1)S(1)}, bf16[3,1,144,3,128]{4,2,3,1,0:T(8,128)(2,1)S(1)}, u32[]{:S(2)}, u32[]{:S(2)}) %collective-permute-start.2) | collective-permute-done | bytes 331808 | tf_op jit(solution)/shard_map/ppermute | solution.py:19
  132.5 1.0 bitcast_dynamic-update-slice_fusion.3
  133.5 4.9 %collective-permute-done.7 = bf16[3,1,144,3,128]{4,2,3,1,0:T(8,128)(2,1)S(1)} collective-permute-done((bf16[3,1,144,3,128]{4,2,3,1,0:T(8,128)(2,1)S(1)}, bf16[3,1,144,3,128]{4,2,3,1,0:T(8,128)(2,1)S(1)}, u32[]{:S(2)}, u32[]{:S(2)}) %collective-permute-start.7) | collective-permute-done | bytes 331808 | tf_op jit(solution)/shard_map/ppermute | solution.py:20
  139.0 1.0 bitcast_dynamic-update-slice_fusion.2
  140.0 3.1 %fusion.96 = f32[2,3,144,1296]{3,2,1,0:T(8,128)} fusion(bf16[2,1296,3,128]{3,1,2,0:T(8,128)(2,1)S(1)} %bitcast.336, bf16[2,144,3,128]{3,2,1,0:T(4,128)(2,1)S(1)} %copy-done.8), kind=kOutput, calls=%fused_computation.172 | convolution fusion | flops 286654464 | bytes 6690816 | tf_op jit(solution)/shard_map/bqhe,bkhe->bhqk/dot_general | solution.py:80
  143.3 1.3 copy-done.6
  144.6 7.1 %multiply_reduce_fusion = (f32[2,3,144]{2,1,0:T(4,128)S(1)}, f32[2,3,144,1296]{3,2,1,0:T(8,128)}) fusion(f32[2,3,144,1296]{3,2,1,0:T(8,128)} %fusion.96, bf16[2,1296,3,128]{3,1,2,0:T(8,128)(2,1)} %bitcast.346, f32[2,1296]{1,0:T(2,128)S(1)} %reshape.1062, f32[2,144,3,128]{3,1,0,2:T(8,128)S(1)} %bitcast.348, f32[3,128]{1,0:T(4,128)S(1)} %bitcast.359, ...), kind=kOutput, calls=%fused_computation.1 | convolution fusion | flops 292586240 | bytes 11409792 | tf_op jit(solution)/shard_map/div | solution.py:75
  151.6 4.0 %fusion.14 = f32[2,3,128,1296]{2,3,1,0:T(8,128)S(1)} fusion(f32[2,3,144,1296]{3,2,1,0:T(8,128)} %get-tuple-element.251, bf16[2,144,3,128]{3,2,1,0:T(4,128)(2,1)S(1)} %copy-done.8), kind=kOutput, calls=%fused_computation.17 | convolution fusion | flops 287774208 | bytes 8681472 | tf_op jit(solution)/shard_map/bhqk,bqhe->bkhe/dot_general | solution.py:87
  155.7 3.2 %multiply_convert_fusion = bf16[2,3,144,1296]{3,2,1,0:T(8,128)(2,1)S(1)} fusion(f32[2,3,144,1296]{3,2,1,0:T(8,128)S(1)} %bitcast.317, f32[2,3,144,1296]{3,2,1,0:T(8,128)} %fusion.96, f32[2,3,144]{2,1,0:T(4,128)S(1)} %get-tuple-element.250), kind=kLoop, calls=%fused_computation | loop fusion | flops 3359232 | bytes 11200896 | tf_op jit(solution)/shard_map/convert_element_type | solution.py:86
  158.9 1.7 convolution_multiply_fusion
  160.8 1.3 fusion.38
  162.1 2.0 fusion.35
  164.9 1.9 collective-permute-start.12
  166.9 4.5 %collective-permute-start.13 = (bf16[1,4,144,3,128]{4,2,3,1,0:T(8,128)(2,1)S(1)}, bf16[1,4,144,3,128]{4,2,3,1,0:T(8,128)(2,1)S(1)}, u32[]{:S(2)}, u32[]{:S(2)}) collective-permute-start(bf16[1,4,144,3,128]{4,2,3,1,0:T(8,128)(2,1)S(1)} %get-tuple-element.231), channel_id=1, source_target_pairs={{32,0},{64,32},{96,64},{128,96},{160,128},{192,160},{224,192},{256... | collective-permute-start | bytes 1327112 | tf_op jit(solution)/shard_map/ppermute | solution.py:20
  171.6 1.3 fusion.40
  172.9 2.0 fusion.36
  175.7 2.2 collective-permute-start.16
  177.9 4.5 %collective-permute-start.17 = (bf16[1,4,144,3,128]{4,2,3,1,0:T(8,128)(2,1)S(1)}, bf16[1,4,144,3,128]{4,2,3,1,0:T(8,128)(2,1)S(1)}, u32[]{:S(2)}, u32[]{:S(2)}) collective-permute-start(bf16[1,4,144,3,128]{4,2,3,1,0:T(8,128)(2,1)S(1)} %get-tuple-element.233), channel_id=1, source_target_pairs={{32,0},{64,32},{96,64},{128,96},{160,128},{192,160},{224,192},{256... | collective-permute-start | bytes 1327112 | tf_op jit(solution)/shard_map/ppermute | solution.py:20
  182.5 0.9 fusion.22
  183.4 1.2 pad_maximum_fusion.14
  184.7 4.5 %collective-permute-start.14 = (bf16[5,1,144,3,128]{4,2,3,1,0:T(8,128)(2,1)}, bf16[5,1,144,3,128]{4,2,3,1,0:T(8,128)(2,1)}, u32[]{:S(2)}, u32[]{:S(2)}) collective-permute-start(bf16[5,1,144,3,128]{4,2,3,1,0:T(8,128)(2,1)} %get-tuple-element.222), channel_id=1, source_target_pairs={{0,2},{2,4},{4,6},{6,8},{8,10},{10,12},{12,14},{14,16},{16,18},{18... | collective-permute-start | bytes 1658888 | tf_op jit(solution)/shard_map/ppermute | solution.py:19
  189.1 1.3 collective-permute-start.15
  190.5 1.3 pad_maximum_fusion.11
  191.7 5.4 %collective-permute-start.18 = (bf16[5,1,144,3,128]{4,2,3,1,0:T(8,128)(2,1)}, bf16[5,1,144,3,128]{4,2,3,1,0:T(8,128)(2,1)}, u32[]{:S(2)}, u32[]{:S(2)}) collective-permute-start(bf16[5,1,144,3,128]{4,2,3,1,0:T(8,128)(2,1)} %get-tuple-element.224), channel_id=1, source_target_pairs={{0,2},{2,4},{4,6},{6,8},{8,10},{10,12},{12,14},{14,16},{16,18},{18... | collective-permute-start | bytes 1658888 | tf_op jit(solution)/shard_map/ppermute | solution.py:19
  197.1 1.5 collective-permute-start.19
  198.6 0.9 fusion.18
  199.6 2.9 %convolution_convert_fusion = bf16[288,1536]{1,0:T(8,128)(2,1)} fusion(bf16[1536,1536]{1,0:T(8,128)(2,1)} %all-gather.3.cloned.1.call-done, bf16[36,8,3,128]{3,2,1,0:T(4,128)(2,1)S(1)} %bitcast.353), kind=kOutput, calls=%fused_computation.9 | convolution fusion | flops 340180992 | bytes 2285568 | tf_op jit(solution)/shard_map/dot_general | solution.py:175
  202.6 3.1 %collective-permute-done.15 = bf16[5,1,144,3,128]{4,2,3,1,0:T(8,128)(2,1)} collective-permute-done((bf16[5,1,144,3,128]{4,2,3,1,0:T(8,128)(2,1)}, bf16[5,1,144,3,128]{4,2,3,1,0:T(8,128)(2,1)}, u32[]{:S(2)}, u32[]{:S(2)}) %collective-permute-start.15) | collective-permute-done | bytes 552992 | tf_op jit(solution)/shard_map/ppermute | solution.py:20
  205.7 1.9 fusion.13
  207.7 2.6 collective-permute-done.18
  210.3 5.0 %collective-permute-done.19 = bf16[5,1,144,3,128]{4,2,3,1,0:T(8,128)(2,1)} collective-permute-done((bf16[5,1,144,3,128]{4,2,3,1,0:T(8,128)(2,1)}, bf16[5,1,144,3,128]{4,2,3,1,0:T(8,128)(2,1)}, u32[]{:S(2)}, u32[]{:S(2)}) %collective-permute-start.19) | collective-permute-done | bytes 552992 | tf_op jit(solution)/shard_map/ppermute | solution.py:20
  215.3 1.6 fusion.12
  217.5 0.8 copy.164
  218.3 1.8 stack.125
  221.2 2.3 fusion.34
  223.9 1.0 maximum_bitcast_fusion
  225.0 4.3 %fusion.7 = bf16[288,1536]{1,0:T(8,128)(2,1)} fusion(bf16[288,1152]{1,0:T(8,128)(2,1)S(1)} %bitcast.352, bf16[1536,1536]{1,0:T(8,128)(2,1)} %all-gather.3.cloned.1.call-done), kind=kOutput, calls=%fused_computation.10 | convolution fusion | flops 1019658240 | bytes 5087232 | tf_op jit(solution)/shard_map/dot_general | solution.py:179
  229.4 6.3 %reduce-scatter.3.cloned.1.call-done = bf16[288,768]{1,0:T(8,128)(2,1)} async-done(((bf16[288,1536]{1,0:T(8,128)(2,1)}), bf16[288,768]{1,0:T(8,128)(2,1)}) %reduce-scatter.3.cloned.1.call-update) | async-done | bytes 442384 | tf_op jit(solution)/shard_map/reduce_scatter | solution.py:176
  235.7 33.2 %reduce-scatter.5.cloned.1.call-done = bf16[288,768]{1,0:T(8,128)(2,1)} async-done(((bf16[288,1536]{1,0:T(8,128)(2,1)}), bf16[288,768]{1,0:T(8,128)(2,1)}) %reduce-scatter.5.cloned.1.call-update) | async-done | bytes 442384 | tf_op jit(solution)/shard_map/reduce_scatter | solution.py:184
  (154 shorter events, 13.7 us)
Async XLA Ops:
  7.2 81.1 %copy-start = (bf16[1,2,144,1536]{3,2,1,0:T(8,128)(2,1)S(1)}, bf16[1,2,144,1536]{3,2,1,0:T(8,128)(2,1)}, u32[]{:S(2)}) copy-start(bf16[1,2,144,1536]{3,2,1,0:T(8,128)(2,1)} %param.43) | copy-start | bytes 2654212
  7.2 81.1 %all-gather.3.cloned.1.call-start = ((), (), s32[]{:S(2)}) async-start(), calls=%async_computation.2 | async-start | bytes 5013504 | tf_op jit(solution)/shard_map/all_gather | solution.py:111
  47.2 188.5 %reduce-scatter.3.cloned.1.call-start = ((), (), s32[]{:S(2)}) async-start(), calls=%async_computation.3 | async-start | bytes 1327104 | tf_op jit(solution)/shard_map/reduce_scatter | solution.py:176
  48.0 6.4 %collective-permute-start.9 = (bf16[1,2,144]{2,1,0:T(2,128)(2,1)S(1)}, bf16[1,2,144]{2,1,0:T(2,128)(2,1)S(1)}, u32[]{:S(2)}, u32[]{:S(2)}) collective-permute-start(bf16[1,2,144]{2,1,0:T(2,128)(2,1)S(1)} %convert_element_type.112), channel_id=1, source_target_pairs={{32,0},{64,32},{96,64},{128,96},{160,128},{192,160},{224,192},{256... | collective-permute-start | bytes 1736 | tf_op jit(solution)/shard_map/ppermute | solution.py:20
  49.9 5.8 %collective-permute-start.8 = (bf16[1,2,144]{2,1,0:T(2,128)(2,1)S(1)}, bf16[1,2,144]{2,1,0:T(2,128)(2,1)S(1)}, u32[]{:S(2)}, u32[]{:S(2)}) collective-permute-start(bf16[1,2,144]{2,1,0:T(2,128)(2,1)S(1)} %convert_element_type.112), channel_id=1, source_target_pairs={{0,32},{32,64},{64,96},{96,128},{128,160},{160,192},{192,224},{224... | collective-permute-start | bytes 1736 | tf_op jit(solution)/shard_map/ppermute | solution.py:19
  55.7 3.4 %collective-permute-start.10 = (bf16[3,1,144]{2,1,0:T(2,128)(2,1)S(1)}, bf16[3,1,144]{2,1,0:T(2,128)(2,1)S(1)}, u32[]{:S(2)}, u32[]{:S(2)}) collective-permute-start(bf16[3,1,144]{2,1,0:T(2,128)(2,1)S(1)} %get-tuple-element.243), channel_id=1, source_target_pairs={{0,2},{2,4},{4,6},{6,8},{8,10},{10,12},{12,14},{14,16},{16,18},{18... | collective-permute-start | bytes 2600 | tf_op jit(solution)/shard_map/ppermute | solution.py:19
  57.8 5.5 %collective-permute-start.11 = (bf16[3,1,144]{2,1,0:T(2,128)(2,1)S(1)}, bf16[3,1,144]{2,1,0:T(2,128)(2,1)S(1)}, u32[]{:S(2)}, u32[]{:S(2)}) collective-permute-start(bf16[3,1,144]{2,1,0:T(2,128)(2,1)S(1)} %get-tuple-element.242), channel_id=1, source_target_pairs={{2,0},{4,2},{6,4},{8,6},{10,8},{12,10},{14,12},{16,14},{18,16},{20... | collective-permute-start | bytes 2600 | tf_op jit(solution)/shard_map/ppermute | solution.py:20
  93.0 8.4 %copy-start.22 = (f32[384]{0:T(512)S(1)}, f32[384]{0:T(512)}, u32[]{:S(2)}) copy-start(f32[384]{0:T(512)} %param.48) | copy-start | bytes 4612
  93.0 26.3 %collective-permute-start.1 = (bf16[1,2,144,3,128]{4,2,3,1,0:T(8,128)(2,1)}, bf16[1,2,144,3,128]{4,2,3,1,0:T(8,128)(2,1)}, u32[]{:S(2)}, u32[]{:S(2)}) collective-permute-start(bf16[1,2,144,3,128]{4,2,3,1,0:T(8,128)(2,1)} %copy.110), channel_id=1, source_target_pairs={{32,0},{64,32},{96,64},{128,96},{160,128},{192,160},{224,192},{256... | collective-permute-start | bytes 663560 | tf_op jit(solution)/shard_map/ppermute | solution.py:20
  96.3 21.9 %collective-permute-start = (bf16[1,2,144,3,128]{4,2,3,1,0:T(8,128)(2,1)}, bf16[1,2,144,3,128]{4,2,3,1,0:T(8,128)(2,1)}, u32[]{:S(2)}, u32[]{:S(2)}) collective-permute-start(bf16[1,2,144,3,128]{4,2,3,1,0:T(8,128)(2,1)} %copy.110), channel_id=1, source_target_pairs={{0,32},{32,64},{64,96},{96,128},{128,160},{160,192},{192,224},{224... | collective-permute-start | bytes 663560 | tf_op jit(solution)/shard_map/ppermute | solution.py:19
  100.7 0.7 copy-start.16
  100.8 13.9 %copy-start.18 = (f32[288,3]{1,0:T(8,128)}, f32[288,3]{1,0:T(8,128)S(1)}, u32[]{:S(2)}) copy-start(f32[288,3]{1,0:T(8,128)S(1)} %get-tuple-element.252) | copy-start | bytes 10372
  101.6 13.0 %collective-permute-start.5 = (bf16[1,2,144,3,128]{4,2,3,1,0:T(8,128)(2,1)S(1)}, bf16[1,2,144,3,128]{4,2,3,1,0:T(8,128)(2,1)S(1)}, u32[]{:S(2)}, u32[]{:S(2)}) collective-permute-start(bf16[1,2,144,3,128]{4,2,3,1,0:T(8,128)(2,1)S(1)} %fusion.73), channel_id=1, source_target_pairs={{32,0},{64,32},{96,64},{128,96},{160,128},{192,160},{224,192},{256... | collective-permute-start | bytes 663560 | tf_op jit(solution)/shard_map/ppermute | solution.py:20
  106.1 8.5 %collective-permute-start.4 = (bf16[1,2,144,3,128]{4,2,3,1,0:T(8,128)(2,1)S(1)}, bf16[1,2,144,3,128]{4,2,3,1,0:T(8,128)(2,1)S(1)}, u32[]{:S(2)}, u32[]{:S(2)}) collective-permute-start(bf16[1,2,144,3,128]{4,2,3,1,0:T(8,128)(2,1)S(1)} %fusion.73), channel_id=1, source_target_pairs={{0,32},{32,64},{64,96},{96,128},{128,160},{160,192},{192,224},{224... | collective-permute-start | bytes 663560 | tf_op jit(solution)/shard_map/ppermute | solution.py:19
  114.8 12.9 %collective-permute-start.6 = (bf16[3,1,144,3,128]{4,2,3,1,0:T(8,128)(2,1)S(1)}, bf16[3,1,144,3,128]{4,2,3,1,0:T(8,128)(2,1)S(1)}, u32[]{:S(2)}, u32[]{:S(2)}) collective-permute-start(bf16[3,1,144,3,128]{4,2,3,1,0:T(8,128)(2,1)S(1)} %get-tuple-element.235), channel_id=1, source_target_pairs={{0,2},{2,4},{4,6},{6,8},{8,10},{10,12},{12,14},{14,16},{16,18},{18... | collective-permute-start | bytes 995336 | tf_op jit(solution)/shard_map/ppermute | solution.py:19
  120.3 18.4 %collective-permute-start.3 = (bf16[3,1,144,3,128]{4,2,3,1,0:T(8,128)(2,1)S(1)}, bf16[3,1,144,3,128]{4,2,3,1,0:T(8,128)(2,1)S(1)}, u32[]{:S(2)}, u32[]{:S(2)}) collective-permute-start(bf16[3,1,144,3,128]{4,2,3,1,0:T(8,128)(2,1)S(1)} %get-tuple-element.236), channel_id=1, source_target_pairs={{2,0},{4,2},{6,4},{8,6},{10,8},{12,10},{14,12},{16,14},{18,16},{20... | collective-permute-start | bytes 995336 | tf_op jit(solution)/shard_map/ppermute | solution.py:20
  121.6 10.9 %collective-permute-start.2 = (bf16[3,1,144,3,128]{4,2,3,1,0:T(8,128)(2,1)S(1)}, bf16[3,1,144,3,128]{4,2,3,1,0:T(8,128)(2,1)S(1)}, u32[]{:S(2)}, u32[]{:S(2)}) collective-permute-start(bf16[3,1,144,3,128]{4,2,3,1,0:T(8,128)(2,1)S(1)} %get-tuple-element.237), channel_id=1, source_target_pairs={{0,2},{2,4},{4,6},{6,8},{8,10},{10,12},{12,14},{14,16},{16,18},{18... | collective-permute-start | bytes 995336 | tf_op jit(solution)/shard_map/ppermute | solution.py:19
  126.2 12.2 %collective-permute-start.7 = (bf16[3,1,144,3,128]{4,2,3,1,0:T(8,128)(2,1)S(1)}, bf16[3,1,144,3,128]{4,2,3,1,0:T(8,128)(2,1)S(1)}, u32[]{:S(2)}, u32[]{:S(2)}) collective-permute-start(bf16[3,1,144,3,128]{4,2,3,1,0:T(8,128)(2,1)S(1)} %get-tuple-element.234), channel_id=1, source_target_pairs={{2,0},{4,2},{6,4},{8,6},{10,8},{12,10},{14,12},{16,14},{18,16},{20... | collective-permute-start | bytes 995336 | tf_op jit(solution)/shard_map/ppermute | solution.py:20
  138.8 1.2 copy-start.8
  140.0 3.1 %copy-start.4 = (bf16[1,2,9,144,3,128]{5,3,2,4,1,0:T(8,128)(2,1)}, bf16[1,2,9,144,3,128]{5,3,2,4,1,0:T(8,128)(2,1)S(1)}, u32[]{:S(2)}) copy-start(bf16[1,2,9,144,3,128]{5,3,2,4,1,0:T(8,128)(2,1)S(1)} %fusion.78) | copy-start | bytes 5971972
  143.1 1.5 copy-start.15
  143.1 1.5 copy-start.23
  143.3 1.3 copy-start.6
  151.6 4.0 %slice-start = ((s8[4866048]{0:T(1024)(128)(4,1)}), s8[4194304]{0:T(1024)(128)(4,1)S(1)}, s32[]{:S(2)}) async-start(s8[4866048]{0:T(1024)(128)(4,1)} %bitcast.316), calls=%async_computation.5 | async-start | bytes 8388608
  151.6 4.1 %slice-start.1 = ((s8[4866048]{0:T(1024)(128)(4,1)}), s8[671744]{0:T(1024)(128)(4,1)S(1)}, s32[]{:S(2)}) async-start(s8[4866048]{0:T(1024)(128)(4,1)} %bitcast.316), calls=%async_computation.6 | async-start | bytes 1343488
  164.9 18.4 %collective-permute-start.12 = (bf16[1,4,144,3,128]{4,2,3,1,0:T(8,128)(2,1)S(1)}, bf16[1,4,144,3,128]{4,2,3,1,0:T(8,128)(2,1)S(1)}, u32[]{:S(2)}, u32[]{:S(2)}) collective-permute-start(bf16[1,4,144,3,128]{4,2,3,1,0:T(8,128)(2,1)S(1)} %get-tuple-element.230), channel_id=1, source_target_pairs={{0,32},{32,64},{64,96},{96,128},{128,160},{160,192},{192,224},{224... | collective-permute-start | bytes 1327112 | tf_op jit(solution)/shard_map/ppermute | solution.py:19
  166.9 16.5 %collective-permute-start.13 = (bf16[1,4,144,3,128]{4,2,3,1,0:T(8,128)(2,1)S(1)}, bf16[1,4,144,3,128]{4,2,3,1,0:T(8,128)(2,1)S(1)}, u32[]{:S(2)}, u32[]{:S(2)}) collective-permute-start(bf16[1,4,144,3,128]{4,2,3,1,0:T(8,128)(2,1)S(1)} %get-tuple-element.231), channel_id=1, source_target_pairs={{32,0},{64,32},{96,64},{128,96},{160,128},{192,160},{224,192},{256... | collective-permute-start | bytes 1327112 | tf_op jit(solution)/shard_map/ppermute | solution.py:20
  175.5 7.0 %copy-start.5 = (bf16[1,2,9,144,3,128]{5,3,2,4,1,0:T(8,128)(2,1)S(1)}, bf16[1,2,9,144,3,128]{5,3,2,4,1,0:T(8,128)(2,1)}, u32[]{:S(2)}) copy-start(bf16[1,2,9,144,3,128]{5,3,2,4,1,0:T(8,128)(2,1)} %copy-done.4) | copy-start | bytes 5971972
  175.7 14.8 %copy-start.2 = (bf16[3,4,144,3,128]{4,2,3,1,0:T(8,128)(2,1)}, bf16[3,4,144,3,128]{4,2,3,1,0:T(8,128)(2,1)S(1)}, u32[]{:S(2)}) copy-start(bf16[3,4,144,3,128]{4,2,3,1,0:T(8,128)(2,1)S(1)} %convert_element_type.124) | copy-start | bytes 3981316
  175.7 14.7 %collective-permute-start.16 = (bf16[1,4,144,3,128]{4,2,3,1,0:T(8,128)(2,1)S(1)}, bf16[1,4,144,3,128]{4,2,3,1,0:T(8,128)(2,1)S(1)}, u32[]{:S(2)}, u32[]{:S(2)}) collective-permute-start(bf16[1,4,144,3,128]{4,2,3,1,0:T(8,128)(2,1)S(1)} %get-tuple-element.232), channel_id=1, source_target_pairs={{0,32},{32,64},{64,96},{96,128},{128,160},{160,192},{192,224},{224... | collective-permute-start | bytes 1327112 | tf_op jit(solution)/shard_map/ppermute | solution.py:19
  177.9 12.5 %collective-permute-start.17 = (bf16[1,4,144,3,128]{4,2,3,1,0:T(8,128)(2,1)S(1)}, bf16[1,4,144,3,128]{4,2,3,1,0:T(8,128)(2,1)S(1)}, u32[]{:S(2)}, u32[]{:S(2)}) collective-permute-start(bf16[1,4,144,3,128]{4,2,3,1,0:T(8,128)(2,1)S(1)} %get-tuple-element.233), channel_id=1, source_target_pairs={{32,0},{64,32},{96,64},{128,96},{160,128},{192,160},{224,192},{256... | collective-permute-start | bytes 1327112 | tf_op jit(solution)/shard_map/ppermute | solution.py:20
  183.4 8.3 %copy-start.9 = (bf16[1,4,144,3,128]{4,2,3,1,0:T(8,128)(2,1)}, bf16[1,4,144,3,128]{4,2,3,1,0:T(8,128)(2,1)S(1)}, u32[]{:S(2)}) copy-start(bf16[1,4,144,3,128]{4,2,3,1,0:T(8,128)(2,1)S(1)} %collective-permute-done.12) | copy-start | bytes 1327108
  183.4 8.3 %copy-start.10 = (bf16[1,4,144,3,128]{4,2,3,1,0:T(8,128)(2,1)}, bf16[1,4,144,3,128]{4,2,3,1,0:T(8,128)(2,1)S(1)}, u32[]{:S(2)}) copy-start(bf16[1,4,144,3,128]{4,2,3,1,0:T(8,128)(2,1)S(1)} %collective-permute-done.13) | copy-start | bytes 1327108
  184.7 13.9 %copy-start.7 = (bf16[1,2,9,144,3,128]{5,3,2,4,1,0:T(8,128)(2,1)S(1)}, bf16[1,2,9,144,3,128]{5,3,2,4,1,0:T(8,128)(2,1)}, u32[]{:S(2)}) copy-start(bf16[1,2,9,144,3,128]{5,3,2,4,1,0:T(8,128)(2,1)} %copy-done.6) | copy-start | bytes 5971972
  184.7 18.0 %collective-permute-start.14 = (bf16[5,1,144,3,128]{4,2,3,1,0:T(8,128)(2,1)}, bf16[5,1,144,3,128]{4,2,3,1,0:T(8,128)(2,1)}, u32[]{:S(2)}, u32[]{:S(2)}) collective-permute-start(bf16[5,1,144,3,128]{4,2,3,1,0:T(8,128)(2,1)} %get-tuple-element.222), channel_id=1, source_target_pairs={{0,2},{2,4},{4,6},{6,8},{8,10},{10,12},{12,14},{14,16},{16,18},{18... | collective-permute-start | bytes 1658888 | tf_op jit(solution)/shard_map/ppermute | solution.py:19
  189.1 16.6 %collective-permute-start.15 = (bf16[5,1,144,3,128]{4,2,3,1,0:T(8,128)(2,1)}, bf16[5,1,144,3,128]{4,2,3,1,0:T(8,128)(2,1)}, u32[]{:S(2)}, u32[]{:S(2)}) collective-permute-start(bf16[5,1,144,3,128]{4,2,3,1,0:T(8,128)(2,1)} %get-tuple-element.223), channel_id=1, source_target_pairs={{2,0},{4,2},{6,4},{8,6},{10,8},{12,10},{14,12},{16,14},{18,16},{20... | collective-permute-start | bytes 1658888 | tf_op jit(solution)/shard_map/ppermute | solution.py:20
  190.4 9.0 %copy-start.11 = (bf16[1,4,144,3,128]{4,2,3,1,0:T(8,128)(2,1)}, bf16[1,4,144,3,128]{4,2,3,1,0:T(8,128)(2,1)S(1)}, u32[]{:S(2)}) copy-start(bf16[1,4,144,3,128]{4,2,3,1,0:T(8,128)(2,1)S(1)} %collective-permute-done.16) | copy-start | bytes 1327108
  190.5 9.0 %copy-start.13 = (bf16[1,4,144,3,128]{4,2,3,1,0:T(8,128)(2,1)}, bf16[1,4,144,3,128]{4,2,3,1,0:T(8,128)(2,1)S(1)}, u32[]{:S(2)}) copy-start(bf16[1,4,144,3,128]{4,2,3,1,0:T(8,128)(2,1)S(1)} %collective-permute-done.17) | copy-start | bytes 1327108
  191.7 18.6 %collective-permute-start.18 = (bf16[5,1,144,3,128]{4,2,3,1,0:T(8,128)(2,1)}, bf16[5,1,144,3,128]{4,2,3,1,0:T(8,128)(2,1)}, u32[]{:S(2)}, u32[]{:S(2)}) collective-permute-start(bf16[5,1,144,3,128]{4,2,3,1,0:T(8,128)(2,1)} %get-tuple-element.224), channel_id=1, source_target_pairs={{0,2},{2,4},{4,6},{6,8},{8,10},{10,12},{12,14},{14,16},{16,18},{18... | collective-permute-start | bytes 1658888 | tf_op jit(solution)/shard_map/ppermute | solution.py:19
  197.1 18.2 %collective-permute-start.19 = (bf16[5,1,144,3,128]{4,2,3,1,0:T(8,128)(2,1)}, bf16[5,1,144,3,128]{4,2,3,1,0:T(8,128)(2,1)}, u32[]{:S(2)}, u32[]{:S(2)}) collective-permute-start(bf16[5,1,144,3,128]{4,2,3,1,0:T(8,128)(2,1)} %get-tuple-element.225), channel_id=1, source_target_pairs={{2,0},{4,2},{6,4},{8,6},{10,8},{12,10},{14,12},{16,14},{18,16},{20... | collective-permute-start | bytes 1658888 | tf_op jit(solution)/shard_map/ppermute | solution.py:20
  202.5 66.3 %reduce-scatter.5.cloned.1.call-start = ((), (), s32[]{:S(2)}) async-start(), calls=%async_computation.4 | async-start | bytes 1327104 | tf_op jit(solution)/shard_map/reduce_scatter | solution.py:184
  202.6 12.7 %copy-start.3 = (bf16[3,4,144,3,128]{4,2,3,1,0:T(8,128)(2,1)S(1)}, bf16[3,4,144,3,128]{4,2,3,1,0:T(8,128)(2,1)}, u32[]{:S(2)}) copy-start(bf16[3,4,144,3,128]{4,2,3,1,0:T(8,128)(2,1)} %copy-done.2) | copy-start | bytes 3981316
  202.6 12.7 %copy-start.12 = (bf16[1,4,144,3,128]{4,2,3,1,0:T(8,128)(2,1)S(1)}, bf16[1,4,144,3,128]{4,2,3,1,0:T(8,128)(2,1)}, u32[]{:S(2)}) copy-start(bf16[1,4,144,3,128]{4,2,3,1,0:T(8,128)(2,1)} %copy-done.11) | copy-start | bytes 1327108
  202.6 12.7 %copy-start.14 = (bf16[1,4,144,3,128]{4,2,3,1,0:T(8,128)(2,1)S(1)}, bf16[1,4,144,3,128]{4,2,3,1,0:T(8,128)(2,1)}, u32[]{:S(2)}) copy-start(bf16[1,4,144,3,128]{4,2,3,1,0:T(8,128)(2,1)} %copy-done.13) | copy-start | bytes 1327108
  207.6 9.2 %copy-start.24 = (pred[2]{0:T(512)(128)(4,1)S(1)}, pred[2]{0:T(512)(128)(4,1)}, u32[]{:S(2)}) copy-start(pred[2]{0:T(512)(128)(4,1)} %constant.473.clone.1) | copy-start | bytes 10
  217.3 3.6 %copy-start.17 = (f32[288,3]{1,0:T(8,128)S(1)}, f32[288,3]{1,0:T(8,128)}, u32[]{:S(2)}) copy-start(f32[288,3]{1,0:T(8,128)} %copy-done.16) | copy-start | bytes 10372
  220.2 0.9 copy-start.19
  220.2 1.0 copy-start.20
  220.2 1.0 copy-start.21
  225.0 43.8 %copy-start.1 = (bf16[1,2,144,1536]{3,2,1,0:T(8,128)(2,1)S(1)}, bf16[1,2,144,1536]{3,2,1,0:T(8,128)(2,1)}, u32[]{:S(2)}) copy-start(bf16[1,2,144,1536]{3,2,1,0:T(8,128)(2,1)} %param.43) | copy-start | bytes 2654212
Sparse Core Ops, SparseCore 0:
  47.4 40.8 all-gather.2
  202.7 32.9 reduce-scatter.2
  239.1 29.7 reduce-scatter.4

commit v2 on v1

v2 whole, which is shorter than its diff:
```python
import functools

import jax
import jax.numpy as jnp
from jax import lax
from jax.experimental import pallas as pl
from jax.experimental.pallas import tpu as pltpu
from jax.sharding import PartitionSpec as P

HEAD_DIM = 128
LANES = 128
TILE = 144
COLUMN = 3 * TILE
WINDOW = 9 * TILE
EXTENDED = 12 * TILE
OWN_TILES = (4, 7)
MASK_LANE = 18
MASK_DEPTH = 1e5
FACTOR = HEAD_DIM ** (-0.5)
VMEM_BYTES = 50 * 1024 * 1024
epsilon = 1e-06


def dot_rows(left, right):
    return lax.dot_general(left, right, (((1,), (1,)), ((), ())), preferred_element_type=jnp.float32)


def dot_plain(left, right):
    return jnp.dot(left, right, preferred_element_type=jnp.float32)


def lane_index(rows):
    return lax.broadcasted_iota(jnp.int32, (rows, LANES), 1)


def norm_inverse(raw_values):
    return lax.rsqrt(jnp.mean(raw_values * raw_values, axis=-1, keepdims=True) + epsilon)


def norm_backward(raw_values, gain_vec, upstream):
    inverse = norm_inverse(raw_values)
    weighted = gain_vec * upstream
    inner_mean = jnp.mean(weighted * raw_values, axis=-1, keepdims=True)
    return inverse * weighted - raw_values * (inverse * inverse * inverse) * inner_mean


def three_parts(values):
    first = values.astype(jnp.bfloat16)
    rest = values - first.astype(jnp.float32)
    second = rest.astype(jnp.bfloat16)
    third = (rest - second.astype(jnp.float32)).astype(jnp.bfloat16)
    return [part.astype(jnp.float32) for part in (first, second, third)]


def extended_copies(own, up, down, left, right, target, sems):
    tile = lambda ref, i: ref.at[pl.ds(i * TILE, TILE)]
    pairs = [
        (left, 0, 3),
        (tile(up, 0), 3, 1),
        (tile(own, 0), 4, 1),
        (tile(down, 0), 5, 1),
        (tile(up, 1), 6, 1),
        (tile(own, 1), 7, 1),
        (tile(down, 1), 8, 1),
        (right, 9, 3),
    ]
    return [
        pltpu.make_async_copy(src, target.at[pl.ds(at * TILE, count * TILE)], sems.at[n])
        for n, (src, at, count) in enumerate(pairs)
    ]


def front_kernel(place, own, up, down, left, right, upstream, *rest):
    blocks, rest = rest[:16], rest[16:]
    (q_gain, k_gain, whole, queries, own_keys, own_values, own_marks, own_k_raw, grad_q, attended,
     message, tok, grad, keys, values, marks, raw, token_sems, block_sems, grad_sem) = rest
    here = place[0]
    north, south = lax.rem(here + 12, 16), lax.rem(here + 4, 16)
    far = lax.rem(here + 8, 16)
    spots = [here, here ^ 2, north, south, north ^ 2, south ^ 2, far, far ^ 2]
    spots = spots + [spot ^ 1 for spot in spots]
    block_copies = [
        pltpu.make_async_copy(block, whole.at[pl.ds(pl.multiple_of(spot * 96, 96), 96)], block_sems.at[n])
        for n, (block, spot) in enumerate(zip(blocks, spots))
    ]
    grad_copy = pltpu.make_async_copy(upstream, grad, grad_sem.at[0])
    token_copies = extended_copies(own, up, down, left, right, tok, token_sems)
    for copy in block_copies + [grad_copy] + token_copies:
        copy.start()
    for copy in block_copies + [grad_copy]:
        copy.wait()
    heads = range(queries.shape[1] // HEAD_DIM)
    inner = queries.shape[1]
    model = whole.shape[0]
    message[:, :inner] = dot_plain(grad[...], whole[:, 3 * inner :]).astype(jnp.bfloat16)
    for copy in token_copies:
        copy.wait()
    chunk = 2 * TILE

    def project(step, carry):
        rows = pl.ds(pl.multiple_of(step * chunk, chunk), chunk)
        result = dot_plain(tok[rows, :model], whole[:, : 3 * inner])
        raw[rows, :] = result[:, : 2 * inner]
        for head in heads:
            lanes = slice(head * HEAD_DIM, (head + 1) * HEAD_DIM)
            q_raw = result[:, lanes]
            queries[rows, lanes] = (q_raw * norm_inverse(q_raw) * q_gain[:, lanes]).astype(jnp.bfloat16)
            k_raw = result[:, inner:][:, lanes]
            keys[rows, lanes] = (k_raw * norm_inverse(k_raw) * k_gain[:, lanes]).astype(jnp.bfloat16)
        values[rows, :] = result[:, 2 * inner :].astype(jnp.bfloat16)
        valid = tok[rows, model:].astype(jnp.float32)
        deep = jnp.where(lane_index(chunk) == MASK_LANE, MASK_DEPTH, 0.0)
        marks[rows, :] = (valid * deep - deep).astype(jnp.bfloat16)
        return carry

    lax.fori_loop(0, EXTENDED // chunk, project, 0)
    lane = lane_index(TILE)
    one_mark = jnp.where(lane == MASK_LANE, 1.0, 0.0)
    for tile, at in enumerate(OWN_TILES):
        mine = slice(tile * TILE, (tile + 1) * TILE)
        ext = slice(at * TILE, (at + 1) * TILE)
        window = slice(tile * COLUMN, tile * COLUMN + WINDOW)
        stats = one_mark
        for head in heads:
            lanes = slice(head * HEAD_DIM, (head + 1) * HEAD_DIM)
            q_aug = jnp.concatenate([queries[ext, lanes], one_mark.astype(jnp.bfloat16)], axis=1)
            win_keys = keys[window, lanes]
            win_values = values[window, lanes]
            k_aug = jnp.concatenate([win_keys, marks[window, :]], axis=1)
            weights = jnp.exp(dot_rows(q_aug, k_aug) * FACTOR)
            total = jnp.sum(weights, axis=-1, keepdims=True)
            probs = weights * (1.0 / total)
            attended[mine, lanes] = dot_plain(probs.astype(jnp.bfloat16), win_values).astype(jnp.bfloat16)
            grad_probs = dot_rows(message[mine, lanes], win_values)
            delta = jnp.sum(probs * grad_probs, axis=-1, keepdims=True)
            grad_scores = (probs * (grad_probs - delta)).astype(jnp.bfloat16)
            upstream_q = dot_plain(grad_scores, win_keys) * FACTOR
            grad_q[mine, lanes] = norm_backward(raw[ext, lanes], q_gain[:, lanes], upstream_q).astype(jnp.bfloat16)
            for n, part in enumerate(three_parts(jnp.log(total) * (1.0 / FACTOR))):
                stats = jnp.where(lane == 3 * head + n, part, stats)
            for n, part in enumerate(three_parts(delta)):
                stats = jnp.where(lane == 9 + 3 * head + n, part, stats)
        message[mine, inner:] = stats.astype(jnp.bfloat16)
        own_keys[mine, :] = keys[ext, :]
        own_values[mine, :] = values[ext, :]
        own_marks[mine, :] = marks[ext, :]
        own_k_raw[mine, :] = raw[ext, inner:]


def back_kernel(place, own, up, down, left, right, queries, keys, values, marks, k_raw, grad_q, whole, k_gain,
                kept, sent, ext, grad_qkv, sems):
    copies = extended_copies(own, up, down, left, right, ext, sems)
    for copy in copies:
        copy.start()
    for copy in copies:
        copy.wait()
    inner = queries.shape[1]
    grad_qkv[:, :inner] = grad_q[...]
    lane = lane_index(TILE)
    for tile in range(2):
        mine = slice(tile * TILE, (tile + 1) * TILE)
        window = slice(tile * COLUMN, tile * COLUMN + WINDOW)
        stats = ext[window, inner:]
        for head in range(inner // HEAD_DIM):
            lanes = slice(head * HEAD_DIM, (head + 1) * HEAD_DIM)
            k_signs = jnp.where((lane >= 3 * head) & (lane < 3 * head + 3), -1.0, 0.0).astype(jnp.bfloat16)
            v_signs = jnp.where((lane >= 9 + 3 * head) & (lane < 12 + 3 * head), -1.0, 0.0).astype(jnp.bfloat16)
            k_aug = jnp.concatenate([keys[mine, lanes], marks[mine, :] + k_signs], axis=1)
            v_aug = jnp.concatenate([values[mine, lanes], v_signs], axis=1)
            win_queries = queries[window, lanes]
            win_upstream = ext[window, lanes]
            probs = jnp.exp(dot_rows(k_aug, jnp.concatenate([win_queries, stats], axis=1)) * FACTOR)
            centred = dot_rows(v_aug, jnp.concatenate([win_upstream, stats], axis=1))
            grad_scores = (probs * centred).astype(jnp.bfloat16)
            grad_v = dot_plain(probs.astype(jnp.bfloat16), win_upstream)
            upstream_k = dot_plain(grad_scores, win_queries) * FACTOR
            grad_k = norm_backward(k_raw[mine, lanes], k_gain[:, lanes], upstream_k)
            grad_qkv[mine, inner + head * HEAD_DIM : inner + (head + 1) * HEAD_DIM] = grad_k.astype(jnp.bfloat16)
            grad_qkv[mine, 2 * inner + head * HEAD_DIM : 2 * inner + (head + 1) * HEAD_DIM] = grad_v.astype(jnp.bfloat16)
    half = kept.shape[1]
    for target, group in ((sent, 1 - place[1]), (kept, place[1])):
        rows = pl.ds(pl.multiple_of(group * half, half), half)
        target[...] = dot_rows(grad_qkv[...], whole[rows, : 3 * inner]).astype(jnp.bfloat16)


def steps(axis, shift, wrap=False):
    count = lax.axis_size(axis)
    return [(i, (i + shift) % count) for i in range(count) if wrap or 0 <= i + shift < count]


def spread_height(own):
    up = lax.ppermute(own, "height", steps("height", 1))
    down = lax.ppermute(own, "height", steps("height", -1))
    return up, down


def spread_width(own, up, down):
    column = lambda i: jnp.concatenate([part[i * TILE : (i + 1) * TILE] for part in (up, own, down)], axis=0)
    left = lax.ppermute(column(1), "width", steps("width", 1))
    right = lax.ppermute(column(0), "width", steps("width", -1))
    return left, right


def flip(x, bit):
    count = lax.axis_size("height")
    return lax.ppermute(x, "height", [(i, i ^ bit) for i in range(count)])


def gather_height(block):
    shift = lambda x, by: lax.ppermute(x, "height", steps("height", by, True))
    rows = block.shape[0]
    north, south = shift(block, 4), shift(block, -4)
    beside = flip(block, 2)
    north_beside, south_beside = shift(beside, 4), shift(beside, -4)
    far, far_beside = shift(north, 4), shift(south_beside, -4)
    mine = [block, beside, north, south, north_beside, south_beside, far, far_beside]
    groups = [mine[:2], mine[2:6], mine[6:]]
    other = []
    for group in groups:
        swapped = flip(jnp.concatenate(group, axis=0), 1)
        other += [swapped[n * rows : (n + 1) * rows] for n in range(len(group))]
    return mine + other


def whole_spec():
    return pl.BlockSpec(memory_space=pltpu.VMEM)


def on_device(tokens, grad_out, qkv_weight, out_weight, q_gain, k_gain, key_valid):
    model = tokens.shape[-1]
    inner = q_gain.shape[0]
    count = tokens.shape[0] * tokens.shape[1] * tokens.shape[2]
    shard_rows = qkv_weight.shape[0]
    place = jnp.stack([lax.axis_index("height"), lax.axis_index("head")]).astype(jnp.int32)
    valid = key_valid.reshape(count, 1).astype(jnp.bfloat16)
    marked = jnp.concatenate([tokens.reshape(count, model), jnp.broadcast_to(valid, (count, LANES))], axis=1)
    up, down = spread_height(marked)
    joined = jnp.concatenate([qkv_weight.reshape(shard_rows, 3 * inner), out_weight], axis=1)
    along_width = lax.all_gather(joined, "width", axis=0, tiled=True)
    left, right = spread_width(marked, up, down)
    blocks = gather_height(along_width)
    q_gains, k_gains = q_gain.reshape(1, inner), k_gain.reshape(1, inner)
    anywhere = pl.BlockSpec(memory_space=pl.ANY)
    shape = jax.ShapeDtypeStruct
    half = jnp.bfloat16
    whole, queries, keys, values, marks, k_raw, grad_q, attended, message = pl.pallas_call(
        front_kernel,
        out_shape=(
            shape((model, 4 * inner), half),
            shape((EXTENDED, inner), half),
            shape((count, inner), half),
            shape((count, inner), half),
            shape((count, LANES), half),
            shape((count, inner), jnp.float32),
            shape((count, inner), half),
            shape((count, inner), half),
            shape((count, inner + LANES), half),
        ),
        in_specs=[pl.BlockSpec(memory_space=pltpu.SMEM)] + [anywhere] * 22 + [whole_spec()] * 2,
        out_specs=tuple(whole_spec() for _ in range(9)),
        scratch_shapes=[
            pltpu.VMEM((EXTENDED, model + LANES), half),
            pltpu.VMEM((count, model), half),
            pltpu.VMEM((EXTENDED, inner), half),
            pltpu.VMEM((EXTENDED, inner), half),
            pltpu.VMEM((EXTENDED, LANES), half),
            pltpu.VMEM((EXTENDED, 2 * inner), jnp.float32),
            pltpu.SemaphoreType.DMA((8,)),
            pltpu.SemaphoreType.DMA((16,)),
            pltpu.SemaphoreType.DMA((1,)),
        ],
        compiler_params=pltpu.CompilerParams(vmem_limit_bytes=VMEM_BYTES),
        name="front",
    )(place, marked, up, down, left, right, grad_out.reshape(count, model), *blocks, q_gains, k_gains)

    group = lax.axis_index("head")
    width = model // 2
    swap = lambda x: lax.ppermute(x, "head", [(0, 1), (1, 0)])
    part = lambda which: lax.dynamic_slice(whole, (which * width, 3 * inner), (width, inner))
    up, down = spread_height(message)
    mixed_sent = dot_rows(attended, part(1 - group)).astype(half)
    mixed_kept = dot_rows(attended, part(group)).astype(half)
    mixed_got = swap(mixed_sent)
    left, right = spread_width(message, up, down)
    kept, sent = pl.pallas_call(
        back_kernel,
        out_shape=(shape((count, width), half), shape((count, width), half)),
        in_specs=[pl.BlockSpec(memory_space=pltpu.SMEM)] + [anywhere] * 5 + [whole_spec()] * 8,
        out_specs=(whole_spec(), whole_spec()),
        scratch_shapes=[
            pltpu.VMEM((EXTENDED, inner + LANES), half),
            pltpu.VMEM((count, 3 * inner), half),
            pltpu.SemaphoreType.DMA((8,)),
        ],
        compiler_params=pltpu.CompilerParams(vmem_limit_bytes=VMEM_BYTES),
        name="back",
    )(place, message, up, down, left, right, queries, keys, values, marks, k_raw, grad_q, whole, k_gains)
    total = lambda a, b: (a.astype(jnp.float32) + b.astype(jnp.float32)).astype(half)
    mixed = total(mixed_kept, mixed_got)
    grad_in = total(kept, swap(sent))
    out_shape = tokens.shape[:3] + (width,)
    return (mixed.reshape(out_shape), grad_in.reshape(out_shape))


def solution(mesh):
    placed = (
        P("height", "width", None, None),
        P("height", "width", None, None),
        P(("height", "width"), None, "head"),
        P(("height", "width"), "head"),
        P("head"),
        P("head"),
        P("height", "width", None),
    )
    return jax.shard_map(
        on_device,
        mesh=mesh,
        in_specs=placed,
        out_specs=(P("height", "width", None, "head"), P("height", "width", None, "head")),
        check_vma=False,
    )
```

time: 278 us -> 199 us (0.72)
  waiting for transfers between devices: 89.4 us -> 49.4 us
  Pallas kernels: 0 us -> 29.7 us
  matrix products: 31 us -> 4.5 us
  other arithmetic: 27.4 us -> 6.02 us
  between operations: 14.7 us -> 1.02 us
  local copies, waits for them, and re-layouts: 19.6 us -> 7.04 us
  starting transfers between devices: 55.6 us -> 61.8 us
    reduce_scatter x2 -> x0, waiting for transfers between devices: 39.5 us -> none  [the longest x1 33.2 us: on_device(): lax.psum_scatter(grad_part.astype(jnp.bfloat16), 'head', scatter_dimensio...]
    pallas_call x0 -> x2, Pallas kernels: none -> 29.7 us  [the longest x1 20 us: on_device(): pl.pallas_call(front_kernel, out_shape=(shape((model, 4 * inner), half),...]
    all_gather x1 -> x0, waiting for transfers between devices: 24 us -> none  [on_device(): whole = lax.all_gather(along_width, 'height', axis=0, tiled=True)]
    ppermute x20, waiting for transfers between devices: 25.9 us -> 49.4 us  [the longest x2 25.8 us: spread_width(): right = lax.ppermute(column(0), 'width', steps('width', -1))]
    dot_general x9 -> x2, matrix products: 23.9 us -> 4.5 us  [dot_rows(): lax.dot_general(left, right, (((1,), (1,)), ((), ())), preferred_element_...]
    scatter-add x16 -> x0, other arithmetic: 7.59 us -> none  [fold_windows(): total.at[row_step:row_step + tile_rows, col_step:col_step + tile_cols]]
    div x1 -> x0, matrix products: 7.08 us -> none  [attend(): attn_probs = weights / jnp.sum(weights, axis=-1, keepdims=True)]
    ppermute x20, starting transfers between devices: 55.4 us -> 61.8 us  [the longest x6 18 us: gather_height(): shift = lambda x, by: lax.ppermute(x, 'height', steps('height', by, True))]
  transfers between devices with their start and end apart: 23 -> 20, of which waited for: 10 -> 11; matrix products, arithmetic and copies ran while one was open for 16% -> 7% of each run, Pallas kernels for 0% -> 5%
where the time goes in v2:
time: 199 us; the launch traced here: 197 us
  starting transfers between devices  61.8 us (31%)
  waiting for transfers between devices  49.4 us (25%)
  blocking collectives  37.7 us (19%)
  Pallas kernels  29.7 us (15%)
  local copies, waits for them, and re-layouts  7.04 us (4%)
  other arithmetic  6.02 us (3%)
  matrix products  4.5 us (2%)
    all_gather x1, blocking collectives, on_device(): along_width = lax.all_gather(joined, 'width', axis=0, tiled=True)  37.7 us
    ppermute x2, waiting for transfers between devices, spread_width(): right = lax.ppermute(column(0), 'width', steps('width', -1))  25.8 us
    pallas_call x1, Pallas kernels, on_device(): pl.pallas_call(front_kernel, out_shape=(shape((model, 4 * inner), half),...  20 us
    ppermute x6, starting transfers between devices, gather_height(): shift = lambda x, by: lax.ppermute(x, 'height', steps('height', by, True))  18 us
    pallas_call x1, Pallas kernels, on_device(): pl.pallas_call(back_kernel, out_shape=(shape((count, width), half), shape...  9.74 us
    ppermute x4, starting transfers between devices, flip(): return lax.ppermute(x, 'height', [(i, i ^ bit) for i in range(count)])  9.64 us
    ppermute x2, starting transfers between devices, on_device(): swap = lambda x: lax.ppermute(x, 'head', [(0, 1), (1, 0)])  9.61 us
    ppermute x2, starting transfers between devices, spread_width(): left = lax.ppermute(column(1), 'width', steps('width', 1))  9.42 us
  transfers between devices with their start and end apart: 20, of which 11 were waited for; matrix products, arithmetic and copies ran while one was open for 7% of the time, Pallas kernels for 5%

profile of v2, /device:TPU:6, one launch (start us, length us, event | category | flops | bytes accessed | tf_op | source)
XLA Modules:
  0.0 197.2 jit_solution(5162016566063094299)
XLA Ops:
  0.6 0.7 copy.9
  1.4 0.7 maximum_bitcast_fusion
  2.1 37.7 %all-gather = bf16[16,6,1536]{2,1,0:T(8,128)(2,1)S(1)} all-gather(bf16[1,6,1536]{2,1,0:T(8,128)(2,1)S(1)} %maximum_bitcast_fusion), channel_id=1, replica_groups=mesh['height'=16,'width'=16,'head'=2] {'width'}, dimensions={0}, use_global_device_ids=true | all-gather | bytes 313344 | tf_op jit(solution)/shard_map/all_gather | solution.py:239
  39.7 0.1 reshape.42.rest_0_
  39.8 3.5 %collective-permute-start.4 = (bf16[96,1536]{1,0:T(8,128)(2,1)S(1)}, bf16[96,1536]{1,0:T(8,128)(2,1)S(1)}, u32[]{:S(2)}, u32[]{:S(2)}) collective-permute-start(bf16[96,1536]{1,0:T(8,128)(2,1)S(1)} %reshape.42.rest_0_), channel_id=1, source_target_pairs={{0,64},{32,96},{64,0},{96,32},{128,192},{160,224},{192,128},{224,1... | collective-permute-start | bytes 884744 | tf_op jit(solution)/shard_map/ppermute | solution.py:206
  43.3 2.4 %collective-permute-start.5 = (bf16[96,1536]{1,0:T(8,128)(2,1)S(1)}, bf16[96,1536]{1,0:T(8,128)(2,1)S(1)}, u32[]{:S(2)}, u32[]{:S(2)}) collective-permute-start(bf16[96,1536]{1,0:T(8,128)(2,1)S(1)} %reshape.42.rest_0_), channel_id=1, source_target_pairs={{0,128},{32,160},{64,192},{96,224},{128,256},{160,288},{192,320},{... | collective-permute-start | bytes 884744 | tf_op jit(solution)/shard_map/ppermute | solution.py:210
  45.7 3.5 %collective-permute-start.6 = (bf16[96,1536]{1,0:T(8,128)(2,1)S(1)}, bf16[96,1536]{1,0:T(8,128)(2,1)S(1)}, u32[]{:S(2)}, u32[]{:S(2)}) collective-permute-start(bf16[96,1536]{1,0:T(8,128)(2,1)S(1)} %reshape.42.rest_0_), channel_id=1, source_target_pairs={{0,384},{32,416},{64,448},{96,480},{128,0},{160,32},{192,64},{224,... | collective-permute-start | bytes 884744 | tf_op jit(solution)/shard_map/ppermute | solution.py:210
  49.2 0.7 convert_element_type.35
  49.9 0.1 convert_element_type.36
  50.0 0.1 broadcast_in_dim.2
  50.1 1.2 pad_maximum_fusion.own
  51.3 0.0 copy-start.6
  51.3 0.0 copy-start.7
  51.4 2.1 %collective-permute-start = (bf16[288,1664]{1,0:T(8,128)(2,1)S(1)}, bf16[288,1664]{1,0:T(8,128)(2,1)}, u32[]{:S(2)}, u32[]{:S(2)}) collective-permute-start(bf16[288,1664]{1,0:T(8,128)(2,1)S(1)} %pad_maximum_fusion.own), channel_id=1, source_target_pairs={{0,32},{32,64},{64,96},{96,128},{128,160},{160,192},{192,224},{224... | collective-permute-start | bytes 2875400 | tf_op jit(solution)/shard_map/ppermute | solution.py:192
  53.4 2.7 %collective-permute-start.8 = (bf16[96,1536]{1,0:T(8,128)(2,1)S(1)}, bf16[96,1536]{1,0:T(8,128)(2,1)S(1)}, u32[]{:S(2)}, u32[]{:S(2)}) collective-permute-start(bf16[96,1536]{1,0:T(8,128)(2,1)S(1)} %collective-permute-done.4.rest_1_), channel_id=1, source_target_pairs={{0,384},{32,416},{64,448},{96,480},{128,0},{160,32},{192,64},{224,... | collective-permute-start | bytes 884744 | tf_op jit(solution)/shard_map/ppermute | solution.py:210
  56.2 2.0 %fusion.6 = (bf16[144,1664]{1,0:T(8,128)(2,1)}, bf16[144,1664]{1,0:T(8,128)(2,1)S(1)}) fusion(bf16[288,1536]{1,0:T(8,128)(2,1)} %bitcast.13, bf16[288,128]{1,0:T(8,128)(2,1)S(1)} %broadcast_in_dim.2), kind=kLoop, calls=%fused_computation.19 | loop fusion | flops 1916928 | bytes 1916928 | tf_op jit(solution)/shard_map/concatenate | solution.py:236
  58.2 4.3 %collective-permute-start.7 = (bf16[96,1536]{1,0:T(8,128)(2,1)S(1)}, bf16[96,1536]{1,0:T(8,128)(2,1)S(1)}, u32[]{:S(2)}, u32[]{:S(2)}) collective-permute-start(bf16[96,1536]{1,0:T(8,128)(2,1)S(1)} %collective-permute-done.4.rest_1_), channel_id=1, source_target_pairs={{0,128},{32,160},{64,192},{96,224},{128,256},{160,288},{192,320},{... | collective-permute-start | bytes 884744 | tf_op jit(solution)/shard_map/ppermute | solution.py:210
  62.5 0.1 pad_add_fusion.place
  62.6 0.0 collective-permute-done.5.rest_2_
  62.6 2.7 %collective-permute-start.9 = (bf16[96,1536]{1,0:T(8,128)(2,1)S(1)}, bf16[96,1536]{1,0:T(8,128)(2,1)S(1)}, u32[]{:S(2)}, u32[]{:S(2)}) collective-permute-start(bf16[96,1536]{1,0:T(8,128)(2,1)S(1)} %collective-permute-done.5.rest_2_), channel_id=1, source_target_pairs={{0,128},{32,160},{64,192},{96,224},{128,256},{160,288},{192,320},{... | collective-permute-start | bytes 884744 | tf_op jit(solution)/shard_map/ppermute | solution.py:210
  65.3 0.7 collective-permute-done.8.rest_5_
  66.0 2.5 %collective-permute-start.10 = (bf16[96,1536]{1,0:T(8,128)(2,1)S(1)}, bf16[96,1536]{1,0:T(8,128)(2,1)S(1)}, u32[]{:S(2)}, u32[]{:S(2)}) collective-permute-start(bf16[96,1536]{1,0:T(8,128)(2,1)S(1)} %collective-permute-done.8.rest_5_), channel_id=1, source_target_pairs={{0,384},{32,416},{64,448},{96,480},{128,0},{160,32},{192,64},{224,... | collective-permute-start | bytes 884744 | tf_op jit(solution)/shard_map/ppermute | solution.py:210
  68.5 2.2 %collective-permute-start.1 = (bf16[288,1664]{1,0:T(8,128)(2,1)S(1)}, bf16[288,1664]{1,0:T(8,128)(2,1)S(1)}, u32[]{:S(2)}, u32[]{:S(2)}) collective-permute-start(bf16[288,1664]{1,0:T(8,128)(2,1)S(1)} %pad_maximum_fusion.own), channel_id=1, source_target_pairs={{32,0},{64,32},{96,64},{128,96},{160,128},{192,160},{224,192},{256... | collective-permute-start | bytes 2875400 | tf_op jit(solution)/shard_map/ppermute | solution.py:193
  70.7 0.0 collective-permute-done.7.rest_4_
  70.8 2.1 %collective-permute-start.11 = (bf16[192,1536]{1,0:T(8,128)(2,1)S(1)}, bf16[192,1536]{1,0:T(8,128)(2,1)S(1)}, u32[]{:S(2)}, u32[]{:S(2)}) collective-permute-start(bf16[192,1536]{1,0:T(8,128)(2,1)S(1)} %pad_maximum_fusion.4), channel_id=1, source_target_pairs={{0,32},{32,0},{64,96},{96,64},{128,160},{160,128},{192,224},{224,1... | collective-permute-start | bytes 1769480 | tf_op jit(solution)/shard_map/ppermute | solution.py:206
  72.9 0.1 pad_maximum_fusion.3
  73.0 2.6 %collective-permute-done.9.rest_6_ = bf16[96,1536]{1,0:T(8,128)(2,1)S(1)} collective-permute-done((bf16[96,1536]{1,0:T(8,128)(2,1)S(1)}, bf16[96,1536]{1,0:T(8,128)(2,1)S(1)}, u32[]{:S(2)}, u32[]{:S(2)}) %collective-permute-start.9) | collective-permute-done | bytes 294944 | tf_op jit(solution)/shard_map/ppermute | solution.py:210
  75.6 1.9 collective-permute-start.12
  77.5 0.3 collective-permute-done.10.rest_7_
  77.8 2.1 %collective-permute-start.13 = (bf16[192,1536]{1,0:T(8,128)(2,1)S(1)}, bf16[192,1536]{1,0:T(8,128)(2,1)S(1)}, u32[]{:S(2)}, u32[]{:S(2)}) collective-permute-start(bf16[192,1536]{1,0:T(8,128)(2,1)S(1)} %pad_maximum_fusion.5), channel_id=1, source_target_pairs={{0,32},{32,0},{64,96},{96,64},{128,160},{160,128},{192,224},{224,1... | collective-permute-start | bytes 1769480 | tf_op jit(solution)/shard_map/ppermute | solution.py:206
  80.0 0.0 collective-permute-done.up
  80.0 1.2 fusion.10
  81.2 3.6 %collective-permute-done.1.down = bf16[288,1664]{1,0:T(8,128)(2,1)S(1)} collective-permute-done((bf16[288,1664]{1,0:T(8,128)(2,1)S(1)}, bf16[288,1664]{1,0:T(8,128)(2,1)S(1)}, u32[]{:S(2)}, u32[]{:S(2)}) %collective-permute-start.1) | collective-permute-done | bytes 958496 | tf_op jit(solution)/shard_map/ppermute | solution.py:193
  84.9 0.1 fusion.11
  84.9 0.1 pad_maximum_fusion.2
  85.1 0.7 copy-done.2
  85.8 1.3 collective-permute-start.3
  87.1 0.1 pad_maximum_fusion.1
  87.2 4.6 %collective-permute-start.2 = (bf16[432,1664]{1,0:T(8,128)(2,1)S(1)}, bf16[432,1664]{1,0:T(8,128)(2,1)S(1)}, u32[]{:S(2)}, u32[]{:S(2)}) collective-permute-start(bf16[432,1664]{1,0:T(8,128)(2,1)S(1)} %pad_maximum_fusion.1), channel_id=1, source_target_pairs={{0,2},{2,4},{4,6},{6,8},{8,10},{10,12},{12,14},{14,16},{16,18},{18... | collective-permute-start | bytes 4313096 | tf_op jit(solution)/shard_map/ppermute | solution.py:199
  91.9 0.8 fusion.13
  92.6 0.0 collective-permute-done.13
  92.6 0.8 fusion.12
  93.5 1.1 fusion.9
  94.6 24.8 %collective-permute-done.3.right = bf16[432,1664]{1,0:T(8,128)(2,1)S(1)} collective-permute-done((bf16[432,1664]{1,0:T(8,128)(2,1)S(1)}, bf16[432,1664]{1,0:T(8,128)(2,1)S(1)}, u32[]{:S(2)}, u32[]{:S(2)}) %collective-permute-start.3) | collective-permute-done | bytes 1437728 | tf_op jit(solution)/shard_map/ppermute | solution.py:200
  119.3 1.3 collective-permute-done.2.left
  120.6 1.1 copy-done.5
  121.8 20.0 %front.1 = (bf16[1536,1536]{1,0:T(8,128)(2,1)}, bf16[1728,384]{1,0:T(8,128)(2,1)}, bf16[288,384]{1,0:T(8,128)(2,1)S(1)}, bf16[288,384]{1,0:T(8,128)(2,1)S(1)}, b...) custom-call(s32[2]{0:T(128)S(1)} %pad_add_fusion.place, ...), custom_call_target="tpu_custom_call" | custom-call | tf_op jit(solution)/shard_map/front/pallas_call | solution.py:246
  141.8 1.9 collective-permute-start.15
  143.7 6.2 %collective-permute-start.16 = (bf16[288,512]{1,0:T(8,128)(2,1)S(1)}, bf16[288,512]{1,0:T(8,128)(2,1)S(1)}, u32[]{:S(2)}, u32[]{:S(2)}) collective-permute-start(bf16[288,512]{1,0:T(8,128)(2,1)S(1)} %get-tuple-element.15.own), channel_id=1, source_target_pairs={{32,0},{64,32},{96,64},{128,96},{160,128},{192,160},{224,192},{256... | collective-permute-start | bytes 884744 | tf_op jit(solution)/shard_map/ppermute | solution.py:193
  149.9 2.4 %collective-permute-done.15.up = bf16[288,512]{1,0:T(8,128)(2,1)S(1)} collective-permute-done((bf16[288,512]{1,0:T(8,128)(2,1)S(1)}, bf16[288,512]{1,0:T(8,128)(2,1)S(1)}, u32[]{:S(2)}, u32[]{:S(2)}) %collective-permute-start.15) | collective-permute-done | bytes 294944 | tf_op jit(solution)/shard_map/ppermute | solution.py:192
  152.4 1.7 collective-permute-done.16.down
  154.2 0.0 copy-start
  154.2 1.4 collective-permute-start.18
  155.7 4.8 %collective-permute-start.17 = (bf16[432,512]{1,0:T(8,128)(2,1)S(1)}, bf16[432,512]{1,0:T(8,128)(2,1)S(1)}, u32[]{:S(2)}, u32[]{:S(2)}) collective-permute-start(bf16[432,512]{1,0:T(8,128)(2,1)S(1)} %pad_maximum_fusion.6), channel_id=1, source_target_pairs={{0,2},{2,4},{4,6},{6,8},{8,10},{10,12},{12,14},{14,16},{16,18},{18... | collective-permute-start | bytes 1327112 | tf_op jit(solution)/shard_map/ppermute | solution.py:199
  160.5 2.2 %convolution_convert_fusion = bf16[288,768]{1,0:T(8,128)(2,1)} fusion(bf16[288,384]{1,0:T(8,128)(2,1)S(1)} %get-tuple-element.13, bf16[1536,1536]{1,0:T(8,128)(2,1)} %get-tuple-element.14.whole, s32[]{:T(128)S(6)} %select_n.7), kind=kOutput, calls=%fused_computation.5 | convolution fusion | flops 170090496 | bytes 1253380 | tf_op jit(solution)/shard_map/dot_general | solution.py:25
  162.7 4.9 %collective-permute-start.14 = (bf16[288,768]{1,0:T(8,128)(2,1)}, bf16[288,768]{1,0:T(8,128)(2,1)S(1)}, u32[]{:S(2)}, u32[]{:S(2)}) collective-permute-start(bf16[288,768]{1,0:T(8,128)(2,1)} %convolution_convert_fusion), channel_id=1, source_target_pairs={{0,1},{1,0},{2,3},{3,2},{4,5},{5,4},{6,7},{7,6},{8,9},{9,8},{10,11... | collective-permute-start | bytes 1327112 | tf_op jit(solution)/shard_map/ppermute | solution.py:278
  167.7 1.0 collective-permute-done.18.right
  168.7 1.8 collective-permute-done.17.left
  170.5 9.7 %back.1 = (bf16[288,768]{1,0:T(8,128)(2,1)S(1)}, bf16[288,768]{1,0:T(8,128)(2,1)S(1)}) custom-call(s32[2]{0:T(128)S(1)} %pad_add_fusion.place, bf16[288,512]{1,0:T(8,128)(2,1)S(1)} %get-tuple-element.15.own, bf16[288,512]{1,0:T(8,128)(2,1)S(1)} %collective-permute-done.15.up, bf16[288,512]{1,0:T(8,128)(2,1)S(1)} %collective-permute-done.16.down, ...), custom_call_target="tpu_custom_call" | custom-call | tf_op jit(solution)/shard_map/back/pallas_call | solution.py:285
  180.3 4.7 %collective-permute-start.19 = (bf16[288,768]{1,0:T(8,128)(2,1)S(1)}, bf16[288,768]{1,0:T(8,128)(2,1)S(1)}, u32[]{:S(2)}, u32[]{:S(2)}) collective-permute-start(bf16[288,768]{1,0:T(8,128)(2,1)S(1)} %get-tuple-element.23), channel_id=1, source_target_pairs={{0,1},{1,0},{2,3},{3,2},{4,5},{5,4},{6,7},{7,6},{8,9},{9,8},{10,11... | collective-permute-start | bytes 1327112 | tf_op jit(solution)/shard_map/ppermute | solution.py:278
  185.0 0.0 collective-permute-done.14
  185.0 2.2 %fusion.2 = bf16[288,768]{1,0:T(8,128)(2,1)} fusion(bf16[288,384]{1,0:T(8,128)(2,1)S(1)} %get-tuple-element.13, bf16[288,768]{1,0:T(8,128)(2,1)S(1)} %collective-permute-done.14, bf16[1536,1536]{1,0:T(8,128)(2,1)} %get-tuple-element.14.whole, s32[]{:T(128)S(6)} %select_n.6), kind=kOutput, calls=%fused_computation.9 | convolution fusion | flops 170975232 | bytes 1695748 | tf_op jit(solution)/shard_map/dot_general | solution.py:25
  187.2 9.1 %collective-permute-done.19 = bf16[288,768]{1,0:T(8,128)(2,1)S(1)} collective-permute-done((bf16[288,768]{1,0:T(8,128)(2,1)S(1)}, bf16[288,768]{1,0:T(8,128)(2,1)S(1)}, u32[]{:S(2)}, u32[]{:S(2)}) %collective-permute-start.19) | collective-permute-done | bytes 442400 | tf_op jit(solution)/shard_map/ppermute | solution.py:278
  196.3 0.9 add_convert_fusion
  (24 shorter events, 0.2 us)
Async XLA Ops:
  39.8 13.6 %collective-permute-start.4 = (bf16[96,1536]{1,0:T(8,128)(2,1)S(1)}, bf16[96,1536]{1,0:T(8,128)(2,1)S(1)}, u32[]{:S(2)}, u32[]{:S(2)}) collective-permute-start(bf16[96,1536]{1,0:T(8,128)(2,1)S(1)} %reshape.42.rest_0_), channel_id=1, source_target_pairs={{0,64},{32,96},{64,0},{96,32},{128,192},{160,224},{192,128},{224,1... | collective-permute-start | bytes 884744 | tf_op jit(solution)/shard_map/ppermute | solution.py:206
  43.3 19.3 %collective-permute-start.5 = (bf16[96,1536]{1,0:T(8,128)(2,1)S(1)}, bf16[96,1536]{1,0:T(8,128)(2,1)S(1)}, u32[]{:S(2)}, u32[]{:S(2)}) collective-permute-start(bf16[96,1536]{1,0:T(8,128)(2,1)S(1)} %reshape.42.rest_0_), channel_id=1, source_target_pairs={{0,128},{32,160},{64,192},{96,224},{128,256},{160,288},{192,320},{... | collective-permute-start | bytes 884744 | tf_op jit(solution)/shard_map/ppermute | solution.py:210
  45.7 22.8 %collective-permute-start.6 = (bf16[96,1536]{1,0:T(8,128)(2,1)S(1)}, bf16[96,1536]{1,0:T(8,128)(2,1)S(1)}, u32[]{:S(2)}, u32[]{:S(2)}) collective-permute-start(bf16[96,1536]{1,0:T(8,128)(2,1)S(1)} %reshape.42.rest_0_), channel_id=1, source_target_pairs={{0,384},{32,416},{64,448},{96,480},{128,0},{160,32},{192,64},{224,... | collective-permute-start | bytes 884744 | tf_op jit(solution)/shard_map/ppermute | solution.py:210
  51.3 17.2 %copy-start.1 = (bf16[288,1664]{1,0:T(8,128)(2,1)}, bf16[288,1664]{1,0:T(8,128)(2,1)S(1)}, u32[]{:S(2)}) copy-start(bf16[288,1664]{1,0:T(8,128)(2,1)S(1)} %pad_maximum_fusion.own) | copy-start | bytes 2875396
  51.3 11.2 %copy-start.6 = (f32[384]{0:T(512)S(1)}, f32[384]{0:T(512)}, u32[]{:S(2)}) copy-start(f32[384]{0:T(512)} %param.12) | copy-start | bytes 4612
  51.3 11.2 %copy-start.7 = (f32[384]{0:T(512)S(1)}, f32[384]{0:T(512)}, u32[]{:S(2)}) copy-start(f32[384]{0:T(512)} %param.11) | copy-start | bytes 4612
  51.4 28.6 %collective-permute-start = (bf16[288,1664]{1,0:T(8,128)(2,1)S(1)}, bf16[288,1664]{1,0:T(8,128)(2,1)}, u32[]{:S(2)}, u32[]{:S(2)}) collective-permute-start(bf16[288,1664]{1,0:T(8,128)(2,1)S(1)} %pad_maximum_fusion.own), channel_id=1, source_target_pairs={{0,32},{32,64},{64,96},{96,128},{128,160},{160,192},{192,224},{224... | collective-permute-start | bytes 2875400 | tf_op jit(solution)/shard_map/ppermute | solution.py:192
  53.4 12.6 %collective-permute-start.8 = (bf16[96,1536]{1,0:T(8,128)(2,1)S(1)}, bf16[96,1536]{1,0:T(8,128)(2,1)S(1)}, u32[]{:S(2)}, u32[]{:S(2)}) collective-permute-start(bf16[96,1536]{1,0:T(8,128)(2,1)S(1)} %collective-permute-done.4.rest_1_), channel_id=1, source_target_pairs={{0,384},{32,416},{64,448},{96,480},{128,0},{160,32},{192,64},{224,... | collective-permute-start | bytes 884744 | tf_op jit(solution)/shard_map/ppermute | solution.py:210
  58.2 12.6 %collective-permute-start.7 = (bf16[96,1536]{1,0:T(8,128)(2,1)S(1)}, bf16[96,1536]{1,0:T(8,128)(2,1)S(1)}, u32[]{:S(2)}, u32[]{:S(2)}) collective-permute-start(bf16[96,1536]{1,0:T(8,128)(2,1)S(1)} %collective-permute-done.4.rest_1_), channel_id=1, source_target_pairs={{0,128},{32,160},{64,192},{96,224},{128,256},{160,288},{192,320},{... | collective-permute-start | bytes 884744 | tf_op jit(solution)/shard_map/ppermute | solution.py:210
  62.6 13.0 %collective-permute-start.9 = (bf16[96,1536]{1,0:T(8,128)(2,1)S(1)}, bf16[96,1536]{1,0:T(8,128)(2,1)S(1)}, u32[]{:S(2)}, u32[]{:S(2)}) collective-permute-start(bf16[96,1536]{1,0:T(8,128)(2,1)S(1)} %collective-permute-done.5.rest_2_), channel_id=1, source_target_pairs={{0,128},{32,160},{64,192},{96,224},{128,256},{160,288},{192,320},{... | collective-permute-start | bytes 884744 | tf_op jit(solution)/shard_map/ppermute | solution.py:210
  66.0 11.8 %collective-permute-start.10 = (bf16[96,1536]{1,0:T(8,128)(2,1)S(1)}, bf16[96,1536]{1,0:T(8,128)(2,1)S(1)}, u32[]{:S(2)}, u32[]{:S(2)}) collective-permute-start(bf16[96,1536]{1,0:T(8,128)(2,1)S(1)} %collective-permute-done.8.rest_5_), channel_id=1, source_target_pairs={{0,384},{32,416},{64,448},{96,480},{128,0},{160,32},{192,64},{224,... | collective-permute-start | bytes 884744 | tf_op jit(solution)/shard_map/ppermute | solution.py:210
  68.5 16.3 %collective-permute-start.1 = (bf16[288,1664]{1,0:T(8,128)(2,1)S(1)}, bf16[288,1664]{1,0:T(8,128)(2,1)S(1)}, u32[]{:S(2)}, u32[]{:S(2)}) collective-permute-start(bf16[288,1664]{1,0:T(8,128)(2,1)S(1)} %pad_maximum_fusion.own), channel_id=1, source_target_pairs={{32,0},{64,32},{96,64},{128,96},{160,128},{192,160},{224,192},{256... | collective-permute-start | bytes 2875400 | tf_op jit(solution)/shard_map/ppermute | solution.py:193
  70.8 21.1 %collective-permute-start.11 = (bf16[192,1536]{1,0:T(8,128)(2,1)S(1)}, bf16[192,1536]{1,0:T(8,128)(2,1)S(1)}, u32[]{:S(2)}, u32[]{:S(2)}) collective-permute-start(bf16[192,1536]{1,0:T(8,128)(2,1)S(1)} %pad_maximum_fusion.4), channel_id=1, source_target_pairs={{0,32},{32,0},{64,96},{96,64},{128,160},{160,128},{192,224},{224,1... | collective-permute-start | bytes 1769480 | tf_op jit(solution)/shard_map/ppermute | solution.py:206
  75.6 17.9 %collective-permute-start.12 = (bf16[384,1536]{1,0:T(8,128)(2,1)S(1)}, bf16[384,1536]{1,0:T(8,128)(2,1)S(1)}, u32[]{:S(2)}, u32[]{:S(2)}) collective-permute-start(bf16[384,1536]{1,0:T(8,128)(2,1)S(1)} %pad_maximum_fusion.3), channel_id=1, source_target_pairs={{0,32},{32,0},{64,96},{96,64},{128,160},{160,128},{192,224},{224,1... | collective-permute-start | bytes 3538952 | tf_op jit(solution)/shard_map/ppermute | solution.py:206
  77.8 14.8 %collective-permute-start.13 = (bf16[192,1536]{1,0:T(8,128)(2,1)S(1)}, bf16[192,1536]{1,0:T(8,128)(2,1)S(1)}, u32[]{:S(2)}, u32[]{:S(2)}) collective-permute-start(bf16[192,1536]{1,0:T(8,128)(2,1)S(1)} %pad_maximum_fusion.5), channel_id=1, source_target_pairs={{0,32},{32,0},{64,96},{96,64},{128,160},{160,128},{192,224},{224,1... | collective-permute-start | bytes 1769480 | tf_op jit(solution)/shard_map/ppermute | solution.py:206
  81.2 3.7 %copy-start.3 = (bf16[144,1664]{1,0:T(8,128)(2,1)S(1)}, bf16[144,1664]{1,0:T(8,128)(2,1)}, u32[]{:S(2)}) copy-start(bf16[144,1664]{1,0:T(8,128)(2,1)} %get-tuple-element.30) | copy-start | bytes 1437700
  84.9 0.9 copy-start.2
  85.8 33.5 %collective-permute-start.3 = (bf16[432,1664]{1,0:T(8,128)(2,1)S(1)}, bf16[432,1664]{1,0:T(8,128)(2,1)S(1)}, u32[]{:S(2)}, u32[]{:S(2)}) collective-permute-start(bf16[432,1664]{1,0:T(8,128)(2,1)S(1)} %pad_maximum_fusion.2), channel_id=1, source_target_pairs={{2,0},{4,2},{6,4},{8,6},{10,8},{12,10},{14,12},{16,14},{18,16},{20... | collective-permute-start | bytes 4313096 | tf_op jit(solution)/shard_map/ppermute | solution.py:200
  87.2 33.4 %collective-permute-start.2 = (bf16[432,1664]{1,0:T(8,128)(2,1)S(1)}, bf16[432,1664]{1,0:T(8,128)(2,1)S(1)}, u32[]{:S(2)}, u32[]{:S(2)}) collective-permute-start(bf16[432,1664]{1,0:T(8,128)(2,1)S(1)} %pad_maximum_fusion.1), channel_id=1, source_target_pairs={{0,2},{2,4},{4,6},{6,8},{8,10},{10,12},{12,14},{14,16},{16,18},{18... | collective-permute-start | bytes 4313096 | tf_op jit(solution)/shard_map/ppermute | solution.py:199
  119.3 1.3 copy-start.4
  120.6 1.1 copy-start.5
  141.8 10.6 %collective-permute-start.15 = (bf16[288,512]{1,0:T(8,128)(2,1)S(1)}, bf16[288,512]{1,0:T(8,128)(2,1)S(1)}, u32[]{:S(2)}, u32[]{:S(2)}) collective-permute-start(bf16[288,512]{1,0:T(8,128)(2,1)S(1)} %get-tuple-element.15.own), channel_id=1, source_target_pairs={{0,32},{32,64},{64,96},{96,128},{128,160},{160,192},{192,224},{224... | collective-permute-start | bytes 884744 | tf_op jit(solution)/shard_map/ppermute | solution.py:192
  143.7 10.4 %collective-permute-start.16 = (bf16[288,512]{1,0:T(8,128)(2,1)S(1)}, bf16[288,512]{1,0:T(8,128)(2,1)S(1)}, u32[]{:S(2)}, u32[]{:S(2)}) collective-permute-start(bf16[288,512]{1,0:T(8,128)(2,1)S(1)} %get-tuple-element.15.own), channel_id=1, source_target_pairs={{32,0},{64,32},{96,64},{128,96},{160,128},{192,160},{224,192},{256... | collective-permute-start | bytes 884744 | tf_op jit(solution)/shard_map/ppermute | solution.py:193
  154.2 16.4 %copy-start = (f32[288,384]{1,0:T(8,128)S(1)}, f32[288,384]{1,0:T(8,128)}, u32[]{:S(2)}) copy-start(f32[288,384]{1,0:T(8,128)} %get-tuple-element.20.k_raw) | copy-start | bytes 1327108
  154.2 14.5 %collective-permute-start.18 = (bf16[432,512]{1,0:T(8,128)(2,1)S(1)}, bf16[432,512]{1,0:T(8,128)(2,1)S(1)}, u32[]{:S(2)}, u32[]{:S(2)}) collective-permute-start(bf16[432,512]{1,0:T(8,128)(2,1)S(1)} %pad_maximum_fusion.7), channel_id=1, source_target_pairs={{2,0},{4,2},{6,4},{8,6},{10,8},{12,10},{14,12},{16,14},{18,16},{20... | collective-permute-start | bytes 1327112 | tf_op jit(solution)/shard_map/ppermute | solution.py:200
  155.7 14.8 %collective-permute-start.17 = (bf16[432,512]{1,0:T(8,128)(2,1)S(1)}, bf16[432,512]{1,0:T(8,128)(2,1)S(1)}, u32[]{:S(2)}, u32[]{:S(2)}) collective-permute-start(bf16[432,512]{1,0:T(8,128)(2,1)S(1)} %pad_maximum_fusion.6), channel_id=1, source_target_pairs={{0,2},{2,4},{4,6},{6,8},{8,10},{10,12},{12,14},{14,16},{16,18},{18... | collective-permute-start | bytes 1327112 | tf_op jit(solution)/shard_map/ppermute | solution.py:199
  162.7 22.2 %collective-permute-start.14 = (bf16[288,768]{1,0:T(8,128)(2,1)}, bf16[288,768]{1,0:T(8,128)(2,1)S(1)}, u32[]{:S(2)}, u32[]{:S(2)}) collective-permute-start(bf16[288,768]{1,0:T(8,128)(2,1)} %convolution_convert_fusion), channel_id=1, source_target_pairs={{0,1},{1,0},{2,3},{3,2},{4,5},{5,4},{6,7},{7,6},{8,9},{9,8},{10,11... | collective-permute-start | bytes 1327112 | tf_op jit(solution)/shard_map/ppermute | solution.py:278
  180.3 16.1 %collective-permute-start.19 = (bf16[288,768]{1,0:T(8,128)(2,1)S(1)}, bf16[288,768]{1,0:T(8,128)(2,1)S(1)}, u32[]{:S(2)}, u32[]{:S(2)}) collective-permute-start(bf16[288,768]{1,0:T(8,128)(2,1)S(1)} %get-tuple-element.23), channel_id=1, source_target_pairs={{0,1},{1,0},{2,3},{3,2},{4,5},{5,4},{6,7},{7,6},{8,9},{9,8},{10,11... | collective-permute-start | bytes 1327112 | tf_op jit(solution)/shard_map/ppermute | solution.py:278

commit v3 on v2

--- a/solution.py
+++ b/solution.py
@@ -71,49 +71,67 @@
 
 
 def front_kernel(place, own, up, down, left, right, upstream, *rest):
-    blocks, rest = rest[:16], rest[16:]
-    (q_gain, k_gain, whole, queries, own_keys, own_values, own_marks, own_k_raw, grad_q, attended,
-     message, tok, grad, keys, values, marks, raw, token_sems, block_sems, grad_sem) = rest
+    pieces, rest = rest[:4], rest[4:]
+    (q_gain, k_gain, whole_out, own_keys, own_values, own_marks, own_k_raw, grad_q, attended, message,
+     whole, tok, grad, keys, values, marks, own_raw, own_queries, token_sems, block_sems, grad_sem, whole_sem) = rest
     here = place[0]
     north, south = lax.rem(here + 12, 16), lax.rem(here + 4, 16)
     far = lax.rem(here + 8, 16)
-    spots = [here, here ^ 2, north, south, north ^ 2, south ^ 2, far, far ^ 2]
-    spots = spots + [spot ^ 1 for spot in spots]
+    near = [here, here ^ 2, north, north ^ 2, south, south ^ 2]
+    spots = [near, [far, far ^ 2], [spot ^ 1 for spot in near], [far ^ 1, far ^ 3]]
+    parts = [(piece, n, spot) for piece, some in zip(pieces, spots) for n, spot in enumerate(some)]
     block_copies = [
-        pltpu.make_async_copy(block, whole.at[pl.ds(pl.multiple_of(spot * 96, 96), 96)], block_sems.at[n])
-        for n, (block, spot) in enumerate(zip(blocks, spots))
+        pltpu.make_async_copy(
+            piece.at[pl.ds(n * 96, 96)], whole.at[pl.ds(pl.multiple_of(spot * 96, 96), 96)], block_sems.at[i]
+        )
+        for i, (piece, n, spot) in enumerate(parts)
     ]
     grad_copy = pltpu.make_async_copy(upstream, grad, grad_sem.at[0])
     token_copies = extended_copies(own, up, down, left, right, tok, token_sems)
+    whole_copy = pltpu.make_async_copy(whole, whole_out, whole_sem.at[0])
     for copy in block_copies + [grad_copy] + token_copies:
         copy.start()
     for copy in block_copies + [grad_copy]:
         copy.wait()
-    heads = range(queries.shape[1] // HEAD_DIM)
-    inner = queries.shape[1]
+    whole_copy.start()
+    inner = own_keys.shape[1]
+    heads = range(inner // HEAD_DIM)
     model = whole.shape[0]
     message[:, :inner] = dot_plain(grad[...], whole[:, 3 * inner :]).astype(jnp.bfloat16)
     for copy in token_copies:
         copy.wait()
     chunk = 2 * TILE
 
+    for tile, at in enumerate(OWN_TILES):
+        mine = slice(tile * TILE, (tile + 1) * TILE)
+        own_queries[mine, :] = tok[at * TILE : (at + 1) * TILE, :model]
+    result = dot_plain(own_queries[:, :model], whole[:, :inner])
+    own_raw[...] = result
+    for head in heads:
+        lanes = slice(head * HEAD_DIM, (head + 1) * HEAD_DIM)
+        own_queries[:, lanes] = (result[:, lanes] * norm_inverse(result[:, lanes]) * q_gain[:, lanes]).astype(jnp.bfloat16)
+
     def project(step, carry):
         rows = pl.ds(pl.multiple_of(step * chunk, chunk), chunk)
-        result = dot_plain(tok[rows, :model], whole[:, : 3 * inner])
-        raw[rows, :] = result[:, : 2 * inner]
+        result = dot_plain(tok[rows, :model], whole[:, inner : 3 * inner])
         for head in heads:
             lanes = slice(head * HEAD_DIM, (head + 1) * HEAD_DIM)
-            q_raw = result[:, lanes]
-            queries[rows, lanes] = (q_raw * norm_inverse(q_raw) * q_gain[:, lanes]).astype(jnp.bfloat16)
-            k_raw = result[:, inner:][:, lanes]
+            k_raw = result[:, lanes]
             keys[rows, lanes] = (k_raw * norm_inverse(k_raw) * k_gain[:, lanes]).astype(jnp.bfloat16)
-        values[rows, :] = result[:, 2 * inner :].astype(jnp.bfloat16)
+        values[rows, :] = result[:, inner:].astype(jnp.bfloat16)
         valid = tok[rows, model:].astype(jnp.float32)
         deep = jnp.where(lane_index(chunk) == MASK_LANE, MASK_DEPTH, 0.0)
         marks[rows, :] = (valid * deep - deep).astype(jnp.bfloat16)
+        for tile, at in enumerate(OWN_TILES):
+            offset = at * TILE % chunk
+
+            @pl.when(step == at * TILE // chunk)
+            def keep():
+                own_k_raw[tile * TILE : (tile + 1) * TILE, :] = result[offset : offset + TILE, :inner]
+
         return carry
 
-    lax.fori_loop(0, EXTENDED // chunk, project, 0)
+    lax.fori_loop(0, EXTENDED // chunk, project, 0, unroll=True)
     lane = lane_index(TILE)
     one_mark = jnp.where(lane == MASK_LANE, 1.0, 0.0)
     for tile, at in enumerate(OWN_TILES):
@@ -123,7 +141,7 @@
         stats = one_mark
         for head in heads:
             lanes = slice(head * HEAD_DIM, (head + 1) * HEAD_DIM)
-            q_aug = jnp.concatenate([queries[ext, lanes], one_mark.astype(jnp.bfloat16)], axis=1)
+            q_aug = jnp.concatenate([own_queries[mine, lanes], one_mark.astype(jnp.bfloat16)], axis=1)
             win_keys = keys[window, lanes]
             win_values = values[window, lanes]
             k_aug = jnp.concatenate([win_keys, marks[window, :]], axis=1)
@@ -135,7 +153,7 @@
             delta = jnp.sum(probs * grad_probs, axis=-1, keepdims=True)
             grad_scores = (probs * (grad_probs - delta)).astype(jnp.bfloat16)
             upstream_q = dot_plain(grad_scores, win_keys) * FACTOR
-            grad_q[mine, lanes] = norm_backward(raw[ext, lanes], q_gain[:, lanes], upstream_q).astype(jnp.bfloat16)
+            grad_q[mine, lanes] = norm_backward(own_raw[mine, lanes], q_gain[:, lanes], upstream_q).astype(jnp.bfloat16)
             for n, part in enumerate(three_parts(jnp.log(total) * (1.0 / FACTOR))):
                 stats = jnp.where(lane == 3 * head + n, part, stats)
             for n, part in enumerate(three_parts(delta)):
@@ -144,17 +162,41 @@
         own_keys[mine, :] = keys[ext, :]
         own_values[mine, :] = values[ext, :]
         own_marks[mine, :] = marks[ext, :]
-        own_k_raw[mine, :] = raw[ext, inner:]
+    whole_copy.wait()
+
+
+def queries_kernel(own, up, down, left, right, whole, q_gain, queries, weight, tok, sems, weight_sem):
+    inner = weight.shape[1]
+    model = weight.shape[0]
+    weight_copy = pltpu.make_async_copy(whole.at[:, pl.ds(0, inner)], weight, weight_sem.at[0])
+    copies = extended_copies(own, up, down, left, right, tok, sems)
+    for copy in [weight_copy] + copies:
+        copy.start()
+    for copy in [weight_copy] + copies:
+        copy.wait()
+    chunk = 4 * TILE
+
+    def project(step, carry):
+        rows = pl.ds(pl.multiple_of(step * chunk, chunk), chunk)
+        result = dot_plain(tok[rows, :model], weight[...])
+        for head in range(inner // HEAD_DIM):
+            lanes = slice(head * HEAD_DIM, (head + 1) * HEAD_DIM)
+            q_raw = result[:, lanes]
+            queries[rows, lanes] = (q_raw * norm_inverse(q_raw) * q_gain[:, lanes]).astype(jnp.bfloat16)
+        return carry
+
+    lax.fori_loop(0, EXTENDED // chunk, project, 0)
 
 
 def back_kernel(place, own, up, down, left, right, queries, keys, values, marks, k_raw, grad_q, whole, k_gain,
-                kept, sent, ext, grad_qkv, sems):
+                kept, sent, ext, grad_qkv, weight, sems, weight_sem):
+    inner = queries.shape[1]
     copies = extended_copies(own, up, down, left, right, ext, sems)
-    for copy in copies:
+    weight_copy = pltpu.make_async_copy(whole.at[:, pl.ds(0, 3 * inner)], weight, weight_sem.at[0])
+    for copy in copies + [weight_copy]:
         copy.start()
     for copy in copies:
         copy.wait()
-    inner = queries.shape[1]
     grad_qkv[:, :inner] = grad_q[...]
     lane = lane_index(TILE)
     for tile in range(2):
@@ -177,10 +219,11 @@
             grad_k = norm_backward(k_raw[mine, lanes], k_gain[:, lanes], upstream_k)
             grad_qkv[mine, inner + head * HEAD_DIM : inner + (head + 1) * HEAD_DIM] = grad_k.astype(jnp.bfloat16)
             grad_qkv[mine, 2 * inner + head * HEAD_DIM : 2 * inner + (head + 1) * HEAD_DIM] = grad_v.astype(jnp.bfloat16)
+    weight_copy.wait()
     half = kept.shape[1]
     for target, group in ((sent, 1 - place[1]), (kept, place[1])):
         rows = pl.ds(pl.multiple_of(group * half, half), half)
-        target[...] = dot_rows(grad_qkv[...], whole[rows, : 3 * inner]).astype(jnp.bfloat16)
+        target[...] = dot_rows(grad_qkv[...], weight[rows, :]).astype(jnp.bfloat16)
 
 
 def steps(axis, shift, wrap=False):
@@ -194,11 +237,14 @@
     return up, down
 
 
-def spread_width(own, up, down):
-    column = lambda i: jnp.concatenate([part[i * TILE : (i + 1) * TILE] for part in (up, own, down)], axis=0)
-    left = lax.ppermute(column(1), "width", steps("width", 1))
-    right = lax.ppermute(column(0), "width", steps("width", -1))
+def spread_width(first, last):
+    left = lax.ppermute(last, "width", steps("width", 1))
+    right = lax.ppermute(first, "width", steps("width", -1))
     return left, right
+
+
+def joined_columns(up, own, down):
+    return [jnp.concatenate([part[i * TILE : (i + 1) * TILE] for part in (up, own, down)], axis=0) for i in (0, 1)]
 
 
 def flip(x, bit):
@@ -206,20 +252,46 @@
     return lax.ppermute(x, "height", [(i, i ^ bit) for i in range(count)])
 
 
-def gather_height(block):
+def gather_height(block, up, own, down):
     shift = lambda x, by: lax.ppermute(x, "height", steps("height", by, True))
     rows = block.shape[0]
-    north, south = shift(block, 4), shift(block, -4)
-    beside = flip(block, 2)
-    north_beside, south_beside = shift(beside, 4), shift(beside, -4)
-    far, far_beside = shift(north, 4), shift(south_beside, -4)
-    mine = [block, beside, north, south, north_beside, south_beside, far, far_beside]
-    groups = [mine[:2], mine[2:6], mine[6:]]
-    other = []
-    for group in groups:
-        swapped = flip(jnp.concatenate(group, axis=0), 1)
-        other += [swapped[n * rows : (n + 1) * rows] for n in range(len(group))]
-    return mine + other
+    pair = jnp.concatenate([block, flip(block, 2)], axis=0)
+    pair, first, last = lax.optimization_barrier((pair, *columns(up, own, down)))
+    left, right = spread_width(first, last)
+    north, south = shift(pair, 4), shift(pair, -4)
+    far, far_beside = shift(north[:rows], 4), shift(south[rows:], -4)
+    near = jnp.concatenate([pair, north, south], axis=0)
+    near, far = lax.optimization_barrier((near, far))
+    near_swapped = flip(near, 1)
+    far_beside, left, right = lax.optimization_barrier((far_beside, left, right))
+    far = jnp.concatenate([far, far_beside], axis=0)
+    return [near, far, near_swapped, flip(far, 1)], left, right
+
+
+def columns_kernel(up, own, down, first, last, sems):
+    copies = [
+        pltpu.make_async_copy(part.at[pl.ds(side * TILE, TILE)], target.at[pl.ds(n * TILE, TILE)], sems.at[3 * side + n])
+        for side, target in enumerate((first, last))
+        for n, part in enumerate((up, own, down))
+    ]
+    for copy in copies:
+        copy.start()
+    for copy in copies:
+        copy.wait()
+
+
+def columns(up, own, down):
+    anywhere = pl.BlockSpec(memory_space=pl.ANY)
+    out = jax.ShapeDtypeStruct((COLUMN, own.shape[1]), own.dtype)
+    return pl.pallas_call(
+        columns_kernel,
+        out_shape=(out, out),
+        in_specs=[anywhere] * 3,
+        out_specs=(whole_spec(), whole_spec()),
+        scratch_shapes=[pltpu.SemaphoreType.DMA((6,))],
+        compiler_params=pltpu.CompilerParams(vmem_limit_bytes=VMEM_BYTES),
+        name="columns",
+    )(up, own, down)
 
 
 def whole_spec():
@@ -237,17 +309,16 @@
     up, down = spread_height(marked)
     joined = jnp.concatenate([qkv_weight.reshape(shard_rows, 3 * inner), out_weight], axis=1)
     along_width = lax.all_gather(joined, "width", axis=0, tiled=True)
-    left, right = spread_width(marked, up, down)
-    blocks = gather_height(along_width)
+    along_width, up, down = lax.optimization_barrier((along_width, up, down))
+    blocks, left, right = gather_height(along_width, up, marked, down)
     q_gains, k_gains = q_gain.reshape(1, inner), k_gain.reshape(1, inner)
     anywhere = pl.BlockSpec(memory_space=pl.ANY)
     shape = jax.ShapeDtypeStruct
     half = jnp.bfloat16
-    whole, queries, keys, values, marks, k_raw, grad_q, attended, message = pl.pallas_call(
+    whole, keys, values, marks, k_raw, grad_q, attended, message = pl.pallas_call(
         front_kernel,
         out_shape=(
             shape((model, 4 * inner), half),
-            shape((EXTENDED, inner), half),
             shape((count, inner), half),
             shape((count, inner), half),
             shape((count, LANES), half),
@@ -256,17 +327,20 @@
             shape((count, inner), half),
             shape((count, inner + LANES), half),
         ),
-        in_specs=[pl.BlockSpec(memory_space=pltpu.SMEM)] + [anywhere] * 22 + [whole_spec()] * 2,
-        out_specs=tuple(whole_spec() for _ in range(9)),
+        in_specs=[pl.BlockSpec(memory_space=pltpu.SMEM)] + [anywhere] * 10 + [whole_spec()] * 2,
+        out_specs=(anywhere,) + tuple(whole_spec() for _ in range(7)),
         scratch_shapes=[
+            pltpu.VMEM((model, 4 * inner), half),
             pltpu.VMEM((EXTENDED, model + LANES), half),
             pltpu.VMEM((count, model), half),
             pltpu.VMEM((EXTENDED, inner), half),
             pltpu.VMEM((EXTENDED, inner), half),
             pltpu.VMEM((EXTENDED, LANES), half),
-            pltpu.VMEM((EXTENDED, 2 * inner), jnp.float32),
+            pltpu.VMEM((count, inner), jnp.float32),
+            pltpu.VMEM((count, model), half),
             pltpu.SemaphoreType.DMA((8,)),
             pltpu.SemaphoreType.DMA((16,)),
+            pltpu.SemaphoreType.DMA((1,)),
             pltpu.SemaphoreType.DMA((1,)),
         ],
         compiler_params=pltpu.CompilerParams(vmem_limit_bytes=VMEM_BYTES),
@@ -277,20 +351,40 @@
     width = model // 2
     swap = lambda x: lax.ppermute(x, "head", [(0, 1), (1, 0)])
     part = lambda which: lax.dynamic_slice(whole, (which * width, 3 * inner), (width, inner))
+    beyond = (marked, up, down, left, right)
     up, down = spread_height(message)
     mixed_sent = dot_rows(attended, part(1 - group)).astype(half)
+    up, down, mixed_sent = lax.optimization_barrier((up, down, mixed_sent))
     mixed_kept = dot_rows(attended, part(group)).astype(half)
     mixed_got = swap(mixed_sent)
-    left, right = spread_width(message, up, down)
+    left, right = spread_width(*joined_columns(up, message, down))
+    up, *beyond = lax.optimization_barrier((up, *beyond))
+    queries = pl.pallas_call(
+        queries_kernel,
+        out_shape=shape((EXTENDED, inner), half),
+        in_specs=[anywhere] * 6 + [whole_spec()],
+        out_specs=whole_spec(),
+        scratch_shapes=[
+            pltpu.VMEM((model, inner), half),
+            pltpu.VMEM((EXTENDED, model + LANES), half),
+            pltpu.SemaphoreType.DMA((8,)),
+            pltpu.SemaphoreType.DMA((1,)),
+        ],
+        compiler_params=pltpu.CompilerParams(vmem_limit_bytes=VMEM_BYTES),
+        cost_estimate=pl.CostEstimate(flops=2 * EXTENDED * model * inner, bytes_accessed=8 * 2**20, transcendentals=0),
+        name="queries",
+    )(*beyond, whole, q_gains)
     kept, sent = pl.pallas_call(
         back_kernel,
         out_shape=(shape((count, width), half), shape((count, width), half)),
-        in_specs=[pl.BlockSpec(memory_space=pltpu.SMEM)] + [anywhere] * 5 + [whole_spec()] * 8,
+        in_specs=[pl.BlockSpec(memory_space=pltpu.SMEM)] + [anywhere] * 5 + [whole_spec()] * 6 + [anywhere, whole_spec()],
         out_specs=(whole_spec(), whole_spec()),
         scratch_shapes=[
             pltpu.VMEM((EXTENDED, inner + LANES), half),
             pltpu.VMEM((count, 3 * inner), half),
+            pltpu.VMEM((model, 3 * inner), half),
             pltpu.SemaphoreType.DMA((8,)),
+            pltpu.SemaphoreType.DMA((1,)),
         ],
         compiler_params=pltpu.CompilerParams(vmem_limit_bytes=VMEM_BYTES),
         name="back",

time: 199 us -> 174 us (0.87)
  starting transfers between devices: 61.8 us -> 47.3 us
  waiting for transfers between devices: 49.4 us -> 38.4 us
  Pallas kernels: 29.7 us -> 37.4 us
  local copies, waits for them, and re-layouts: 7.04 us -> 2.35 us
    ppermute x4, waiting for transfers between devices: 28.9 us -> 0.01 us  [the longest x2 0.01 us: spread_width(): right = lax.ppermute(first, 'width', steps('width', -1))]
    ppermute x6 -> x4, waiting for transfers between devices: 3.6 us -> 20 us  [gather_height(): shift = lambda x, by: lax.ppermute(x, 'height', steps('height', by, True))]
    pallas_call x0 -> x2, Pallas kernels: none -> 11.5 us  [the longest x1 8.06 us: on_device(): pl.pallas_call(queries_kernel, out_shape=shape((EXTENDED, inner), half),...]
    ppermute x6 -> x4, starting transfers between devices: 18 us -> 11.7 us  [gather_height(): shift = lambda x, by: lax.ppermute(x, 'height', steps('height', by, True))]
    ppermute x4 -> x3, waiting for transfers between devices: 0.01 us -> 4.78 us  [flip(): return lax.ppermute(x, 'height', [(i, i ^ bit) for i in range(count)])]
    slice x8 -> x4, local copies, waits for them, and re-layouts: 4.09 us -> 0.1 us  [the longest x2 0.06 us: joined_columns(): part[i * TILE:(i + 1) * TILE]]
    ppermute x2, waiting for transfers between devices: 5.37 us -> 1.65 us  [spread_height(): down = lax.ppermute(own, 'height', steps('height', -1))]
    ppermute x4, starting transfers between devices: 12.1 us -> 8.72 us  [the longest x2 6.13 us: spread_width(): left = lax.ppermute(last, 'width', steps('width', 1))]
  transfers between devices with their start and end apart: 20 -> 17, of which waited for: 11 -> 8; matrix products, arithmetic and copies ran while one was open for 7% -> 4% of each run, Pallas kernels for 5% -> 12%
where the time goes in v3:
time: 174 us; the launch traced here: 173 us
  starting transfers between devices  47.3 us (27%)
  waiting for transfers between devices  38.4 us (22%)
  blocking collectives  37.9 us (22%)
  Pallas kernels  37.4 us (21%)
  other arithmetic  4.36 us (3%)
  matrix products  3.74 us (2%)
  local copies, waits for them, and re-layouts  2.35 us (1%)
    all_gather x1, blocking collectives, on_device(): along_width = lax.all_gather(joined, 'width', axis=0, tiled=True)  37.9 us
    ppermute x4, waiting for transfers between devices, gather_height(): shift = lambda x, by: lax.ppermute(x, 'height', steps('height', by, True))  20 us
    pallas_call x1, Pallas kernels, on_device(): pl.pallas_call(front_kernel, out_shape=(shape((model, 4 * inner), half),...  17.3 us
    ppermute x4, starting transfers between devices, gather_height(): shift = lambda x, by: lax.ppermute(x, 'height', steps('height', by, True))  11.7 us
    ppermute x2, waiting for transfers between devices, on_device(): swap = lambda x: lax.ppermute(x, 'head', [(0, 1), (1, 0)])  10.9 us
    ppermute x2, starting transfers between devices, spread_height(): down = lax.ppermute(own, 'height', steps('height', -1))  8.94 us
    pallas_call x1, Pallas kernels, on_device(): pl.pallas_call(back_kernel, out_shape=(shape((count, width), half), shape...  8.63 us
    pallas_call x1, Pallas kernels, on_device(): pl.pallas_call(queries_kernel, out_shape=shape((EXTENDED, inner), half),...  8.06 us
  transfers between devices with their start and end apart: 17, of which 8 were waited for; matrix products, arithmetic and copies ran while one was open for 4% of the time, Pallas kernels for 12%

profile of v3, /device:TPU:6, one launch (start us, length us, event | category | flops | bytes accessed | tf_op | source)
XLA Modules:
  0.0 172.7 jit_solution(16831613940041660860)
XLA Ops:
  0.6 0.0 copy-start.10
  0.6 0.0 copy-start.11
  0.7 0.7 convert_element_type.35
  1.3 0.1 convert_element_type.36
  1.4 0.1 broadcast_in_dim.2
  1.5 1.2 pad_maximum_fusion.1.own
  2.8 0.0 copy-start
  2.8 1.9 %collective-permute-start = (bf16[288,1664]{1,0:T(8,128)(2,1)S(1)}, bf16[288,1664]{1,0:T(8,128)(2,1)S(1)}, u32[]{:S(2)}, u32[]{:S(2)}) collective-permute-start(bf16[288,1664]{1,0:T(8,128)(2,1)S(1)} %pad_maximum_fusion.1.own), channel_id=1, source_target_pairs={{0,32},{32,64},{64,96},{96,128},{128,160},{160,192},{192,224},{224... | collective-permute-start | bytes 2875400 | tf_op jit(solution)/shard_map/ppermute | solution.py:235
  4.7 4.5 %collective-permute-start.1 = (bf16[288,1664]{1,0:T(8,128)(2,1)S(1)}, bf16[288,1664]{1,0:T(8,128)(2,1)S(1)}, u32[]{:S(2)}, u32[]{:S(2)}) collective-permute-start(bf16[288,1664]{1,0:T(8,128)(2,1)S(1)} %pad_maximum_fusion.1.own), channel_id=1, source_target_pairs={{32,0},{64,32},{96,64},{128,96},{160,128},{192,160},{224,192},{256... | collective-permute-start | bytes 2875400 | tf_op jit(solution)/shard_map/ppermute | solution.py:236
  9.3 0.0 copy-done.10
  9.3 0.0 copy-done.11
  9.3 37.9 %all-gather = bf16[16,6,1536]{2,1,0:T(8,128)(2,1)S(1)} all-gather(bf16[1,6,1536]{2,1,0:T(8,128)(2,1)S(1)} %maximum_bitcast_fusion), channel_id=1, replica_groups=mesh['height'=16,'width'=16,'head'=2] {'width'}, dimensions={0}, use_global_device_ids=true | all-gather | bytes 313344 | tf_op jit(solution)/shard_map/all_gather | solution.py:311
  47.2 0.8 reshape.42
  48.0 0.0 collective-permute-done.up
  48.0 0.0 collective-permute-done.1.down
  48.0 0.0 copy-start.4
  48.0 2.4 %collective-permute-start.2 = (bf16[96,1536]{1,0:T(8,128)(2,1)}, bf16[96,1536]{1,0:T(8,128)(2,1)S(1)}, u32[]{:S(2)}, u32[]{:S(2)}) collective-permute-start(bf16[96,1536]{1,0:T(8,128)(2,1)} %reshape.42), channel_id=1, source_target_pairs={{0,64},{32,96},{64,0},{96,32},{128,192},{160,224},{192,128},{224,1... | collective-permute-start | bytes 884744 | tf_op jit(solution)/shard_map/ppermute | solution.py:252
  50.5 3.4 %columns.1 = (bf16[432,1664]{1,0:T(8,128)(2,1)}, bf16[432,1664]{1,0:T(8,128)(2,1)}) custom-call(bf16[288,1664]{1,0:T(8,128)(2,1)S(1)} %collective-permute-done.up, bf16[288,1664]{1,0:T(8,128)(2,1)S(1)} %pad_maximum_fusion.1.own, bf16[288,1664]{1,0:T(8,128)(2,1)S(1)} %collective-permute-done.1.down), custom_call_target="tpu_custom_call" | custom-call | tf_op jit(solution)/shard_map/columns/pallas_call | solution.py:286
  53.9 0.0 copy-done
  53.9 3.1 %collective-permute-done.2 = bf16[96,1536]{1,0:T(8,128)(2,1)S(1)} collective-permute-done((bf16[96,1536]{1,0:T(8,128)(2,1)}, bf16[96,1536]{1,0:T(8,128)(2,1)S(1)}, u32[]{:S(2)}, u32[]{:S(2)}) %collective-permute-start.2) | collective-permute-done | bytes 294944 | tf_op jit(solution)/shard_map/ppermute | solution.py:252
  57.0 0.0 copy-done.9
  57.1 0.0 copy-done.2
  57.1 0.0 copy-done.4
  57.1 1.9 %collective-permute-start.7 = (bf16[192,1536]{1,0:T(8,128)(2,1)S(1)}, bf16[192,1536]{1,0:T(8,128)(2,1)S(1)}, u32[]{:S(2)}, u32[]{:S(2)}) collective-permute-start(bf16[192,1536]{1,0:T(8,128)(2,1)S(1)} %pad_maximum_fusion.2), channel_id=1, source_target_pairs={{0,128},{32,160},{64,192},{96,224},{128,256},{160,288},{192,320},{... | collective-permute-start | bytes 1769480 | tf_op jit(solution)/shard_map/ppermute | solution.py:256
  59.0 3.9 %collective-permute-start.3 = (bf16[192,1536]{1,0:T(8,128)(2,1)S(1)}, bf16[192,1536]{1,0:T(8,128)(2,1)S(1)}, u32[]{:S(2)}, u32[]{:S(2)}) collective-permute-start(bf16[192,1536]{1,0:T(8,128)(2,1)S(1)} %pad_maximum_fusion.2), channel_id=1, source_target_pairs={{0,384},{32,416},{64,448},{96,480},{128,0},{160,32},{192,64},{224,... | collective-permute-start | bytes 1769480 | tf_op jit(solution)/shard_map/ppermute | solution.py:256
  62.9 1.6 collective-permute-start.5
  64.5 1.3 collective-permute-start.6
  65.8 6.2 %collective-permute-done.7 = bf16[192,1536]{1,0:T(8,128)(2,1)S(1)} collective-permute-done((bf16[192,1536]{1,0:T(8,128)(2,1)S(1)}, bf16[192,1536]{1,0:T(8,128)(2,1)S(1)}, u32[]{:S(2)}, u32[]{:S(2)}) %collective-permute-start.7) | collective-permute-done | bytes 589856 | tf_op jit(solution)/shard_map/ppermute | solution.py:256
  72.0 3.1 %collective-permute-start.8 = (bf16[96,1536]{1,0:T(8,128)(2,1)S(1)}, bf16[96,1536]{1,0:T(8,128)(2,1)S(1)}, u32[]{:S(2)}, u32[]{:S(2)}) collective-permute-start(bf16[96,1536]{1,0:T(8,128)(2,1)S(1)} %slice.33), channel_id=1, source_target_pairs={{0,128},{32,160},{64,192},{96,224},{128,256},{160,288},{192,320},{... | collective-permute-start | bytes 884744 | tf_op jit(solution)/shard_map/ppermute | solution.py:256
  75.2 0.0 collective-permute-done.3
  75.2 1.4 pad_maximum_fusion.rest_0_
  76.6 4.1 %collective-permute-done.8 = bf16[96,1536]{1,0:T(8,128)(2,1)S(1)} collective-permute-done((bf16[96,1536]{1,0:T(8,128)(2,1)S(1)}, bf16[96,1536]{1,0:T(8,128)(2,1)S(1)}, u32[]{:S(2)}, u32[]{:S(2)}) %collective-permute-start.8) | collective-permute-done | bytes 294944 | tf_op jit(solution)/shard_map/ppermute | solution.py:256
  80.7 1.9 %collective-permute-start.9 = (bf16[576,1536]{1,0:T(8,128)(2,1)}, bf16[576,1536]{1,0:T(8,128)(2,1)}, u32[]{:S(2)}, u32[]{:S(2)}) collective-permute-start(bf16[576,1536]{1,0:T(8,128)(2,1)} %pad_maximum_fusion.rest_0_), channel_id=1, source_target_pairs={{0,32},{32,0},{64,96},{96,64},{128,160},{160,128},{192,224},{224,1... | collective-permute-start | bytes 5308424 | tf_op jit(solution)/shard_map/ppermute | solution.py:252
  82.6 2.7 %collective-permute-start.4 = (bf16[96,1536]{1,0:T(8,128)(2,1)S(1)}, bf16[96,1536]{1,0:T(8,128)(2,1)S(1)}, u32[]{:S(2)}, u32[]{:S(2)}) collective-permute-start(bf16[96,1536]{1,0:T(8,128)(2,1)S(1)} %slice.32), channel_id=1, source_target_pairs={{0,384},{32,416},{64,448},{96,480},{128,0},{160,32},{192,64},{224,... | collective-permute-start | bytes 884744 | tf_op jit(solution)/shard_map/ppermute | solution.py:256
  85.4 9.7 %collective-permute-done.4 = bf16[96,1536]{1,0:T(8,128)(2,1)S(1)} collective-permute-done((bf16[96,1536]{1,0:T(8,128)(2,1)S(1)}, bf16[96,1536]{1,0:T(8,128)(2,1)S(1)}, u32[]{:S(2)}, u32[]{:S(2)}) %collective-permute-start.4) | collective-permute-done | bytes 294944 | tf_op jit(solution)/shard_map/ppermute | solution.py:256
  95.1 0.0 collective-permute-done.5.left
  95.1 0.0 collective-permute-done.6.right
  95.1 0.0 copy-start.8
  95.2 1.1 copy-done.7
  96.3 2.1 %collective-permute-start.10 = (bf16[192,1536]{1,0:T(8,128)(2,1)S(1)}, bf16[192,1536]{1,0:T(8,128)(2,1)S(1)}, u32[]{:S(2)}, u32[]{:S(2)}) collective-permute-start(bf16[192,1536]{1,0:T(8,128)(2,1)S(1)} %constant_dynamic-update-slice_fusion.rest_1_), channel_id=1, source_target_pairs={{0,32},{32,0},{64,96},{96,64},{128,160},{160,128},{192,224},{224,1... | collective-permute-start | bytes 1769480 | tf_op jit(solution)/shard_map/ppermute | solution.py:252
  98.4 0.0 copy-done.8
  98.4 0.0 copy-done.12
  98.5 0.1 pad_add_fusion.place
  98.5 1.6 collective-permute-done.10.rest_3_
  100.2 0.0 collective-permute-done.9.rest_2_
  100.2 0.0 copy-done.6
  100.2 17.3 %front.1 = (bf16[1536,1536]{1,0:T(8,128)(2,1)}, bf16[288,384]{1,0:T(8,128)(2,1)S(1)}, bf16[288,384]{1,0:T(8,128)(2,1)S(1)}, bf16[288,128]{1,0:T(8,128)(2,1)S(1)}...) custom-call(s32[2]{0:T(128)S(1)} %pad_add_fusion.place, ...), custom_call_target="tpu_custom_call" | custom-call | tf_op jit(solution)/shard_map/front/pallas_call | solution.py:318
  117.5 2.1 %collective-permute-start.11 = (bf16[288,512]{1,0:T(8,128)(2,1)S(1)}, bf16[288,512]{1,0:T(8,128)(2,1)S(1)}, u32[]{:S(2)}, u32[]{:S(2)}) collective-permute-start(bf16[288,512]{1,0:T(8,128)(2,1)S(1)} %get-tuple-element.49.own), channel_id=1, source_target_pairs={{0,32},{32,64},{64,96},{96,128},{128,160},{160,192},{192,224},{224... | collective-permute-start | bytes 884744 | tf_op jit(solution)/shard_map/ppermute | solution.py:235
  119.6 4.4 %collective-permute-start.12 = (bf16[288,512]{1,0:T(8,128)(2,1)S(1)}, bf16[288,512]{1,0:T(8,128)(2,1)S(1)}, u32[]{:S(2)}, u32[]{:S(2)}) collective-permute-start(bf16[288,512]{1,0:T(8,128)(2,1)S(1)} %get-tuple-element.49.own), channel_id=1, source_target_pairs={{32,0},{64,32},{96,64},{128,96},{160,128},{192,160},{224,192},{256... | collective-permute-start | bytes 884744 | tf_op jit(solution)/shard_map/ppermute | solution.py:236
  124.0 1.5 convolution_convert_fusion
  125.6 1.0 collective-permute-done.11.up
  126.6 1.7 collective-permute-done.12.down
  128.3 1.3 collective-permute-start.15
  129.7 4.6 %collective-permute-start.14 = (bf16[432,512]{1,0:T(8,128)(2,1)S(1)}, bf16[432,512]{1,0:T(8,128)(2,1)S(1)}, u32[]{:S(2)}, u32[]{:S(2)}) collective-permute-start(bf16[432,512]{1,0:T(8,128)(2,1)S(1)} %pad_maximum_fusion.3), channel_id=1, source_target_pairs={{0,2},{2,4},{4,6},{6,8},{8,10},{10,12},{12,14},{14,16},{16,18},{18... | collective-permute-start | bytes 1327112 | tf_op jit(solution)/shard_map/ppermute | solution.py:241
  134.2 4.9 %collective-permute-start.13 = (bf16[288,768]{1,0:T(8,128)(2,1)S(1)}, bf16[288,768]{1,0:T(8,128)(2,1)S(1)}, u32[]{:S(2)}, u32[]{:S(2)}) collective-permute-start(bf16[288,768]{1,0:T(8,128)(2,1)S(1)} %convolution_convert_fusion), channel_id=1, source_target_pairs={{0,1},{1,0},{2,3},{3,2},{4,5},{5,4},{6,7},{7,6},{8,9},{9,8},{10,11... | collective-permute-start | bytes 1327112 | tf_op jit(solution)/shard_map/ppermute | solution.py:352
  139.2 8.1 %queries.1 = bf16[1728,384]{1,0:T(8,128)(2,1)} custom-call(bf16[288,1664]{1,0:T(8,128)(2,1)S(1)} %copy-done.1, bf16[288,1664]{1,0:T(8,128)(2,1)S(1)} %copy-done.3, bf16[288,1664]{1,0:T(8,128)(2,1)S(1)} %copy-done.5, bf16[432,1664]{1,0:T(8,128)(2,1)} %copy-done.7, bf16[432,1664]{1,0:T(8,128)(2,1)} %copy-done.8, bf16[1536,1536]{1,0:T(8,128)(2,1)} %get-tuple-element.48.whole, ...), custom_call_target="tpu_custom_call" | custom-call | flops 2038431744 | bytes 8388608 | tf_op jit(solution)/shard_map/queries/pallas_call | solution.py:362
  147.3 0.0 collective-permute-done.15.right
  147.3 0.0 collective-permute-done.14.left
  147.3 8.6 %back.1 = (bf16[288,768]{1,0:T(8,128)(2,1)S(1)}, bf16[288,768]{1,0:T(8,128)(2,1)S(1)}) custom-call(s32[2]{0:T(128)S(1)} %pad_add_fusion.place, bf16[288,512]{1,0:T(8,128)(2,1)S(1)} %get-tuple-element.49.own, bf16[288,512]{1,0:T(8,128)(2,1)S(1)} %collective-permute-done.11.up, bf16[288,512]{1,0:T(8,128)(2,1)S(1)} %collective-permute-done.12.down, ...), custom_call_target="tpu_custom_call" | custom-call | tf_op jit(solution)/shard_map/back/pallas_call | solution.py:377
  155.9 2.6 %collective-permute-start.16 = (bf16[288,768]{1,0:T(8,128)(2,1)S(1)}, bf16[288,768]{1,0:T(8,128)(2,1)S(1)}, u32[]{:S(2)}, u32[]{:S(2)}) collective-permute-start(bf16[288,768]{1,0:T(8,128)(2,1)S(1)} %get-tuple-element.65), channel_id=1, source_target_pairs={{0,1},{1,0},{2,3},{3,2},{4,5},{5,4},{6,7},{7,6},{8,9},{9,8},{10,11... | collective-permute-start | bytes 1327112 | tf_op jit(solution)/shard_map/ppermute | solution.py:352
  158.6 0.0 collective-permute-done.13
  158.6 2.3 %fusion.2 = bf16[288,768]{1,0:T(8,128)(2,1)} fusion(bf16[288,384]{1,0:T(8,128)(2,1)S(1)} %get-tuple-element.47, bf16[288,768]{1,0:T(8,128)(2,1)S(1)} %collective-permute-done.13, bf16[1536,1536]{1,0:T(8,128)(2,1)} %get-tuple-element.48.whole, s32[]{:T(128)S(6)} %select_n.6), kind=kOutput, calls=%fused_computation.5 | convolution fusion | flops 170975232 | bytes 1695748 | tf_op jit(solution)/shard_map/dot_general | solution.py:25
  160.9 10.9 %collective-permute-done.16 = bf16[288,768]{1,0:T(8,128)(2,1)S(1)} collective-permute-done((bf16[288,768]{1,0:T(8,128)(2,1)S(1)}, bf16[288,768]{1,0:T(8,128)(2,1)S(1)}, u32[]{:S(2)}, u32[]{:S(2)}) %collective-permute-start.16) | collective-permute-done | bytes 442400 | tf_op jit(solution)/shard_map/ppermute | solution.py:352
  171.8 0.9 add_convert_fusion
  (26 shorter events, 0.3 us)
Async XLA Ops:
  0.6 8.7 %copy-start.10 = (bf16[6,3,384]{2,1,0:T(4,128)(2,1)S(1)}, bf16[6,3,384]{2,1,0:T(4,128)(2,1)}, u32[]{:S(2)}) copy-start(bf16[6,3,384]{2,1,0:T(4,128)(2,1)} %param.9) | copy-start | bytes 41476
  0.6 8.7 %copy-start.11 = (bf16[6,384]{1,0:T(8,128)(2,1)S(1)}, bf16[6,384]{1,0:T(8,128)(2,1)}, u32[]{:S(2)}) copy-start(bf16[6,384]{1,0:T(8,128)(2,1)} %param.10) | copy-start | bytes 13828
  2.8 51.1 %copy-start = (bf16[288,1664]{1,0:T(8,128)(2,1)}, bf16[288,1664]{1,0:T(8,128)(2,1)S(1)}, u32[]{:S(2)}) copy-start(bf16[288,1664]{1,0:T(8,128)(2,1)S(1)} %pad_maximum_fusion.1.own) | copy-start | bytes 2875396
  2.8 45.2 %collective-permute-start = (bf16[288,1664]{1,0:T(8,128)(2,1)S(1)}, bf16[288,1664]{1,0:T(8,128)(2,1)S(1)}, u32[]{:S(2)}, u32[]{:S(2)}) collective-permute-start(bf16[288,1664]{1,0:T(8,128)(2,1)S(1)} %pad_maximum_fusion.1.own), channel_id=1, source_target_pairs={{0,32},{32,64},{64,96},{96,128},{128,160},{160,192},{192,224},{224... | collective-permute-start | bytes 2875400 | tf_op jit(solution)/shard_map/ppermute | solution.py:235
  4.7 43.3 %collective-permute-start.1 = (bf16[288,1664]{1,0:T(8,128)(2,1)S(1)}, bf16[288,1664]{1,0:T(8,128)(2,1)S(1)}, u32[]{:S(2)}, u32[]{:S(2)}) collective-permute-start(bf16[288,1664]{1,0:T(8,128)(2,1)S(1)} %pad_maximum_fusion.1.own), channel_id=1, source_target_pairs={{32,0},{64,32},{96,64},{128,96},{160,128},{192,160},{224,192},{256... | collective-permute-start | bytes 2875400 | tf_op jit(solution)/shard_map/ppermute | solution.py:236
  48.0 9.0 %copy-start.9 = (bf16[96,1536]{1,0:T(8,128)(2,1)S(1)}, bf16[96,1536]{1,0:T(8,128)(2,1)}, u32[]{:S(2)}) copy-start(bf16[96,1536]{1,0:T(8,128)(2,1)} %reshape.42) | copy-start | bytes 884740
  48.0 9.0 %copy-start.2 = (bf16[288,1664]{1,0:T(8,128)(2,1)}, bf16[288,1664]{1,0:T(8,128)(2,1)S(1)}, u32[]{:S(2)}) copy-start(bf16[288,1664]{1,0:T(8,128)(2,1)S(1)} %collective-permute-done.up) | copy-start | bytes 2875396
  48.0 9.0 %copy-start.4 = (bf16[288,1664]{1,0:T(8,128)(2,1)}, bf16[288,1664]{1,0:T(8,128)(2,1)S(1)}, u32[]{:S(2)}) copy-start(bf16[288,1664]{1,0:T(8,128)(2,1)S(1)} %collective-permute-done.1.down) | copy-start | bytes 2875396
  48.0 9.0 %collective-permute-start.2 = (bf16[96,1536]{1,0:T(8,128)(2,1)}, bf16[96,1536]{1,0:T(8,128)(2,1)S(1)}, u32[]{:S(2)}, u32[]{:S(2)}) collective-permute-start(bf16[96,1536]{1,0:T(8,128)(2,1)} %reshape.42), channel_id=1, source_target_pairs={{0,64},{32,96},{64,0},{96,32},{128,192},{160,224},{192,128},{224,1... | collective-permute-start | bytes 884744 | tf_op jit(solution)/shard_map/ppermute | solution.py:252
  57.1 14.9 %collective-permute-start.7 = (bf16[192,1536]{1,0:T(8,128)(2,1)S(1)}, bf16[192,1536]{1,0:T(8,128)(2,1)S(1)}, u32[]{:S(2)}, u32[]{:S(2)}) collective-permute-start(bf16[192,1536]{1,0:T(8,128)(2,1)S(1)} %pad_maximum_fusion.2), channel_id=1, source_target_pairs={{0,128},{32,160},{64,192},{96,224},{128,256},{160,288},{192,320},{... | collective-permute-start | bytes 1769480 | tf_op jit(solution)/shard_map/ppermute | solution.py:256
  59.0 16.2 %collective-permute-start.3 = (bf16[192,1536]{1,0:T(8,128)(2,1)S(1)}, bf16[192,1536]{1,0:T(8,128)(2,1)S(1)}, u32[]{:S(2)}, u32[]{:S(2)}) collective-permute-start(bf16[192,1536]{1,0:T(8,128)(2,1)S(1)} %pad_maximum_fusion.2), channel_id=1, source_target_pairs={{0,384},{32,416},{64,448},{96,480},{128,0},{160,32},{192,64},{224,... | collective-permute-start | bytes 1769480 | tf_op jit(solution)/shard_map/ppermute | solution.py:256
  62.9 32.2 %collective-permute-start.5 = (bf16[432,1664]{1,0:T(8,128)(2,1)}, bf16[432,1664]{1,0:T(8,128)(2,1)S(1)}, u32[]{:S(2)}, u32[]{:S(2)}) collective-permute-start(bf16[432,1664]{1,0:T(8,128)(2,1)} %get-tuple-element.40), channel_id=1, source_target_pairs={{0,2},{2,4},{4,6},{6,8},{8,10},{10,12},{12,14},{14,16},{16,18},{18... | collective-permute-start | bytes 4313096 | tf_op jit(solution)/shard_map/ppermute | solution.py:241
  64.5 30.6 %collective-permute-start.6 = (bf16[432,1664]{1,0:T(8,128)(2,1)}, bf16[432,1664]{1,0:T(8,128)(2,1)S(1)}, u32[]{:S(2)}, u32[]{:S(2)}) collective-permute-start(bf16[432,1664]{1,0:T(8,128)(2,1)} %get-tuple-element.41), channel_id=1, source_target_pairs={{2,0},{4,2},{6,4},{8,6},{10,8},{12,10},{14,12},{16,14},{18,16},{20... | collective-permute-start | bytes 4313096 | tf_op jit(solution)/shard_map/ppermute | solution.py:242
  72.0 8.6 %collective-permute-start.8 = (bf16[96,1536]{1,0:T(8,128)(2,1)S(1)}, bf16[96,1536]{1,0:T(8,128)(2,1)S(1)}, u32[]{:S(2)}, u32[]{:S(2)}) collective-permute-start(bf16[96,1536]{1,0:T(8,128)(2,1)S(1)} %slice.33), channel_id=1, source_target_pairs={{0,128},{32,160},{64,192},{96,224},{128,256},{160,288},{192,320},{... | collective-permute-start | bytes 884744 | tf_op jit(solution)/shard_map/ppermute | solution.py:256
  76.6 21.9 %copy-start.12 = (f32[384]{0:T(512)S(1)}, f32[384]{0:T(512)}, u32[]{:S(2)}) copy-start(f32[384]{0:T(512)} %param.11) | copy-start | bytes 4612
  76.6 21.9 %copy-start.13 = (f32[384]{0:T(512)S(1)}, f32[384]{0:T(512)}, u32[]{:S(2)}) copy-start(f32[384]{0:T(512)} %param.12) | copy-start | bytes 4612
  76.6 23.6 %copy-start.6 = (bf16[1,2,144,1536]{3,2,1,0:T(8,128)(2,1)S(1)}, bf16[1,2,144,1536]{3,2,1,0:T(8,128)(2,1)}, u32[]{:S(2)}) copy-start(bf16[1,2,144,1536]{3,2,1,0:T(8,128)(2,1)} %param.8) | copy-start | bytes 2654212
  80.7 19.5 %collective-permute-start.9 = (bf16[576,1536]{1,0:T(8,128)(2,1)}, bf16[576,1536]{1,0:T(8,128)(2,1)}, u32[]{:S(2)}, u32[]{:S(2)}) collective-permute-start(bf16[576,1536]{1,0:T(8,128)(2,1)} %pad_maximum_fusion.rest_0_), channel_id=1, source_target_pairs={{0,32},{32,0},{64,96},{96,64},{128,160},{160,128},{192,224},{224,1... | collective-permute-start | bytes 5308424 | tf_op jit(solution)/shard_map/ppermute | solution.py:252
  82.6 12.5 %collective-permute-start.4 = (bf16[96,1536]{1,0:T(8,128)(2,1)S(1)}, bf16[96,1536]{1,0:T(8,128)(2,1)S(1)}, u32[]{:S(2)}, u32[]{:S(2)}) collective-permute-start(bf16[96,1536]{1,0:T(8,128)(2,1)S(1)} %slice.32), channel_id=1, source_target_pairs={{0,384},{32,416},{64,448},{96,480},{128,0},{160,32},{192,64},{224,... | collective-permute-start | bytes 884744 | tf_op jit(solution)/shard_map/ppermute | solution.py:256
  95.1 1.2 copy-start.7
  95.1 3.3 %copy-start.8 = (bf16[432,1664]{1,0:T(8,128)(2,1)}, bf16[432,1664]{1,0:T(8,128)(2,1)S(1)}, u32[]{:S(2)}) copy-start(bf16[432,1664]{1,0:T(8,128)(2,1)S(1)} %collective-permute-done.6.right) | copy-start | bytes 4313092
  96.3 3.9 %collective-permute-start.10 = (bf16[192,1536]{1,0:T(8,128)(2,1)S(1)}, bf16[192,1536]{1,0:T(8,128)(2,1)S(1)}, u32[]{:S(2)}, u32[]{:S(2)}) collective-permute-start(bf16[192,1536]{1,0:T(8,128)(2,1)S(1)} %constant_dynamic-update-slice_fusion.rest_1_), channel_id=1, source_target_pairs={{0,32},{32,0},{64,96},{96,64},{128,160},{160,128},{192,224},{224,1... | collective-permute-start | bytes 1769480 | tf_op jit(solution)/shard_map/ppermute | solution.py:252
  117.5 9.0 %collective-permute-start.11 = (bf16[288,512]{1,0:T(8,128)(2,1)S(1)}, bf16[288,512]{1,0:T(8,128)(2,1)S(1)}, u32[]{:S(2)}, u32[]{:S(2)}) collective-permute-start(bf16[288,512]{1,0:T(8,128)(2,1)S(1)} %get-tuple-element.49.own), channel_id=1, source_target_pairs={{0,32},{32,64},{64,96},{96,128},{128,160},{160,192},{192,224},{224... | collective-permute-start | bytes 884744 | tf_op jit(solution)/shard_map/ppermute | solution.py:235
  119.6 8.6 %collective-permute-start.12 = (bf16[288,512]{1,0:T(8,128)(2,1)S(1)}, bf16[288,512]{1,0:T(8,128)(2,1)S(1)}, u32[]{:S(2)}, u32[]{:S(2)}) collective-permute-start(bf16[288,512]{1,0:T(8,128)(2,1)S(1)} %get-tuple-element.49.own), channel_id=1, source_target_pairs={{32,0},{64,32},{96,64},{128,96},{160,128},{192,160},{224,192},{256... | collective-permute-start | bytes 884744 | tf_op jit(solution)/shard_map/ppermute | solution.py:236
  125.5 13.7 %copy-start.1 = (bf16[288,1664]{1,0:T(8,128)(2,1)S(1)}, bf16[288,1664]{1,0:T(8,128)(2,1)}, u32[]{:S(2)}) copy-start(bf16[288,1664]{1,0:T(8,128)(2,1)} %copy-done) | copy-start | bytes 2875396
  125.5 13.7 %copy-start.3 = (bf16[288,1664]{1,0:T(8,128)(2,1)S(1)}, bf16[288,1664]{1,0:T(8,128)(2,1)}, u32[]{:S(2)}) copy-start(bf16[288,1664]{1,0:T(8,128)(2,1)} %copy-done.2) | copy-start | bytes 2875396
  125.6 13.7 %copy-start.5 = (bf16[288,1664]{1,0:T(8,128)(2,1)S(1)}, bf16[288,1664]{1,0:T(8,128)(2,1)}, u32[]{:S(2)}) copy-start(bf16[288,1664]{1,0:T(8,128)(2,1)} %copy-done.4) | copy-start | bytes 2875396
  128.3 19.0 %collective-permute-start.15 = (bf16[432,512]{1,0:T(8,128)(2,1)S(1)}, bf16[432,512]{1,0:T(8,128)(2,1)S(1)}, u32[]{:S(2)}, u32[]{:S(2)}) collective-permute-start(bf16[432,512]{1,0:T(8,128)(2,1)S(1)} %pad_maximum_fusion.4), channel_id=1, source_target_pairs={{2,0},{4,2},{6,4},{8,6},{10,8},{12,10},{14,12},{16,14},{18,16},{20... | collective-permute-start | bytes 1327112 | tf_op jit(solution)/shard_map/ppermute | solution.py:242
  129.7 17.7 %collective-permute-start.14 = (bf16[432,512]{1,0:T(8,128)(2,1)S(1)}, bf16[432,512]{1,0:T(8,128)(2,1)S(1)}, u32[]{:S(2)}, u32[]{:S(2)}) collective-permute-start(bf16[432,512]{1,0:T(8,128)(2,1)S(1)} %pad_maximum_fusion.3), channel_id=1, source_target_pairs={{0,2},{2,4},{4,6},{6,8},{8,10},{10,12},{12,14},{14,16},{16,18},{18... | collective-permute-start | bytes 1327112 | tf_op jit(solution)/shard_map/ppermute | solution.py:241
  134.2 24.4 %collective-permute-start.13 = (bf16[288,768]{1,0:T(8,128)(2,1)S(1)}, bf16[288,768]{1,0:T(8,128)(2,1)S(1)}, u32[]{:S(2)}, u32[]{:S(2)}) collective-permute-start(bf16[288,768]{1,0:T(8,128)(2,1)S(1)} %convolution_convert_fusion), channel_id=1, source_target_pairs={{0,1},{1,0},{2,3},{3,2},{4,5},{5,4},{6,7},{7,6},{8,9},{9,8},{10,11... | collective-permute-start | bytes 1327112 | tf_op jit(solution)/shard_map/ppermute | solution.py:352
  155.9 15.9 %collective-permute-start.16 = (bf16[288,768]{1,0:T(8,128)(2,1)S(1)}, bf16[288,768]{1,0:T(8,128)(2,1)S(1)}, u32[]{:S(2)}, u32[]{:S(2)}) collective-permute-start(bf16[288,768]{1,0:T(8,128)(2,1)S(1)} %get-tuple-element.65), channel_id=1, source_target_pairs={{0,1},{1,0},{2,3},{3,2},{4,5},{5,4},{6,7},{7,6},{8,9},{9,8},{10,11... | collective-permute-start | bytes 1327112 | tf_op jit(solution)/shard_map/ppermute | solution.py:352

commit v4 on v3

--- a/solution.py
+++ b/solution.py
@@ -70,7 +70,30 @@
     ]
 
 
-def front_kernel(place, own, up, down, left, right, upstream, *rest):
+def token_copies_of(core, own, up, down, left, right, shared, target, sems):
+    pairs = [
+        (left, 0, 2, core),
+        (shared, 0, 1, 2 - 2 * core),
+        (up, 0, 1, 3),
+        (own, 0, 1, 4),
+        (down, 0, 1, 5),
+        (up, 1, 1, 6),
+        (own, 1, 1, 7),
+        (down, 1, 1, 8),
+        (right, 0, 2, 9 + core),
+        (shared, 1, 1, 11 - 2 * core),
+    ]
+    return [
+        pltpu.make_async_copy(
+            src.at[pl.ds(first * TILE, count * TILE)],
+            target.at[pl.ds(pl.multiple_of(at * TILE, TILE), count * TILE)],
+            sems.at[n],
+        )
+        for n, (src, first, count, at) in enumerate(pairs)
+    ]
+
+
+def front_kernel(place, own, up, down, left, right, shared, upstream, *rest):
     pieces, rest = rest[:4], rest[4:]
     (q_gain, k_gain, whole_out, own_keys, own_values, own_marks, own_k_raw, grad_q, attended, message,
      whole, tok, grad, keys, values, marks, own_raw, own_queries, token_sems, block_sems, grad_sem, whole_sem) = rest
@@ -87,7 +110,7 @@
         for i, (piece, n, spot) in enumerate(parts)
     ]
     grad_copy = pltpu.make_async_copy(upstream, grad, grad_sem.at[0])
-    token_copies = extended_copies(own, up, down, left, right, tok, token_sems)
+    token_copies = token_copies_of(lax.rem(here, 2), own, up, down, left, right, shared, tok, token_sems)
     whole_copy = pltpu.make_async_copy(whole, whole_out, whole_sem.at[0])
     for copy in block_copies + [grad_copy] + token_copies:
         copy.start()
@@ -165,11 +188,11 @@
     whole_copy.wait()
 
 
-def queries_kernel(own, up, down, left, right, whole, q_gain, queries, weight, tok, sems, weight_sem):
+def queries_kernel(place, own, up, down, left, right, shared, whole, q_gain, queries, weight, tok, sems, weight_sem):
     inner = weight.shape[1]
     model = weight.shape[0]
     weight_copy = pltpu.make_async_copy(whole.at[:, pl.ds(0, inner)], weight, weight_sem.at[0])
-    copies = extended_copies(own, up, down, left, right, tok, sems)
+    copies = token_copies_of(lax.rem(place[0], 2), own, up, down, left, right, shared, tok, sems)
     for copy in [weight_copy] + copies:
         copy.start()
     for copy in [weight_copy] + copies:
@@ -185,19 +208,29 @@
             queries[rows, lanes] = (q_raw * norm_inverse(q_raw) * q_gain[:, lanes]).astype(jnp.bfloat16)
         return carry
 
-    lax.fori_loop(0, EXTENDED // chunk, project, 0)
-
-
-def back_kernel(place, own, up, down, left, right, queries, keys, values, marks, k_raw, grad_q, whole, k_gain,
-                kept, sent, ext, grad_qkv, weight, sems, weight_sem):
+    lax.fori_loop(0, EXTENDED // chunk, project, 0, unroll=True)
+
+
+def back_kernel(place, own, up, down, left, right, queries_in, keys_in, values_in, marks_in, k_raw_in, grad_q_in, whole,
+                k_gain, kept, sent, ext, grad_qkv, weight, queries, keys, values, marks, k_raw, sems, load_sems, weight_sem):
     inner = queries.shape[1]
+    loads = [
+        pltpu.make_async_copy(src, dst, load_sems.at[n])
+        for n, (src, dst) in enumerate((
+            (queries_in, queries),
+            (keys_in, keys),
+            (values_in, values),
+            (marks_in, marks),
+            (k_raw_in, k_raw),
+            (grad_q_in, grad_qkv.at[:, pl.ds(0, inner)]),
+        ))
+    ]
     copies = extended_copies(own, up, down, left, right, ext, sems)
     weight_copy = pltpu.make_async_copy(whole.at[:, pl.ds(0, 3 * inner)], weight, weight_sem.at[0])
-    for copy in copies + [weight_copy]:
+    for copy in copies + loads + [weight_copy]:
         copy.start()
-    for copy in copies:
+    for copy in copies + loads:
         copy.wait()
-    grad_qkv[:, :inner] = grad_q[...]
     lane = lane_index(TILE)
     for tile in range(2):
         mine = slice(tile * TILE, (tile + 1) * TILE)
@@ -252,46 +285,56 @@
     return lax.ppermute(x, "height", [(i, i ^ bit) for i in range(count)])
 
 
-def gather_height(block, up, own, down):
+def gather_height(block, place, up, own, down):
     shift = lambda x, by: lax.ppermute(x, "height", steps("height", by, True))
     rows = block.shape[0]
     pair = jnp.concatenate([block, flip(block, 2)], axis=0)
-    pair, first, last = lax.optimization_barrier((pair, *columns(up, own, down)))
+    pair, first, last = lax.optimization_barrier((pair, *columns(place, up, own, down)))
     left, right = spread_width(first, last)
+    core = place[0] & 1
+    give = lambda part: lax.dynamic_slice(part, ((1 - core) * TILE, 0), (TILE, part.shape[1]))
+    shared = flip(jnp.concatenate([give(left), give(right)], axis=0), 1)
     north, south = shift(pair, 4), shift(pair, -4)
     far, far_beside = shift(north[:rows], 4), shift(south[rows:], -4)
     near = jnp.concatenate([pair, north, south], axis=0)
     near, far = lax.optimization_barrier((near, far))
-    near_swapped = flip(near, 1)
-    far_beside, left, right = lax.optimization_barrier((far_beside, left, right))
     far = jnp.concatenate([far, far_beside], axis=0)
-    return [near, far, near_swapped, flip(far, 1)], left, right
-
-
-def columns_kernel(up, own, down, first, last, sems):
-    copies = [
-        pltpu.make_async_copy(part.at[pl.ds(side * TILE, TILE)], target.at[pl.ds(n * TILE, TILE)], sems.at[3 * side + n])
-        for side, target in enumerate((first, last))
-        for n, part in enumerate((up, own, down))
-    ]
-    for copy in copies:
-        copy.start()
-    for copy in copies:
-        copy.wait()
-
-
-def columns(up, own, down):
+    return [near, far, flip(near, 1), flip(far, 1)], left, right, shared
+
+
+def columns_kernel(place, up, own, down, first, last, sems):
+    def copy_all(upper, lower):
+        copies = [
+            pltpu.make_async_copy(part.at[pl.ds(side * TILE, TILE)], target.at[pl.ds(n * TILE, TILE)], sems.at[2 * side + n])
+            for side, target in enumerate((first, last))
+            for n, part in enumerate((upper, lower))
+        ]
+        for copy in copies:
+            copy.start()
+        for copy in copies:
+            copy.wait()
+
+    @pl.when(place[0] % 2 == 0)
+    def even():
+        copy_all(up, own)
+
+    @pl.when(place[0] % 2 == 1)
+    def odd():
+        copy_all(own, down)
+
+
+def columns(place, up, own, down):
     anywhere = pl.BlockSpec(memory_space=pl.ANY)
-    out = jax.ShapeDtypeStruct((COLUMN, own.shape[1]), own.dtype)
+    out = jax.ShapeDtypeStruct((2 * TILE, own.shape[1]), own.dtype)
     return pl.pallas_call(
         columns_kernel,
         out_shape=(out, out),
-        in_specs=[anywhere] * 3,
+        in_specs=[pl.BlockSpec(memory_space=pltpu.SMEM)] + [anywhere] * 3,
         out_specs=(whole_spec(), whole_spec()),
-        scratch_shapes=[pltpu.SemaphoreType.DMA((6,))],
+        scratch_shapes=[pltpu.SemaphoreType.DMA((4,))],
         compiler_params=pltpu.CompilerParams(vmem_limit_bytes=VMEM_BYTES),
         name="columns",
-    )(up, own, down)
+    )(place, up, own, down)
 
 
 def whole_spec():
@@ -310,7 +353,7 @@
     joined = jnp.concatenate([qkv_weight.reshape(shard_rows, 3 * inner), out_weight], axis=1)
     along_width = lax.all_gather(joined, "width", axis=0, tiled=True)
     along_width, up, down = lax.optimization_barrier((along_width, up, down))
-    blocks, left, right = gather_height(along_width, up, marked, down)
+    blocks, left, right, shared = gather_height(along_width, place, up, marked, down)
     q_gains, k_gains = q_gain.reshape(1, inner), k_gain.reshape(1, inner)
     anywhere = pl.BlockSpec(memory_space=pl.ANY)
     shape = jax.ShapeDtypeStruct
@@ -327,7 +370,7 @@
             shape((count, inner), half),
             shape((count, inner + LANES), half),
         ),
-        in_specs=[pl.BlockSpec(memory_space=pltpu.SMEM)] + [anywhere] * 10 + [whole_spec()] * 2,
+        in_specs=[pl.BlockSpec(memory_space=pltpu.SMEM)] + [anywhere] * 11 + [whole_spec()] * 2,
         out_specs=(anywhere,) + tuple(whole_spec() for _ in range(7)),
         scratch_shapes=[
             pltpu.VMEM((model, 4 * inner), half),
@@ -338,20 +381,20 @@
             pltpu.VMEM((EXTENDED, LANES), half),
             pltpu.VMEM((count, inner), jnp.float32),
             pltpu.VMEM((count, model), half),
-            pltpu.SemaphoreType.DMA((8,)),
+            pltpu.SemaphoreType.DMA((10,)),
             pltpu.SemaphoreType.DMA((16,)),
             pltpu.SemaphoreType.DMA((1,)),
             pltpu.SemaphoreType.DMA((1,)),
         ],
         compiler_params=pltpu.CompilerParams(vmem_limit_bytes=VMEM_BYTES),
         name="front",
-    )(place, marked, up, down, left, right, grad_out.reshape(count, model), *blocks, q_gains, k_gains)
+    )(place, marked, up, down, left, right, shared, grad_out.reshape(count, model), *blocks, q_gains, k_gains)
 
     group = lax.axis_index("head")
     width = model // 2
     swap = lambda x: lax.ppermute(x, "head", [(0, 1), (1, 0)])
     part = lambda which: lax.dynamic_slice(whole, (which * width, 3 * inner), (width, inner))
-    beyond = (marked, up, down, left, right)
+    beyond = (marked, up, down, left, right, shared)
     up, down = spread_height(message)
     mixed_sent = dot_rows(attended, part(1 - group)).astype(half)
     up, down, mixed_sent = lax.optimization_barrier((up, down, mixed_sent))
@@ -362,28 +405,34 @@
     queries = pl.pallas_call(
         queries_kernel,
         out_shape=shape((EXTENDED, inner), half),
-        in_specs=[anywhere] * 6 + [whole_spec()],
+        in_specs=[pl.BlockSpec(memory_space=pltpu.SMEM)] + [anywhere] * 7 + [whole_spec()],
         out_specs=whole_spec(),
         scratch_shapes=[
             pltpu.VMEM((model, inner), half),
             pltpu.VMEM((EXTENDED, model + LANES), half),
-            pltpu.SemaphoreType.DMA((8,)),
+            pltpu.SemaphoreType.DMA((10,)),
             pltpu.SemaphoreType.DMA((1,)),
         ],
         compiler_params=pltpu.CompilerParams(vmem_limit_bytes=VMEM_BYTES),
         cost_estimate=pl.CostEstimate(flops=2 * EXTENDED * model * inner, bytes_accessed=8 * 2**20, transcendentals=0),
         name="queries",
-    )(*beyond, whole, q_gains)
+    )(place, *beyond, whole, q_gains)
     kept, sent = pl.pallas_call(
         back_kernel,
         out_shape=(shape((count, width), half), shape((count, width), half)),
-        in_specs=[pl.BlockSpec(memory_space=pltpu.SMEM)] + [anywhere] * 5 + [whole_spec()] * 6 + [anywhere, whole_spec()],
+        in_specs=[pl.BlockSpec(memory_space=pltpu.SMEM)] + [anywhere] * 12 + [whole_spec()],
         out_specs=(whole_spec(), whole_spec()),
         scratch_shapes=[
             pltpu.VMEM((EXTENDED, inner + LANES), half),
             pltpu.VMEM((count, 3 * inner), half),
             pltpu.VMEM((model, 3 * inner), half),
+            pltpu.VMEM((EXTENDED, inner), half),
+            pltpu.VMEM((count, inner), half),
+            pltpu.VMEM((count, inner), half),
+            pltpu.VMEM((count, LANES), half),
+            pltpu.VMEM((count, inner), jnp.float32),
             pltpu.SemaphoreType.DMA((8,)),
+            pltpu.SemaphoreType.DMA((6,)),
             pltpu.SemaphoreType.DMA((1,)),
         ],
         compiler_params=pltpu.CompilerParams(vmem_limit_bytes=VMEM_BYTES),

time: 174 us -> 169 us (0.971)
  waiting for transfers between devices: 38.4 us -> 23.4 us
  starting transfers between devices: 47.3 us -> 53.4 us
  other arithmetic: 4.36 us -> 6.44 us
    ppermute x4, waiting for transfers between devices: 20 us -> 4.47 us  [gather_height(): shift = lambda x, by: lax.ppermute(x, 'height', steps('height', by, True))]
    ppermute x2, starting transfers between devices: 6.13 us -> 9.81 us  [spread_width(): left = lax.ppermute(last, 'width', steps('width', 1))]
    ppermute x3 -> x4, starting transfers between devices: 6.39 us -> 8.8 us  [flip(): return lax.ppermute(x, 'height', [(i, i ^ bit) for i in range(count)])]
    ppermute x3 -> x4, waiting for transfers between devices: 4.78 us -> 5.16 us  [flip(): return lax.ppermute(x, 'height', [(i, i ^ bit) for i in range(count)])]
  transfers between devices with their start and end apart: 17 -> 18, of which waited for: 8 -> 6; matrix products, arithmetic and copies ran while one was open for 4% -> 6% of each run, Pallas kernels for 12% -> 12%
where the time goes in v4:
time: 169 us; the launch traced here: 168 us
  starting transfers between devices  53.4 us (32%)
  blocking collectives  37.9 us (22%)
  Pallas kernels  37.7 us (22%)
  waiting for transfers between devices  23.4 us (14%)
  other arithmetic  6.44 us (4%)
  local copies, waits for them, and re-layouts  3.96 us (2%)
  matrix products  3.89 us (2%)
    all_gather x1, blocking collectives, on_device(): along_width = lax.all_gather(joined, 'width', axis=0, tiled=True)  37.9 us
    pallas_call x1, Pallas kernels, on_device(): pl.pallas_call(front_kernel, out_shape=(shape((model, 4 * inner), half),...  17.3 us
    ppermute x4, starting transfers between devices, gather_height(): shift = lambda x, by: lax.ppermute(x, 'height', steps('height', by, True))  11.7 us
    ppermute x2, waiting for transfers between devices, on_device(): swap = lambda x: lax.ppermute(x, 'head', [(0, 1), (1, 0)])  11.2 us
    ppermute x2, starting transfers between devices, spread_width(): left = lax.ppermute(last, 'width', steps('width', 1))  9.81 us
    pallas_call x1, Pallas kernels, on_device(): pl.pallas_call(back_kernel, out_shape=(shape((count, width), half), shape...  9.15 us
    ppermute x2, starting transfers between devices, spread_height(): down = lax.ppermute(own, 'height', steps('height', -1))  8.95 us
    ppermute x4, starting transfers between devices, flip(): return lax.ppermute(x, 'height', [(i, i ^ bit) for i in range(count)])  8.8 us
  transfers between devices with their start and end apart: 18, of which 6 were waited for; matrix products, arithmetic and copies ran while one was open for 6% of the time, Pallas kernels for 12%

profile of v4, /device:TPU:6, one launch (start us, length us, event | category | flops | bytes accessed | tf_op | source)
XLA Modules:
  0.0 167.8 jit_solution(3790411944867028734)
XLA Ops:
  0.7 0.7 convert_element_type.35
  1.3 0.1 convert_element_type.36
  1.4 0.1 broadcast_in_dim.2
  1.5 1.2 pad_maximum_fusion.1.own
  2.8 1.9 %collective-permute-start = (bf16[288,1664]{1,0:T(8,128)(2,1)S(1)}, bf16[288,1664]{1,0:T(8,128)(2,1)S(1)}, u32[]{:S(2)}, u32[]{:S(2)}) collective-permute-start(bf16[288,1664]{1,0:T(8,128)(2,1)S(1)} %pad_maximum_fusion.1.own), channel_id=1, source_target_pairs={{0,32},{32,64},{64,96},{96,128},{128,160},{160,192},{192,224},{224... | collective-permute-start | bytes 2875400 | tf_op jit(solution)/shard_map/ppermute | solution.py:268
  4.7 4.5 %collective-permute-start.1 = (bf16[288,1664]{1,0:T(8,128)(2,1)S(1)}, bf16[288,1664]{1,0:T(8,128)(2,1)S(1)}, u32[]{:S(2)}, u32[]{:S(2)}) collective-permute-start(bf16[288,1664]{1,0:T(8,128)(2,1)S(1)} %pad_maximum_fusion.1.own), channel_id=1, source_target_pairs={{32,0},{64,32},{96,64},{128,96},{160,128},{192,160},{224,192},{256... | collective-permute-start | bytes 2875400 | tf_op jit(solution)/shard_map/ppermute | solution.py:269
  9.3 37.9 %all-gather = bf16[16,6,1536]{2,1,0:T(8,128)(2,1)S(1)} all-gather(bf16[1,6,1536]{2,1,0:T(8,128)(2,1)S(1)} %maximum_bitcast_fusion), channel_id=1, replica_groups=mesh['height'=16,'width'=16,'head'=2] {'width'}, dimensions={0}, use_global_device_ids=true | all-gather | bytes 313344 | tf_op jit(solution)/shard_map/all_gather | solution.py:354
  47.2 0.8 reshape.42
  48.0 0.0 collective-permute-done.up
  48.0 0.0 collective-permute-done.1.down
  48.0 0.0 copy-start.4
  48.0 2.4 %collective-permute-start.2 = (bf16[96,1536]{1,0:T(8,128)(2,1)}, bf16[96,1536]{1,0:T(8,128)(2,1)S(1)}, u32[]{:S(2)}, u32[]{:S(2)}) collective-permute-start(bf16[96,1536]{1,0:T(8,128)(2,1)} %reshape.42), channel_id=1, source_target_pairs={{0,64},{32,96},{64,0},{96,32},{128,192},{160,224},{192,128},{224,1... | collective-permute-start | bytes 884744 | tf_op jit(solution)/shard_map/ppermute | solution.py:285
  50.5 0.1 pad_add_fusion.place
  50.5 3.0 %columns.1 = (bf16[288,1664]{1,0:T(8,128)(2,1)}, bf16[288,1664]{1,0:T(8,128)(2,1)}) custom-call(s32[2]{0:T(128)S(1)} %pad_add_fusion.place, bf16[288,1664]{1,0:T(8,128)(2,1)S(1)} %collective-permute-done.up, bf16[288,1664]{1,0:T(8,128)(2,1)S(1)} %pad_maximum_fusion.1.own, bf16[288,1664]{1,0:T(8,128)(2,1)} %copy-done.4), custom_call_target="tpu_custom_call" | custom-call | tf_op jit(solution)/shard_map/columns/pallas_call | solution.py:329
  53.6 3.4 %collective-permute-done.2 = bf16[96,1536]{1,0:T(8,128)(2,1)S(1)} collective-permute-done((bf16[96,1536]{1,0:T(8,128)(2,1)}, bf16[96,1536]{1,0:T(8,128)(2,1)S(1)}, u32[]{:S(2)}, u32[]{:S(2)}) %collective-permute-start.2) | collective-permute-done | bytes 294944 | tf_op jit(solution)/shard_map/ppermute | solution.py:285
  57.1 1.3 collective-permute-start.4
  58.4 1.9 %collective-permute-start.6 = (bf16[192,1536]{1,0:T(8,128)(2,1)S(1)}, bf16[192,1536]{1,0:T(8,128)(2,1)S(1)}, u32[]{:S(2)}, u32[]{:S(2)}) collective-permute-start(bf16[192,1536]{1,0:T(8,128)(2,1)S(1)} %pad_maximum_fusion.3), channel_id=1, source_target_pairs={{0,128},{32,160},{64,192},{96,224},{128,256},{160,288},{192,320},{... | collective-permute-start | bytes 1769480 | tf_op jit(solution)/shard_map/ppermute | solution.py:289
  60.3 3.9 %collective-permute-start.7 = (bf16[192,1536]{1,0:T(8,128)(2,1)S(1)}, bf16[192,1536]{1,0:T(8,128)(2,1)}, u32[]{:S(2)}, u32[]{:S(2)}) collective-permute-start(bf16[192,1536]{1,0:T(8,128)(2,1)S(1)} %pad_maximum_fusion.3), channel_id=1, source_target_pairs={{0,384},{32,416},{64,448},{96,480},{128,0},{160,32},{192,64},{224,... | collective-permute-start | bytes 1769480 | tf_op jit(solution)/shard_map/ppermute | solution.py:289
  64.2 4.6 %collective-permute-start.3 = (bf16[288,1664]{1,0:T(8,128)(2,1)}, bf16[288,1664]{1,0:T(8,128)(2,1)S(1)}, u32[]{:S(2)}, u32[]{:S(2)}) collective-permute-start(bf16[288,1664]{1,0:T(8,128)(2,1)} %get-tuple-element.37), channel_id=1, source_target_pairs={{0,2},{2,4},{4,6},{6,8},{8,10},{10,12},{12,14},{14,16},{16,18},{18... | collective-permute-start | bytes 2875400 | tf_op jit(solution)/shard_map/ppermute | solution.py:274
  68.8 4.5 %collective-permute-done.6 = bf16[192,1536]{1,0:T(8,128)(2,1)S(1)} collective-permute-done((bf16[192,1536]{1,0:T(8,128)(2,1)S(1)}, bf16[192,1536]{1,0:T(8,128)(2,1)S(1)}, u32[]{:S(2)}, u32[]{:S(2)}) %collective-permute-start.6) | collective-permute-done | bytes 589856 | tf_op jit(solution)/shard_map/ppermute | solution.py:289
  73.3 0.7 slice.32
  74.0 2.9 %collective-permute-start.8 = (bf16[96,1536]{1,0:T(8,128)(2,1)}, bf16[96,1536]{1,0:T(8,128)(2,1)S(1)}, u32[]{:S(2)}, u32[]{:S(2)}) collective-permute-start(bf16[96,1536]{1,0:T(8,128)(2,1)} %slice.32), channel_id=1, source_target_pairs={{0,128},{32,160},{64,192},{96,224},{128,256},{160,288},{192,320},{... | collective-permute-start | bytes 884744 | tf_op jit(solution)/shard_map/ppermute | solution.py:289
  76.9 0.0 collective-permute-done.7
  76.9 1.0 slice.33
  77.9 3.0 %collective-permute-start.9 = (bf16[96,1536]{1,0:T(8,128)(2,1)S(1)}, bf16[96,1536]{1,0:T(8,128)(2,1)S(1)}, u32[]{:S(2)}, u32[]{:S(2)}) collective-permute-start(bf16[96,1536]{1,0:T(8,128)(2,1)S(1)} %slice.33), channel_id=1, source_target_pairs={{0,384},{32,416},{64,448},{96,480},{128,0},{160,32},{192,64},{224,... | collective-permute-start | bytes 884744 | tf_op jit(solution)/shard_map/ppermute | solution.py:289
  80.9 2.4 %pad_maximum_fusion.rest_0_ = bf16[576,1536]{1,0:T(8,128)(2,1)} fusion(bf16[192,1536]{1,0:T(8,128)(2,1)} %collective-permute-done.7, bf16[192,1536]{1,0:T(8,128)(2,1)S(1)} %collective-permute-done.6, bf16[192,1536]{1,0:T(8,128)(2,1)S(1)} %pad_maximum_fusion.3), kind=kLoop, calls=%fused_computation | loop fusion | flops 5308416 | bytes 3538944 | tf_op jit(solution)/shard_map/concatenate | solution.py:299
  83.3 0.0 collective-permute-done.8
  83.3 1.9 %collective-permute-start.10 = (bf16[576,1536]{1,0:T(8,128)(2,1)}, bf16[576,1536]{1,0:T(8,128)(2,1)}, u32[]{:S(2)}, u32[]{:S(2)}) collective-permute-start(bf16[576,1536]{1,0:T(8,128)(2,1)} %pad_maximum_fusion.rest_0_), channel_id=1, source_target_pairs={{0,32},{32,0},{64,96},{96,64},{128,160},{160,128},{192,224},{224,1... | collective-permute-start | bytes 5308424 | tf_op jit(solution)/shard_map/ppermute | solution.py:285
  85.2 0.0 collective-permute-done.4.right
  85.3 1.0 copy-done.9
  86.3 0.0 copy-start.13
  86.3 0.0 copy-start.14
  86.3 0.0 copy-start.8
  86.3 0.0 collective-permute-done.3.left
  86.4 1.0 pad_maximum_fusion.2
  87.4 2.4 %collective-permute-start.5 = (bf16[288,1664]{1,0:T(8,128)(2,1)}, bf16[288,1664]{1,0:T(8,128)(2,1)}, u32[]{:S(2)}, u32[]{:S(2)}) collective-permute-start(bf16[288,1664]{1,0:T(8,128)(2,1)} %pad_maximum_fusion.2), channel_id=1, source_target_pairs={{0,32},{32,0},{64,96},{96,64},{128,160},{160,128},{192,224},{224,1... | collective-permute-start | bytes 2875400 | tf_op jit(solution)/shard_map/ppermute | solution.py:285
  89.8 0.0 collective-permute-done.9
  89.9 2.1 %collective-permute-start.11 = (bf16[192,1536]{1,0:T(8,128)(2,1)S(1)}, bf16[192,1536]{1,0:T(8,128)(2,1)S(1)}, u32[]{:S(2)}, u32[]{:S(2)}) collective-permute-start(bf16[192,1536]{1,0:T(8,128)(2,1)S(1)} %constant_dynamic-update-slice_fusion.rest_1_), channel_id=1, source_target_pairs={{0,32},{32,0},{64,96},{96,64},{128,160},{160,128},{192,224},{224,1... | collective-permute-start | bytes 1769480 | tf_op jit(solution)/shard_map/ppermute | solution.py:285
  92.0 0.0 copy-done.13
  92.0 1.7 %collective-permute-done.11.rest_3_ = bf16[192,1536]{1,0:T(8,128)(2,1)S(1)} collective-permute-done((bf16[192,1536]{1,0:T(8,128)(2,1)S(1)}, bf16[192,1536]{1,0:T(8,128)(2,1)S(1)}, u32[]{:S(2)}, u32[]{:S(2)}) %collective-permute-start.11) | collective-permute-done | bytes 589856 | tf_op jit(solution)/shard_map/ppermute | solution.py:285
  93.8 0.0 collective-permute-done.5.shared
  93.8 0.0 collective-permute-done.10.rest_2_
  93.8 17.3 %front.1 = (bf16[1536,1536]{1,0:T(8,128)(2,1)}, bf16[288,384]{1,0:T(8,128)(2,1)S(1)}, bf16[288,384]{1,0:T(8,128)(2,1)S(1)}, bf16[288,128]{1,0:T(8,128)(2,1)S(1)}...) custom-call(s32[2]{0:T(128)S(1)} %pad_add_fusion.place, ...), custom_call_target="tpu_custom_call" | custom-call | tf_op jit(solution)/shard_map/front/pallas_call | solution.py:361
  111.1 2.0 %collective-permute-start.12 = (bf16[288,512]{1,0:T(8,128)(2,1)S(1)}, bf16[288,512]{1,0:T(8,128)(2,1)S(1)}, u32[]{:S(2)}, u32[]{:S(2)}) collective-permute-start(bf16[288,512]{1,0:T(8,128)(2,1)S(1)} %get-tuple-element.44.own), channel_id=1, source_target_pairs={{0,32},{32,64},{64,96},{96,128},{128,160},{160,192},{192,224},{224... | collective-permute-start | bytes 884744 | tf_op jit(solution)/shard_map/ppermute | solution.py:268
  113.2 4.4 %collective-permute-start.13 = (bf16[288,512]{1,0:T(8,128)(2,1)S(1)}, bf16[288,512]{1,0:T(8,128)(2,1)S(1)}, u32[]{:S(2)}, u32[]{:S(2)}) collective-permute-start(bf16[288,512]{1,0:T(8,128)(2,1)S(1)} %get-tuple-element.44.own), channel_id=1, source_target_pairs={{32,0},{64,32},{96,64},{128,96},{160,128},{192,160},{224,192},{256... | collective-permute-start | bytes 884744 | tf_op jit(solution)/shard_map/ppermute | solution.py:269
  117.6 0.0 copy-start.1
  117.6 0.0 copy-start.3
  117.7 0.0 copy-start.5
  117.7 0.0 copy-start.7
  117.7 1.6 convolution_convert_fusion
  119.3 0.9 collective-permute-done.12.up
  120.2 1.7 collective-permute-done.13.down
  121.9 1.3 collective-permute-start.16
  123.2 5.2 %collective-permute-start.15 = (bf16[432,512]{1,0:T(8,128)(2,1)S(1)}, bf16[432,512]{1,0:T(8,128)(2,1)S(1)}, u32[]{:S(2)}, u32[]{:S(2)}) collective-permute-start(bf16[432,512]{1,0:T(8,128)(2,1)S(1)} %pad_maximum_fusion.4), channel_id=1, source_target_pairs={{0,2},{2,4},{4,6},{6,8},{8,10},{10,12},{12,14},{14,16},{16,18},{18... | collective-permute-start | bytes 1327112 | tf_op jit(solution)/shard_map/ppermute | solution.py:274
  128.5 4.9 %collective-permute-start.14 = (bf16[288,768]{1,0:T(8,128)(2,1)S(1)}, bf16[288,768]{1,0:T(8,128)(2,1)S(1)}, u32[]{:S(2)}, u32[]{:S(2)}) collective-permute-start(bf16[288,768]{1,0:T(8,128)(2,1)S(1)} %convolution_convert_fusion), channel_id=1, source_target_pairs={{0,1},{1,0},{2,3},{3,2},{4,5},{5,4},{6,7},{7,6},{8,9},{9,8},{10,11... | collective-permute-start | bytes 1327112 | tf_op jit(solution)/shard_map/ppermute | solution.py:395
  133.4 8.2 %queries.1.queries_in = bf16[1728,384]{1,0:T(8,128)(2,1)} custom-call(s32[2]{0:T(128)S(1)} %pad_add_fusion.place, bf16[288,1664]{1,0:T(8,128)(2,1)S(1)} %copy-done.1, bf16[288,1664]{1,0:T(8,128)(2,1)S(1)} %copy-done.3, bf16[288,1664]{1,0:T(8,128)(2,1)S(1)} %copy-done.5, bf16[288,1664]{1,0:T(8,128)(2,1)S(1)} %copy-done.7, bf16[288,1664]{1,0:T(8,128)(2,1)} %copy-done.9, ...), custom_call_target="tpu_custom_call" | custom-call | flops 2038431744 | bytes 8388608 | tf_op jit(solution)/shard_map/queries/pallas_call | solution.py:405
  141.7 0.0 collective-permute-done.16.right
  141.7 0.0 collective-permute-done.15.left
  141.7 9.1 %back.1 = (bf16[288,768]{1,0:T(8,128)(2,1)S(1)}, bf16[288,768]{1,0:T(8,128)(2,1)S(1)}) custom-call(s32[2]{0:T(128)S(1)} %pad_add_fusion.place, bf16[288,512]{1,0:T(8,128)(2,1)S(1)} %get-tuple-element.44.own, bf16[288,512]{1,0:T(8,128)(2,1)S(1)} %collective-permute-done.12.up, bf16[288,512]{1,0:T(8,128)(2,1)S(1)} %collective-permute-done.13.down, ...), custom_call_target="tpu_custom_call" | custom-call | tf_op jit(solution)/shard_map/back/pallas_call | solution.py:420
  150.8 2.6 %collective-permute-start.17 = (bf16[288,768]{1,0:T(8,128)(2,1)S(1)}, bf16[288,768]{1,0:T(8,128)(2,1)S(1)}, u32[]{:S(2)}, u32[]{:S(2)}) collective-permute-start(bf16[288,768]{1,0:T(8,128)(2,1)S(1)} %get-tuple-element.61), channel_id=1, source_target_pairs={{0,1},{1,0},{2,3},{3,2},{4,5},{5,4},{6,7},{7,6},{8,9},{9,8},{10,11... | collective-permute-start | bytes 1327112 | tf_op jit(solution)/shard_map/ppermute | solution.py:395
  153.5 0.0 collective-permute-done.14
  153.5 2.3 %fusion.2 = bf16[288,768]{1,0:T(8,128)(2,1)} fusion(bf16[288,384]{1,0:T(8,128)(2,1)S(1)} %get-tuple-element.42, bf16[288,768]{1,0:T(8,128)(2,1)S(1)} %collective-permute-done.14, bf16[1536,1536]{1,0:T(8,128)(2,1)} %get-tuple-element.43.whole, s32[]{:T(128)S(6)} %select_n.11), kind=kOutput, calls=%fused_computation.5 | convolution fusion | flops 170975232 | bytes 1695748 | tf_op jit(solution)/shard_map/dot_general | solution.py:25
  155.7 11.2 %collective-permute-done.17 = bf16[288,768]{1,0:T(8,128)(2,1)S(1)} collective-permute-done((bf16[288,768]{1,0:T(8,128)(2,1)S(1)}, bf16[288,768]{1,0:T(8,128)(2,1)S(1)}, u32[]{:S(2)}, u32[]{:S(2)}) %collective-permute-start.17) | collective-permute-done | bytes 442400 | tf_op jit(solution)/shard_map/ppermute | solution.py:395
  167.0 0.9 add_convert_fusion
  (33 shorter events, 0.3 us)
Async XLA Ops:
  0.6 8.7 %copy-start.11 = (bf16[6,3,384]{2,1,0:T(4,128)(2,1)S(1)}, bf16[6,3,384]{2,1,0:T(4,128)(2,1)}, u32[]{:S(2)}) copy-start(bf16[6,3,384]{2,1,0:T(4,128)(2,1)} %param.9) | copy-start | bytes 41476
  0.6 8.7 %copy-start.12 = (bf16[6,384]{1,0:T(8,128)(2,1)S(1)}, bf16[6,384]{1,0:T(8,128)(2,1)}, u32[]{:S(2)}) copy-start(bf16[6,384]{1,0:T(8,128)(2,1)} %param.10) | copy-start | bytes 13828
  2.8 50.8 %copy-start = (bf16[288,1664]{1,0:T(8,128)(2,1)}, bf16[288,1664]{1,0:T(8,128)(2,1)S(1)}, u32[]{:S(2)}) copy-start(bf16[288,1664]{1,0:T(8,128)(2,1)S(1)} %pad_maximum_fusion.1.own) | copy-start | bytes 2875396
  2.8 45.2 %collective-permute-start = (bf16[288,1664]{1,0:T(8,128)(2,1)S(1)}, bf16[288,1664]{1,0:T(8,128)(2,1)S(1)}, u32[]{:S(2)}, u32[]{:S(2)}) collective-permute-start(bf16[288,1664]{1,0:T(8,128)(2,1)S(1)} %pad_maximum_fusion.1.own), channel_id=1, source_target_pairs={{0,32},{32,64},{64,96},{96,128},{128,160},{160,192},{192,224},{224... | collective-permute-start | bytes 2875400 | tf_op jit(solution)/shard_map/ppermute | solution.py:268
  4.7 43.3 %collective-permute-start.1 = (bf16[288,1664]{1,0:T(8,128)(2,1)S(1)}, bf16[288,1664]{1,0:T(8,128)(2,1)S(1)}, u32[]{:S(2)}, u32[]{:S(2)}) collective-permute-start(bf16[288,1664]{1,0:T(8,128)(2,1)S(1)} %pad_maximum_fusion.1.own), channel_id=1, source_target_pairs={{32,0},{64,32},{96,64},{128,96},{160,128},{192,160},{224,192},{256... | collective-permute-start | bytes 2875400 | tf_op jit(solution)/shard_map/ppermute | solution.py:269
  48.0 9.0 %copy-start.10 = (bf16[96,1536]{1,0:T(8,128)(2,1)S(1)}, bf16[96,1536]{1,0:T(8,128)(2,1)}, u32[]{:S(2)}) copy-start(bf16[96,1536]{1,0:T(8,128)(2,1)} %reshape.42) | copy-start | bytes 884740
  48.0 9.0 %copy-start.2 = (bf16[288,1664]{1,0:T(8,128)(2,1)}, bf16[288,1664]{1,0:T(8,128)(2,1)S(1)}, u32[]{:S(2)}) copy-start(bf16[288,1664]{1,0:T(8,128)(2,1)S(1)} %collective-permute-done.up) | copy-start | bytes 2875396
  48.0 2.5 %copy-start.4 = (bf16[288,1664]{1,0:T(8,128)(2,1)}, bf16[288,1664]{1,0:T(8,128)(2,1)S(1)}, u32[]{:S(2)}) copy-start(bf16[288,1664]{1,0:T(8,128)(2,1)S(1)} %collective-permute-done.1.down) | copy-start | bytes 2875396
  48.0 9.0 %collective-permute-start.2 = (bf16[96,1536]{1,0:T(8,128)(2,1)}, bf16[96,1536]{1,0:T(8,128)(2,1)S(1)}, u32[]{:S(2)}, u32[]{:S(2)}) collective-permute-start(bf16[96,1536]{1,0:T(8,128)(2,1)} %reshape.42), channel_id=1, source_target_pairs={{0,64},{32,96},{64,0},{96,32},{128,192},{160,224},{192,128},{224,1... | collective-permute-start | bytes 884744 | tf_op jit(solution)/shard_map/ppermute | solution.py:285
  57.1 28.2 %collective-permute-start.4 = (bf16[288,1664]{1,0:T(8,128)(2,1)}, bf16[288,1664]{1,0:T(8,128)(2,1)S(1)}, u32[]{:S(2)}, u32[]{:S(2)}) collective-permute-start(bf16[288,1664]{1,0:T(8,128)(2,1)} %get-tuple-element.38), channel_id=1, source_target_pairs={{2,0},{4,2},{6,4},{8,6},{10,8},{12,10},{14,12},{16,14},{18,16},{20... | collective-permute-start | bytes 2875400 | tf_op jit(solution)/shard_map/ppermute | solution.py:275
  58.4 14.9 %collective-permute-start.6 = (bf16[192,1536]{1,0:T(8,128)(2,1)S(1)}, bf16[192,1536]{1,0:T(8,128)(2,1)S(1)}, u32[]{:S(2)}, u32[]{:S(2)}) collective-permute-start(bf16[192,1536]{1,0:T(8,128)(2,1)S(1)} %pad_maximum_fusion.3), channel_id=1, source_target_pairs={{0,128},{32,160},{64,192},{96,224},{128,256},{160,288},{192,320},{... | collective-permute-start | bytes 1769480 | tf_op jit(solution)/shard_map/ppermute | solution.py:289
  60.3 16.6 %collective-permute-start.7 = (bf16[192,1536]{1,0:T(8,128)(2,1)S(1)}, bf16[192,1536]{1,0:T(8,128)(2,1)}, u32[]{:S(2)}, u32[]{:S(2)}) collective-permute-start(bf16[192,1536]{1,0:T(8,128)(2,1)S(1)} %pad_maximum_fusion.3), channel_id=1, source_target_pairs={{0,384},{32,416},{64,448},{96,480},{128,0},{160,32},{192,64},{224,... | collective-permute-start | bytes 1769480 | tf_op jit(solution)/shard_map/ppermute | solution.py:289
  64.2 22.1 %collective-permute-start.3 = (bf16[288,1664]{1,0:T(8,128)(2,1)}, bf16[288,1664]{1,0:T(8,128)(2,1)S(1)}, u32[]{:S(2)}, u32[]{:S(2)}) collective-permute-start(bf16[288,1664]{1,0:T(8,128)(2,1)} %get-tuple-element.37), channel_id=1, source_target_pairs={{0,2},{2,4},{4,6},{6,8},{8,10},{10,12},{12,14},{14,16},{16,18},{18... | collective-permute-start | bytes 2875400 | tf_op jit(solution)/shard_map/ppermute | solution.py:274
  74.0 9.3 %collective-permute-start.8 = (bf16[96,1536]{1,0:T(8,128)(2,1)}, bf16[96,1536]{1,0:T(8,128)(2,1)S(1)}, u32[]{:S(2)}, u32[]{:S(2)}) collective-permute-start(bf16[96,1536]{1,0:T(8,128)(2,1)} %slice.32), channel_id=1, source_target_pairs={{0,128},{32,160},{64,192},{96,224},{128,256},{160,288},{192,320},{... | collective-permute-start | bytes 884744 | tf_op jit(solution)/shard_map/ppermute | solution.py:289
  77.9 11.9 %collective-permute-start.9 = (bf16[96,1536]{1,0:T(8,128)(2,1)S(1)}, bf16[96,1536]{1,0:T(8,128)(2,1)S(1)}, u32[]{:S(2)}, u32[]{:S(2)}) collective-permute-start(bf16[96,1536]{1,0:T(8,128)(2,1)S(1)} %slice.33), channel_id=1, source_target_pairs={{0,384},{32,416},{64,448},{96,480},{128,0},{160,32},{192,64},{224,... | collective-permute-start | bytes 884744 | tf_op jit(solution)/shard_map/ppermute | solution.py:289
  83.3 10.5 %collective-permute-start.10 = (bf16[576,1536]{1,0:T(8,128)(2,1)}, bf16[576,1536]{1,0:T(8,128)(2,1)}, u32[]{:S(2)}, u32[]{:S(2)}) collective-permute-start(bf16[576,1536]{1,0:T(8,128)(2,1)} %pad_maximum_fusion.rest_0_), channel_id=1, source_target_pairs={{0,32},{32,0},{64,96},{96,64},{128,160},{160,128},{192,224},{224,1... | collective-permute-start | bytes 5308424 | tf_op jit(solution)/shard_map/ppermute | solution.py:285
  85.2 1.0 copy-start.9
  86.3 5.7 %copy-start.13 = (f32[384]{0:T(512)S(1)}, f32[384]{0:T(512)}, u32[]{:S(2)}) copy-start(f32[384]{0:T(512)} %param.11) | copy-start | bytes 4612
  86.3 5.7 %copy-start.14 = (f32[384]{0:T(512)S(1)}, f32[384]{0:T(512)}, u32[]{:S(2)}) copy-start(f32[384]{0:T(512)} %param.12) | copy-start | bytes 4612
  86.3 7.5 %copy-start.8 = (bf16[1,2,144,1536]{3,2,1,0:T(8,128)(2,1)S(1)}, bf16[1,2,144,1536]{3,2,1,0:T(8,128)(2,1)}, u32[]{:S(2)}) copy-start(bf16[1,2,144,1536]{3,2,1,0:T(8,128)(2,1)} %param.8) | copy-start | bytes 2654212
  86.3 3.6 %copy-start.6 = (bf16[288,1664]{1,0:T(8,128)(2,1)}, bf16[288,1664]{1,0:T(8,128)(2,1)S(1)}, u32[]{:S(2)}) copy-start(bf16[288,1664]{1,0:T(8,128)(2,1)S(1)} %collective-permute-done.3.left) | copy-start | bytes 2875396
  87.4 6.4 %collective-permute-start.5 = (bf16[288,1664]{1,0:T(8,128)(2,1)}, bf16[288,1664]{1,0:T(8,128)(2,1)}, u32[]{:S(2)}, u32[]{:S(2)}) collective-permute-start(bf16[288,1664]{1,0:T(8,128)(2,1)} %pad_maximum_fusion.2), channel_id=1, source_target_pairs={{0,32},{32,0},{64,96},{96,64},{128,160},{160,128},{192,224},{224,1... | collective-permute-start | bytes 2875400 | tf_op jit(solution)/shard_map/ppermute | solution.py:285
  89.9 3.9 %collective-permute-start.11 = (bf16[192,1536]{1,0:T(8,128)(2,1)S(1)}, bf16[192,1536]{1,0:T(8,128)(2,1)S(1)}, u32[]{:S(2)}, u32[]{:S(2)}) collective-permute-start(bf16[192,1536]{1,0:T(8,128)(2,1)S(1)} %constant_dynamic-update-slice_fusion.rest_1_), channel_id=1, source_target_pairs={{0,32},{32,0},{64,96},{96,64},{128,160},{160,128},{192,224},{224,1... | collective-permute-start | bytes 1769480 | tf_op jit(solution)/shard_map/ppermute | solution.py:285
  111.1 9.0 %collective-permute-start.12 = (bf16[288,512]{1,0:T(8,128)(2,1)S(1)}, bf16[288,512]{1,0:T(8,128)(2,1)S(1)}, u32[]{:S(2)}, u32[]{:S(2)}) collective-permute-start(bf16[288,512]{1,0:T(8,128)(2,1)S(1)} %get-tuple-element.44.own), channel_id=1, source_target_pairs={{0,32},{32,64},{64,96},{96,128},{128,160},{160,192},{192,224},{224... | collective-permute-start | bytes 884744 | tf_op jit(solution)/shard_map/ppermute | solution.py:268
  113.2 8.6 %collective-permute-start.13 = (bf16[288,512]{1,0:T(8,128)(2,1)S(1)}, bf16[288,512]{1,0:T(8,128)(2,1)S(1)}, u32[]{:S(2)}, u32[]{:S(2)}) collective-permute-start(bf16[288,512]{1,0:T(8,128)(2,1)S(1)} %get-tuple-element.44.own), channel_id=1, source_target_pairs={{32,0},{64,32},{96,64},{128,96},{160,128},{192,160},{224,192},{256... | collective-permute-start | bytes 884744 | tf_op jit(solution)/shard_map/ppermute | solution.py:269
  117.6 15.8 %copy-start.1 = (bf16[288,1664]{1,0:T(8,128)(2,1)S(1)}, bf16[288,1664]{1,0:T(8,128)(2,1)}, u32[]{:S(2)}) copy-start(bf16[288,1664]{1,0:T(8,128)(2,1)} %copy-done) | copy-start | bytes 2875396
  117.6 15.8 %copy-start.3 = (bf16[288,1664]{1,0:T(8,128)(2,1)S(1)}, bf16[288,1664]{1,0:T(8,128)(2,1)}, u32[]{:S(2)}) copy-start(bf16[288,1664]{1,0:T(8,128)(2,1)} %copy-done.2) | copy-start | bytes 2875396
  117.7 15.8 %copy-start.5 = (bf16[288,1664]{1,0:T(8,128)(2,1)S(1)}, bf16[288,1664]{1,0:T(8,128)(2,1)}, u32[]{:S(2)}) copy-start(bf16[288,1664]{1,0:T(8,128)(2,1)} %copy-done.4) | copy-start | bytes 2875396
  117.7 15.8 %copy-start.7 = (bf16[288,1664]{1,0:T(8,128)(2,1)S(1)}, bf16[288,1664]{1,0:T(8,128)(2,1)}, u32[]{:S(2)}) copy-start(bf16[288,1664]{1,0:T(8,128)(2,1)} %copy-done.6) | copy-start | bytes 2875396
  121.9 19.7 %collective-permute-start.16 = (bf16[432,512]{1,0:T(8,128)(2,1)S(1)}, bf16[432,512]{1,0:T(8,128)(2,1)S(1)}, u32[]{:S(2)}, u32[]{:S(2)}) collective-permute-start(bf16[432,512]{1,0:T(8,128)(2,1)S(1)} %pad_maximum_fusion.5), channel_id=1, source_target_pairs={{2,0},{4,2},{6,4},{8,6},{10,8},{12,10},{14,12},{16,14},{18,16},{20... | collective-permute-start | bytes 1327112 | tf_op jit(solution)/shard_map/ppermute | solution.py:275
  123.2 18.4 %collective-permute-start.15 = (bf16[432,512]{1,0:T(8,128)(2,1)S(1)}, bf16[432,512]{1,0:T(8,128)(2,1)S(1)}, u32[]{:S(2)}, u32[]{:S(2)}) collective-permute-start(bf16[432,512]{1,0:T(8,128)(2,1)S(1)} %pad_maximum_fusion.4), channel_id=1, source_target_pairs={{0,2},{2,4},{4,6},{6,8},{8,10},{10,12},{12,14},{14,16},{16,18},{18... | collective-permute-start | bytes 1327112 | tf_op jit(solution)/shard_map/ppermute | solution.py:274
  128.5 25.0 %collective-permute-start.14 = (bf16[288,768]{1,0:T(8,128)(2,1)S(1)}, bf16[288,768]{1,0:T(8,128)(2,1)S(1)}, u32[]{:S(2)}, u32[]{:S(2)}) collective-permute-start(bf16[288,768]{1,0:T(8,128)(2,1)S(1)} %convolution_convert_fusion), channel_id=1, source_target_pairs={{0,1},{1,0},{2,3},{3,2},{4,5},{5,4},{6,7},{7,6},{8,9},{9,8},{10,11... | collective-permute-start | bytes 1327112 | tf_op jit(solution)/shard_map/ppermute | solution.py:395
  150.8 16.1 %collective-permute-start.17 = (bf16[288,768]{1,0:T(8,128)(2,1)S(1)}, bf16[288,768]{1,0:T(8,128)(2,1)S(1)}, u32[]{:S(2)}, u32[]{:S(2)}) collective-permute-start(bf16[288,768]{1,0:T(8,128)(2,1)S(1)} %get-tuple-element.61), channel_id=1, source_target_pairs={{0,1},{1,0},{2,3},{3,2},{4,5},{5,4},{6,7},{7,6},{8,9},{9,8},{10,11... | collective-permute-start | bytes 1327112 | tf_op jit(solution)/shard_map/ppermute | solution.py:395

commit v5 on v4

--- a/solution.py
+++ b/solution.py
@@ -15,6 +15,7 @@
 EXTENDED = 12 * TILE
 OWN_TILES = (4, 7)
 MASK_LANE = 18
+SIDE_LANES = (19, 20)
 MASK_DEPTH = 1e5
 FACTOR = HEAD_DIM ** (-0.5)
 VMEM_BYTES = 50 * 1024 * 1024
@@ -31,6 +32,22 @@
 
 def lane_index(rows):
     return lax.broadcasted_iota(jnp.int32, (rows, LANES), 1)
+
+
+def side_rows(rows):
+    row = lax.broadcasted_iota(jnp.int32, (rows, LANES), 0)
+    lane = lane_index(rows)
+    first = (row < TILE) & (lane == SIDE_LANES[0])
+    second = (row >= TILE) & (lane == SIDE_LANES[1])
+    return jnp.where(first | second, 1.0, 0.0)
+
+
+def side_marks(start, rows):
+    row = start + lax.broadcasted_iota(jnp.int32, (rows, LANES), 0)
+    lane = lane_index(rows)
+    last = (row >= WINDOW) & (lane == SIDE_LANES[0])
+    first = (row < COLUMN) & (lane == SIDE_LANES[1])
+    return jnp.where(first | last, -MASK_DEPTH, 0.0)
 
 
 def norm_inverse(raw_values):
@@ -144,7 +161,7 @@
         values[rows, :] = result[:, inner:].astype(jnp.bfloat16)
         valid = tok[rows, model:].astype(jnp.float32)
         deep = jnp.where(lane_index(chunk) == MASK_LANE, MASK_DEPTH, 0.0)
-        marks[rows, :] = (valid * deep - deep).astype(jnp.bfloat16)
+        marks[rows, :] = (valid * deep - deep + side_marks(step * chunk, chunk)).astype(jnp.bfloat16)
         for tile, at in enumerate(OWN_TILES):
             offset = at * TILE % chunk
 
@@ -155,33 +172,31 @@
         return carry
 
     lax.fori_loop(0, EXTENDED // chunk, project, 0, unroll=True)
-    lane = lane_index(TILE)
-    one_mark = jnp.where(lane == MASK_LANE, 1.0, 0.0)
+    count = own_keys.shape[0]
+    lane = lane_index(count)
+    stats = jnp.where(lane == MASK_LANE, 1.0, 0.0)
+    query_marks = (stats + side_rows(count)).astype(jnp.bfloat16)
+    for head in heads:
+        lanes = slice(head * HEAD_DIM, (head + 1) * HEAD_DIM)
+        q_aug = jnp.concatenate([own_queries[:, lanes], query_marks], axis=1)
+        k_aug = jnp.concatenate([keys[:, lanes], marks[...]], axis=1)
+        weights = jnp.exp(dot_rows(q_aug, k_aug) * FACTOR)
+        total = jnp.sum(weights, axis=-1, keepdims=True)
+        probs = weights * (1.0 / total)
+        attended[:, lanes] = dot_plain(probs.astype(jnp.bfloat16), values[:, lanes]).astype(jnp.bfloat16)
+        grad_probs = dot_rows(message[:, lanes], values[:, lanes])
+        delta = jnp.sum(probs * grad_probs, axis=-1, keepdims=True)
+        grad_scores = (probs * (grad_probs - delta)).astype(jnp.bfloat16)
+        upstream_q = dot_plain(grad_scores, keys[:, lanes]) * FACTOR
+        grad_q[:, lanes] = norm_backward(own_raw[:, lanes], q_gain[:, lanes], upstream_q).astype(jnp.bfloat16)
+        for n, part in enumerate(three_parts(jnp.log(total) * (1.0 / FACTOR))):
+            stats = jnp.where(lane == 3 * head + n, part, stats)
+        for n, part in enumerate(three_parts(delta)):
+            stats = jnp.where(lane == 9 + 3 * head + n, part, stats)
+    message[:, inner:] = stats.astype(jnp.bfloat16)
     for tile, at in enumerate(OWN_TILES):
         mine = slice(tile * TILE, (tile + 1) * TILE)
         ext = slice(at * TILE, (at + 1) * TILE)
-        window = slice(tile * COLUMN, tile * COLUMN + WINDOW)
-        stats = one_mark
-        for head in heads:
-            lanes = slice(head * HEAD_DIM, (head + 1) * HEAD_DIM)
-            q_aug = jnp.concatenate([own_queries[mine, lanes], one_mark.astype(jnp.bfloat16)], axis=1)
-            win_keys = keys[window, lanes]
-            win_values = values[window, lanes]
-            k_aug = jnp.concatenate([win_keys, marks[window, :]], axis=1)
-            weights = jnp.exp(dot_rows(q_aug, k_aug) * FACTOR)
-            total = jnp.sum(weights, axis=-1, keepdims=True)
-            probs = weights * (1.0 / total)
-            attended[mine, lanes] = dot_plain(probs.astype(jnp.bfloat16), win_values).astype(jnp.bfloat16)
-            grad_probs = dot_rows(message[mine, lanes], win_values)
-            delta = jnp.sum(probs * grad_probs, axis=-1, keepdims=True)
-            grad_scores = (probs * (grad_probs - delta)).astype(jnp.bfloat16)
-            upstream_q = dot_plain(grad_scores, win_keys) * FACTOR
-            grad_q[mine, lanes] = norm_backward(own_raw[mine, lanes], q_gain[:, lanes], upstream_q).astype(jnp.bfloat16)
-            for n, part in enumerate(three_parts(jnp.log(total) * (1.0 / FACTOR))):
-                stats = jnp.where(lane == 3 * head + n, part, stats)
-            for n, part in enumerate(three_parts(delta)):
-                stats = jnp.where(lane == 9 + 3 * head + n, part, stats)
-        message[mine, inner:] = stats.astype(jnp.bfloat16)
         own_keys[mine, :] = keys[ext, :]
         own_values[mine, :] = values[ext, :]
         own_marks[mine, :] = marks[ext, :]
@@ -195,63 +210,47 @@
     copies = token_copies_of(lax.rem(place[0], 2), own, up, down, left, right, shared, tok, sems)
     for copy in [weight_copy] + copies:
         copy.start()
-    for copy in [weight_copy] + copies:
-        copy.wait()
+    weight_copy.wait()
     chunk = 4 * TILE
-
-    def project(step, carry):
-        rows = pl.ds(pl.multiple_of(step * chunk, chunk), chunk)
+    for step, arrived in enumerate((copies[:3], copies[3:7], copies[7:])):
+        for copy in arrived:
+            copy.wait()
+        rows = slice(step * chunk, (step + 1) * chunk)
         result = dot_plain(tok[rows, :model], weight[...])
         for head in range(inner // HEAD_DIM):
             lanes = slice(head * HEAD_DIM, (head + 1) * HEAD_DIM)
             q_raw = result[:, lanes]
             queries[rows, lanes] = (q_raw * norm_inverse(q_raw) * q_gain[:, lanes]).astype(jnp.bfloat16)
-        return carry
-
-    lax.fori_loop(0, EXTENDED // chunk, project, 0, unroll=True)
-
-
-def back_kernel(place, own, up, down, left, right, queries_in, keys_in, values_in, marks_in, k_raw_in, grad_q_in, whole,
-                k_gain, kept, sent, ext, grad_qkv, weight, queries, keys, values, marks, k_raw, sems, load_sems, weight_sem):
+
+
+def back_kernel(place, own, up, down, left, right, queries, keys, values, marks, k_raw, grad_q, whole, k_gain,
+                kept, sent, ext, grad_qkv, weight, sems, weight_sem):
     inner = queries.shape[1]
-    loads = [
-        pltpu.make_async_copy(src, dst, load_sems.at[n])
-        for n, (src, dst) in enumerate((
-            (queries_in, queries),
-            (keys_in, keys),
-            (values_in, values),
-            (marks_in, marks),
-            (k_raw_in, k_raw),
-            (grad_q_in, grad_qkv.at[:, pl.ds(0, inner)]),
-        ))
-    ]
     copies = extended_copies(own, up, down, left, right, ext, sems)
     weight_copy = pltpu.make_async_copy(whole.at[:, pl.ds(0, 3 * inner)], weight, weight_sem.at[0])
-    for copy in copies + loads + [weight_copy]:
+    for copy in copies + [weight_copy]:
         copy.start()
-    for copy in copies + loads:
+    for copy in copies:
         copy.wait()
-    lane = lane_index(TILE)
-    for tile in range(2):
-        mine = slice(tile * TILE, (tile + 1) * TILE)
-        window = slice(tile * COLUMN, tile * COLUMN + WINDOW)
-        stats = ext[window, inner:]
-        for head in range(inner // HEAD_DIM):
-            lanes = slice(head * HEAD_DIM, (head + 1) * HEAD_DIM)
-            k_signs = jnp.where((lane >= 3 * head) & (lane < 3 * head + 3), -1.0, 0.0).astype(jnp.bfloat16)
-            v_signs = jnp.where((lane >= 9 + 3 * head) & (lane < 12 + 3 * head), -1.0, 0.0).astype(jnp.bfloat16)
-            k_aug = jnp.concatenate([keys[mine, lanes], marks[mine, :] + k_signs], axis=1)
-            v_aug = jnp.concatenate([values[mine, lanes], v_signs], axis=1)
-            win_queries = queries[window, lanes]
-            win_upstream = ext[window, lanes]
-            probs = jnp.exp(dot_rows(k_aug, jnp.concatenate([win_queries, stats], axis=1)) * FACTOR)
-            centred = dot_rows(v_aug, jnp.concatenate([win_upstream, stats], axis=1))
-            grad_scores = (probs * centred).astype(jnp.bfloat16)
-            grad_v = dot_plain(probs.astype(jnp.bfloat16), win_upstream)
-            upstream_k = dot_plain(grad_scores, win_queries) * FACTOR
-            grad_k = norm_backward(k_raw[mine, lanes], k_gain[:, lanes], upstream_k)
-            grad_qkv[mine, inner + head * HEAD_DIM : inner + (head + 1) * HEAD_DIM] = grad_k.astype(jnp.bfloat16)
-            grad_qkv[mine, 2 * inner + head * HEAD_DIM : 2 * inner + (head + 1) * HEAD_DIM] = grad_v.astype(jnp.bfloat16)
+    grad_qkv[:, :inner] = grad_q[...]
+    count = keys.shape[0]
+    lane = lane_index(count)
+    stats = ext[:, inner:] + side_marks(0, EXTENDED).astype(jnp.bfloat16)
+    key_marks = marks[...] + side_rows(count).astype(jnp.bfloat16)
+    for head in range(inner // HEAD_DIM):
+        lanes = slice(head * HEAD_DIM, (head + 1) * HEAD_DIM)
+        k_signs = jnp.where((lane >= 3 * head) & (lane < 3 * head + 3), -1.0, 0.0).astype(jnp.bfloat16)
+        v_signs = jnp.where((lane >= 9 + 3 * head) & (lane < 12 + 3 * head), -1.0, 0.0).astype(jnp.bfloat16)
+        k_aug = jnp.concatenate([keys[:, lanes], key_marks + k_signs], axis=1)
+        v_aug = jnp.concatenate([values[:, lanes], v_signs], axis=1)
+        probs = jnp.exp(dot_rows(k_aug, jnp.concatenate([queries[:, lanes], stats], axis=1)) * FACTOR)
+        centred = dot_rows(v_aug, jnp.concatenate([ext[:, lanes], stats], axis=1))
+        grad_scores = (probs * centred).astype(jnp.bfloat16)
+        grad_v = dot_plain(probs.astype(jnp.bfloat16), ext[:, lanes])
+        upstream_k = dot_plain(grad_scores, queries[:, lanes]) * FACTOR
+        grad_k = norm_backward(k_raw[:, lanes], k_gain[:, lanes], upstream_k)
+        grad_qkv[:, inner + head * HEAD_DIM : inner + (head + 1) * HEAD_DIM] = grad_k.astype(jnp.bfloat16)
+        grad_qkv[:, 2 * inner + head * HEAD_DIM : 2 * inner + (head + 1) * HEAD_DIM] = grad_v.astype(jnp.bfloat16)
     weight_copy.wait()
     half = kept.shape[1]
     for target, group in ((sent, 1 - place[1]), (kept, place[1])):
@@ -420,19 +419,13 @@
     kept, sent = pl.pallas_call(
         back_kernel,
         out_shape=(shape((count, width), half), shape((count, width), half)),
-        in_specs=[pl.BlockSpec(memory_space=pltpu.SMEM)] + [anywhere] * 12 + [whole_spec()],
+        in_specs=[pl.BlockSpec(memory_space=pltpu.SMEM)] + [anywhere] * 5 + [whole_spec()] * 6 + [anywhere, whole_spec()],
         out_specs=(whole_spec(), whole_spec()),
         scratch_shapes=[
             pltpu.VMEM((EXTENDED, inner + LANES), half),
             pltpu.VMEM((count, 3 * inner), half),
             pltpu.VMEM((model, 3 * inner), half),
-            pltpu.VMEM((EXTENDED, inner), half),
-            pltpu.VMEM((count, inner), half),
-            pltpu.VMEM((count, inner), half),
-            pltpu.VMEM((count, LANES), half),
-            pltpu.VMEM((count, inner), jnp.float32),
             pltpu.SemaphoreType.DMA((8,)),
-            pltpu.SemaphoreType.DMA((6,)),
             pltpu.SemaphoreType.DMA((1,)),
         ],
         compiler_params=pltpu.CompilerParams(vmem_limit_bytes=VMEM_BYTES),

time: 169 us -> 165 us (0.976)
  Pallas kernels: 37.7 us -> 34.5 us
  transfers between devices with their start and end apart: 18 -> 18, of which waited for: 6 -> 6; matrix products, arithmetic and copies ran while one was open for 6% -> 6% of each run, Pallas kernels for 12% -> 11%
where the time goes in v5:
time: 165 us; the launch traced here: 164 us
  starting transfers between devices  53.1 us (32%)
  blocking collectives  37.9 us (23%)
  Pallas kernels  34.5 us (21%)
  waiting for transfers between devices  23.4 us (14%)
  other arithmetic  6.44 us (4%)
  local copies, waits for them, and re-layouts  3.96 us (2%)
  matrix products  3.88 us (2%)
    all_gather x1, blocking collectives, on_device(): along_width = lax.all_gather(joined, 'width', axis=0, tiled=True)  37.9 us
    pallas_call x1, Pallas kernels, on_device(): pl.pallas_call(front_kernel, out_shape=(shape((model, 4 * inner), half),...  15.7 us
    ppermute x4, starting transfers between devices, gather_height(): shift = lambda x, by: lax.ppermute(x, 'height', steps('height', by, True))  11.7 us
    ppermute x2, waiting for transfers between devices, on_device(): swap = lambda x: lax.ppermute(x, 'head', [(0, 1), (1, 0)])  11.2 us
    ppermute x2, starting transfers between devices, spread_width(): left = lax.ppermute(last, 'width', steps('width', 1))  9.81 us
    ppermute x2, starting transfers between devices, spread_height(): down = lax.ppermute(own, 'height', steps('height', -1))  9.14 us
    ppermute x4, starting transfers between devices, flip(): return lax.ppermute(x, 'height', [(i, i ^ bit) for i in range(count)])  8.62 us
    pallas_call x1, Pallas kernels, on_device(): pl.pallas_call(back_kernel, out_shape=(shape((count, width), half), shape...  8.13 us
  transfers between devices with their start and end apart: 18, of which 6 were waited for; matrix products, arithmetic and copies ran while one was open for 6% of the time, Pallas kernels for 11%

profile of v5, /device:TPU:6, one launch (start us, length us, event | category | flops | bytes accessed | tf_op | source)
XLA Modules:
  0.0 164.4 jit_solution(9718290647638418973)
XLA Ops:
  0.6 0.0 copy-start.11
  0.6 0.0 copy-start.12
  0.7 0.7 convert_element_type.35
  1.3 0.1 convert_element_type.36
  1.4 0.1 broadcast_in_dim.2
  1.5 1.2 pad_maximum_fusion.1.own
  2.8 0.0 copy-start
  2.8 1.9 %collective-permute-start = (bf16[288,1664]{1,0:T(8,128)(2,1)S(1)}, bf16[288,1664]{1,0:T(8,128)(2,1)S(1)}, u32[]{:S(2)}, u32[]{:S(2)}) collective-permute-start(bf16[288,1664]{1,0:T(8,128)(2,1)S(1)} %pad_maximum_fusion.1.own), channel_id=1, source_target_pairs={{0,32},{32,64},{64,96},{96,128},{128,160},{160,192},{192,224},{224... | collective-permute-start | bytes 2875400 | tf_op jit(solution)/shard_map/ppermute | solution.py:267
  4.7 4.5 %collective-permute-start.1 = (bf16[288,1664]{1,0:T(8,128)(2,1)S(1)}, bf16[288,1664]{1,0:T(8,128)(2,1)S(1)}, u32[]{:S(2)}, u32[]{:S(2)}) collective-permute-start(bf16[288,1664]{1,0:T(8,128)(2,1)S(1)} %pad_maximum_fusion.1.own), channel_id=1, source_target_pairs={{32,0},{64,32},{96,64},{128,96},{160,128},{192,160},{224,192},{256... | collective-permute-start | bytes 2875400 | tf_op jit(solution)/shard_map/ppermute | solution.py:268
  9.3 0.0 copy-done.11
  9.3 0.0 copy-done.12
  9.3 37.9 %all-gather = bf16[16,6,1536]{2,1,0:T(8,128)(2,1)S(1)} all-gather(bf16[1,6,1536]{2,1,0:T(8,128)(2,1)S(1)} %maximum_bitcast_fusion), channel_id=1, replica_groups=mesh['height'=16,'width'=16,'head'=2] {'width'}, dimensions={0}, use_global_device_ids=true | all-gather | bytes 313344 | tf_op jit(solution)/shard_map/all_gather | solution.py:353
  47.2 0.8 reshape.42
  48.0 0.0 collective-permute-done.up
  48.0 0.0 collective-permute-done.1.down
  48.0 0.0 copy-start.4
  48.0 2.4 %collective-permute-start.2 = (bf16[96,1536]{1,0:T(8,128)(2,1)}, bf16[96,1536]{1,0:T(8,128)(2,1)S(1)}, u32[]{:S(2)}, u32[]{:S(2)}) collective-permute-start(bf16[96,1536]{1,0:T(8,128)(2,1)} %reshape.42), channel_id=1, source_target_pairs={{0,64},{32,96},{64,0},{96,32},{128,192},{160,224},{192,128},{224,1... | collective-permute-start | bytes 884744 | tf_op jit(solution)/shard_map/ppermute | solution.py:284
  50.5 0.1 pad_add_fusion.place
  50.5 3.0 %columns.1 = (bf16[288,1664]{1,0:T(8,128)(2,1)}, bf16[288,1664]{1,0:T(8,128)(2,1)}) custom-call(s32[2]{0:T(128)S(1)} %pad_add_fusion.place, bf16[288,1664]{1,0:T(8,128)(2,1)S(1)} %collective-permute-done.up, bf16[288,1664]{1,0:T(8,128)(2,1)S(1)} %pad_maximum_fusion.1.own, bf16[288,1664]{1,0:T(8,128)(2,1)} %copy-done.4), custom_call_target="tpu_custom_call" | custom-call | tf_op jit(solution)/shard_map/columns/pallas_call | solution.py:328
  53.6 3.4 %collective-permute-done.2 = bf16[96,1536]{1,0:T(8,128)(2,1)S(1)} collective-permute-done((bf16[96,1536]{1,0:T(8,128)(2,1)}, bf16[96,1536]{1,0:T(8,128)(2,1)S(1)}, u32[]{:S(2)}, u32[]{:S(2)}) %collective-permute-start.2) | collective-permute-done | bytes 294944 | tf_op jit(solution)/shard_map/ppermute | solution.py:284
  57.1 1.3 collective-permute-start.4
  58.4 1.9 %collective-permute-start.6 = (bf16[192,1536]{1,0:T(8,128)(2,1)S(1)}, bf16[192,1536]{1,0:T(8,128)(2,1)S(1)}, u32[]{:S(2)}, u32[]{:S(2)}) collective-permute-start(bf16[192,1536]{1,0:T(8,128)(2,1)S(1)} %pad_maximum_fusion.3), channel_id=1, source_target_pairs={{0,128},{32,160},{64,192},{96,224},{128,256},{160,288},{192,320},{... | collective-permute-start | bytes 1769480 | tf_op jit(solution)/shard_map/ppermute | solution.py:288
  60.3 3.9 %collective-permute-start.7 = (bf16[192,1536]{1,0:T(8,128)(2,1)S(1)}, bf16[192,1536]{1,0:T(8,128)(2,1)}, u32[]{:S(2)}, u32[]{:S(2)}) collective-permute-start(bf16[192,1536]{1,0:T(8,128)(2,1)S(1)} %pad_maximum_fusion.3), channel_id=1, source_target_pairs={{0,384},{32,416},{64,448},{96,480},{128,0},{160,32},{192,64},{224,... | collective-permute-start | bytes 1769480 | tf_op jit(solution)/shard_map/ppermute | solution.py:288
  64.2 4.6 %collective-permute-start.3 = (bf16[288,1664]{1,0:T(8,128)(2,1)}, bf16[288,1664]{1,0:T(8,128)(2,1)S(1)}, u32[]{:S(2)}, u32[]{:S(2)}) collective-permute-start(bf16[288,1664]{1,0:T(8,128)(2,1)} %get-tuple-element.37), channel_id=1, source_target_pairs={{0,2},{2,4},{4,6},{6,8},{8,10},{10,12},{12,14},{14,16},{16,18},{18... | collective-permute-start | bytes 2875400 | tf_op jit(solution)/shard_map/ppermute | solution.py:273
  68.8 4.5 %collective-permute-done.6 = bf16[192,1536]{1,0:T(8,128)(2,1)S(1)} collective-permute-done((bf16[192,1536]{1,0:T(8,128)(2,1)S(1)}, bf16[192,1536]{1,0:T(8,128)(2,1)S(1)}, u32[]{:S(2)}, u32[]{:S(2)}) %collective-permute-start.6) | collective-permute-done | bytes 589856 | tf_op jit(solution)/shard_map/ppermute | solution.py:288
  73.3 0.7 slice.32
  74.0 2.9 %collective-permute-start.8 = (bf16[96,1536]{1,0:T(8,128)(2,1)}, bf16[96,1536]{1,0:T(8,128)(2,1)S(1)}, u32[]{:S(2)}, u32[]{:S(2)}) collective-permute-start(bf16[96,1536]{1,0:T(8,128)(2,1)} %slice.32), channel_id=1, source_target_pairs={{0,128},{32,160},{64,192},{96,224},{128,256},{160,288},{192,320},{... | collective-permute-start | bytes 884744 | tf_op jit(solution)/shard_map/ppermute | solution.py:288
  76.9 0.0 collective-permute-done.7
  76.9 1.0 slice.33
  77.9 3.0 %collective-permute-start.9 = (bf16[96,1536]{1,0:T(8,128)(2,1)S(1)}, bf16[96,1536]{1,0:T(8,128)(2,1)S(1)}, u32[]{:S(2)}, u32[]{:S(2)}) collective-permute-start(bf16[96,1536]{1,0:T(8,128)(2,1)S(1)} %slice.33), channel_id=1, source_target_pairs={{0,384},{32,416},{64,448},{96,480},{128,0},{160,32},{192,64},{224,... | collective-permute-start | bytes 884744 | tf_op jit(solution)/shard_map/ppermute | solution.py:288
  80.9 2.4 %pad_maximum_fusion.rest_0_ = bf16[576,1536]{1,0:T(8,128)(2,1)} fusion(bf16[192,1536]{1,0:T(8,128)(2,1)} %collective-permute-done.7, bf16[192,1536]{1,0:T(8,128)(2,1)S(1)} %collective-permute-done.6, bf16[192,1536]{1,0:T(8,128)(2,1)S(1)} %pad_maximum_fusion.3), kind=kLoop, calls=%fused_computation | loop fusion | flops 5308416 | bytes 3538944 | tf_op jit(solution)/shard_map/concatenate | solution.py:298
  83.3 0.0 collective-permute-done.8
  83.3 1.9 %collective-permute-start.10 = (bf16[576,1536]{1,0:T(8,128)(2,1)}, bf16[576,1536]{1,0:T(8,128)(2,1)}, u32[]{:S(2)}, u32[]{:S(2)}) collective-permute-start(bf16[576,1536]{1,0:T(8,128)(2,1)} %pad_maximum_fusion.rest_0_), channel_id=1, source_target_pairs={{0,32},{32,0},{64,96},{96,64},{128,160},{160,128},{192,224},{224,1... | collective-permute-start | bytes 5308424 | tf_op jit(solution)/shard_map/ppermute | solution.py:284
  85.2 0.0 collective-permute-done.4.right
  85.3 1.0 copy-done.9
  86.3 0.0 copy-start.13
  86.3 0.0 copy-start.14
  86.3 0.0 copy-start.8
  86.3 0.0 collective-permute-done.3.left
  86.4 1.0 pad_maximum_fusion.2
  87.4 2.4 %collective-permute-start.5 = (bf16[288,1664]{1,0:T(8,128)(2,1)}, bf16[288,1664]{1,0:T(8,128)(2,1)}, u32[]{:S(2)}, u32[]{:S(2)}) collective-permute-start(bf16[288,1664]{1,0:T(8,128)(2,1)} %pad_maximum_fusion.2), channel_id=1, source_target_pairs={{0,32},{32,0},{64,96},{96,64},{128,160},{160,128},{192,224},{224,1... | collective-permute-start | bytes 2875400 | tf_op jit(solution)/shard_map/ppermute | solution.py:284
  89.8 0.0 collective-permute-done.9
  89.9 1.9 %collective-permute-start.11 = (bf16[192,1536]{1,0:T(8,128)(2,1)S(1)}, bf16[192,1536]{1,0:T(8,128)(2,1)S(1)}, u32[]{:S(2)}, u32[]{:S(2)}) collective-permute-start(bf16[192,1536]{1,0:T(8,128)(2,1)S(1)} %constant_dynamic-update-slice_fusion.rest_1_), channel_id=1, source_target_pairs={{0,32},{32,0},{64,96},{96,64},{128,160},{160,128},{192,224},{224,1... | collective-permute-start | bytes 1769480 | tf_op jit(solution)/shard_map/ppermute | solution.py:284
  91.9 1.9 %collective-permute-done.11.rest_3_ = bf16[192,1536]{1,0:T(8,128)(2,1)S(1)} collective-permute-done((bf16[192,1536]{1,0:T(8,128)(2,1)S(1)}, bf16[192,1536]{1,0:T(8,128)(2,1)S(1)}, u32[]{:S(2)}, u32[]{:S(2)}) %collective-permute-start.11) | collective-permute-done | bytes 589856 | tf_op jit(solution)/shard_map/ppermute | solution.py:284
  93.8 0.0 collective-permute-done.5.shared
  93.8 0.0 collective-permute-done.10.rest_2_
  93.8 15.7 %front.1 = (bf16[1536,1536]{1,0:T(8,128)(2,1)}, bf16[288,384]{1,0:T(8,128)(2,1)S(1)}, bf16[288,384]{1,0:T(8,128)(2,1)S(1)}, bf16[288,128]{1,0:T(8,128)(2,1)S(1)}...) custom-call(s32[2]{0:T(128)S(1)} %pad_add_fusion.place, ...), custom_call_target="tpu_custom_call" | custom-call | tf_op jit(solution)/shard_map/front/pallas_call | solution.py:360
  109.5 2.0 %collective-permute-start.12 = (bf16[288,512]{1,0:T(8,128)(2,1)S(1)}, bf16[288,512]{1,0:T(8,128)(2,1)S(1)}, u32[]{:S(2)}, u32[]{:S(2)}) collective-permute-start(bf16[288,512]{1,0:T(8,128)(2,1)S(1)} %get-tuple-element.44.own), channel_id=1, source_target_pairs={{0,32},{32,64},{64,96},{96,128},{128,160},{160,192},{192,224},{224... | collective-permute-start | bytes 884744 | tf_op jit(solution)/shard_map/ppermute | solution.py:267
  111.6 4.6 %collective-permute-start.13 = (bf16[288,512]{1,0:T(8,128)(2,1)S(1)}, bf16[288,512]{1,0:T(8,128)(2,1)S(1)}, u32[]{:S(2)}, u32[]{:S(2)}) collective-permute-start(bf16[288,512]{1,0:T(8,128)(2,1)S(1)} %get-tuple-element.44.own), channel_id=1, source_target_pairs={{32,0},{64,32},{96,64},{128,96},{160,128},{192,160},{224,192},{256... | collective-permute-start | bytes 884744 | tf_op jit(solution)/shard_map/ppermute | solution.py:268
  116.3 1.6 convolution_convert_fusion
  117.9 0.7 collective-permute-done.12.up
  118.6 1.7 %collective-permute-done.13.down = bf16[288,512]{1,0:T(8,128)(2,1)S(1)} collective-permute-done((bf16[288,512]{1,0:T(8,128)(2,1)S(1)}, bf16[288,512]{1,0:T(8,128)(2,1)S(1)}, u32[]{:S(2)}, u32[]{:S(2)}) %collective-permute-start.13) | collective-permute-done | bytes 294944 | tf_op jit(solution)/shard_map/ppermute | solution.py:268
  120.3 1.3 collective-permute-start.16
  121.7 5.2 %collective-permute-start.15 = (bf16[432,512]{1,0:T(8,128)(2,1)S(1)}, bf16[432,512]{1,0:T(8,128)(2,1)S(1)}, u32[]{:S(2)}, u32[]{:S(2)}) collective-permute-start(bf16[432,512]{1,0:T(8,128)(2,1)S(1)} %pad_maximum_fusion.4), channel_id=1, source_target_pairs={{0,2},{2,4},{4,6},{6,8},{8,10},{10,12},{12,14},{14,16},{16,18},{18... | collective-permute-start | bytes 1327112 | tf_op jit(solution)/shard_map/ppermute | solution.py:273
  126.9 4.7 %collective-permute-start.14 = (bf16[288,768]{1,0:T(8,128)(2,1)S(1)}, bf16[288,768]{1,0:T(8,128)(2,1)S(1)}, u32[]{:S(2)}, u32[]{:S(2)}) collective-permute-start(bf16[288,768]{1,0:T(8,128)(2,1)S(1)} %convolution_convert_fusion), channel_id=1, source_target_pairs={{0,1},{1,0},{2,3},{3,2},{4,5},{5,4},{6,7},{7,6},{8,9},{9,8},{10,11... | collective-permute-start | bytes 1327112 | tf_op jit(solution)/shard_map/ppermute | solution.py:394
  131.6 7.6 %queries.1 = bf16[1728,384]{1,0:T(8,128)(2,1)} custom-call(s32[2]{0:T(128)S(1)} %pad_add_fusion.place, bf16[288,1664]{1,0:T(8,128)(2,1)S(1)} %copy-done.1, bf16[288,1664]{1,0:T(8,128)(2,1)S(1)} %copy-done.3, bf16[288,1664]{1,0:T(8,128)(2,1)S(1)} %copy-done.5, bf16[288,1664]{1,0:T(8,128)(2,1)S(1)} %copy-done.7, bf16[288,1664]{1,0:T(8,128)(2,1)} %copy-done.9, ...), custom_call_target="tpu_custom_call" | custom-call | flops 2038431744 | bytes 8388608 | tf_op jit(solution)/shard_map/queries/pallas_call | solution.py:404
  139.2 0.0 collective-permute-done.16.right
  139.2 0.0 collective-permute-done.15.left
  139.2 8.1 %back.1 = (bf16[288,768]{1,0:T(8,128)(2,1)S(1)}, bf16[288,768]{1,0:T(8,128)(2,1)S(1)}) custom-call(s32[2]{0:T(128)S(1)} %pad_add_fusion.place, bf16[288,512]{1,0:T(8,128)(2,1)S(1)} %get-tuple-element.44.own, bf16[288,512]{1,0:T(8,128)(2,1)S(1)} %collective-permute-done.12.up, bf16[288,512]{1,0:T(8,128)(2,1)S(1)} %collective-permute-done.13.down, ...), custom_call_target="tpu_custom_call" | custom-call | tf_op jit(solution)/shard_map/back/pallas_call | solution.py:419
  147.4 2.6 %collective-permute-start.17 = (bf16[288,768]{1,0:T(8,128)(2,1)S(1)}, bf16[288,768]{1,0:T(8,128)(2,1)S(1)}, u32[]{:S(2)}, u32[]{:S(2)}) collective-permute-start(bf16[288,768]{1,0:T(8,128)(2,1)S(1)} %get-tuple-element.61), channel_id=1, source_target_pairs={{0,1},{1,0},{2,3},{3,2},{4,5},{5,4},{6,7},{7,6},{8,9},{9,8},{10,11... | collective-permute-start | bytes 1327112 | tf_op jit(solution)/shard_map/ppermute | solution.py:394
  150.0 0.0 collective-permute-done.14
  150.0 2.3 %fusion.2 = bf16[288,768]{1,0:T(8,128)(2,1)} fusion(bf16[288,384]{1,0:T(8,128)(2,1)S(1)} %get-tuple-element.42, bf16[288,768]{1,0:T(8,128)(2,1)S(1)} %collective-permute-done.14, bf16[1536,1536]{1,0:T(8,128)(2,1)} %get-tuple-element.43.whole, s32[]{:T(128)S(6)} %select_n.11), kind=kOutput, calls=%fused_computation.5 | convolution fusion | flops 170975232 | bytes 1695748 | tf_op jit(solution)/shard_map/dot_general | solution.py:26
  152.3 11.2 %collective-permute-done.17 = bf16[288,768]{1,0:T(8,128)(2,1)S(1)} collective-permute-done((bf16[288,768]{1,0:T(8,128)(2,1)S(1)}, bf16[288,768]{1,0:T(8,128)(2,1)S(1)}, u32[]{:S(2)}, u32[]{:S(2)}) %collective-permute-start.17) | collective-permute-done | bytes 442400 | tf_op jit(solution)/shard_map/ppermute | solution.py:394
  163.5 0.9 add_convert_fusion
  (33 shorter events, 0.3 us)
Async XLA Ops:
  0.6 8.7 %copy-start.11 = (bf16[6,3,384]{2,1,0:T(4,128)(2,1)S(1)}, bf16[6,3,384]{2,1,0:T(4,128)(2,1)}, u32[]{:S(2)}) copy-start(bf16[6,3,384]{2,1,0:T(4,128)(2,1)} %param.9) | copy-start | bytes 41476
  0.6 8.7 %copy-start.12 = (bf16[6,384]{1,0:T(8,128)(2,1)S(1)}, bf16[6,384]{1,0:T(8,128)(2,1)}, u32[]{:S(2)}) copy-start(bf16[6,384]{1,0:T(8,128)(2,1)} %param.10) | copy-start | bytes 13828
  2.8 50.8 %copy-start = (bf16[288,1664]{1,0:T(8,128)(2,1)}, bf16[288,1664]{1,0:T(8,128)(2,1)S(1)}, u32[]{:S(2)}) copy-start(bf16[288,1664]{1,0:T(8,128)(2,1)S(1)} %pad_maximum_fusion.1.own) | copy-start | bytes 2875396
  2.8 45.2 %collective-permute-start = (bf16[288,1664]{1,0:T(8,128)(2,1)S(1)}, bf16[288,1664]{1,0:T(8,128)(2,1)S(1)}, u32[]{:S(2)}, u32[]{:S(2)}) collective-permute-start(bf16[288,1664]{1,0:T(8,128)(2,1)S(1)} %pad_maximum_fusion.1.own), channel_id=1, source_target_pairs={{0,32},{32,64},{64,96},{96,128},{128,160},{160,192},{192,224},{224... | collective-permute-start | bytes 2875400 | tf_op jit(solution)/shard_map/ppermute | solution.py:267
  4.7 43.3 %collective-permute-start.1 = (bf16[288,1664]{1,0:T(8,128)(2,1)S(1)}, bf16[288,1664]{1,0:T(8,128)(2,1)S(1)}, u32[]{:S(2)}, u32[]{:S(2)}) collective-permute-start(bf16[288,1664]{1,0:T(8,128)(2,1)S(1)} %pad_maximum_fusion.1.own), channel_id=1, source_target_pairs={{32,0},{64,32},{96,64},{128,96},{160,128},{192,160},{224,192},{256... | collective-permute-start | bytes 2875400 | tf_op jit(solution)/shard_map/ppermute | solution.py:268
  48.0 9.0 %copy-start.10 = (bf16[96,1536]{1,0:T(8,128)(2,1)S(1)}, bf16[96,1536]{1,0:T(8,128)(2,1)}, u32[]{:S(2)}) copy-start(bf16[96,1536]{1,0:T(8,128)(2,1)} %reshape.42) | copy-start | bytes 884740
  48.0 9.0 %copy-start.2 = (bf16[288,1664]{1,0:T(8,128)(2,1)}, bf16[288,1664]{1,0:T(8,128)(2,1)S(1)}, u32[]{:S(2)}) copy-start(bf16[288,1664]{1,0:T(8,128)(2,1)S(1)} %collective-permute-done.up) | copy-start | bytes 2875396
  48.0 2.5 %copy-start.4 = (bf16[288,1664]{1,0:T(8,128)(2,1)}, bf16[288,1664]{1,0:T(8,128)(2,1)S(1)}, u32[]{:S(2)}) copy-start(bf16[288,1664]{1,0:T(8,128)(2,1)S(1)} %collective-permute-done.1.down) | copy-start | bytes 2875396
  48.0 9.0 %collective-permute-start.2 = (bf16[96,1536]{1,0:T(8,128)(2,1)}, bf16[96,1536]{1,0:T(8,128)(2,1)S(1)}, u32[]{:S(2)}, u32[]{:S(2)}) collective-permute-start(bf16[96,1536]{1,0:T(8,128)(2,1)} %reshape.42), channel_id=1, source_target_pairs={{0,64},{32,96},{64,0},{96,32},{128,192},{160,224},{192,128},{224,1... | collective-permute-start | bytes 884744 | tf_op jit(solution)/shard_map/ppermute | solution.py:284
  57.1 28.2 %collective-permute-start.4 = (bf16[288,1664]{1,0:T(8,128)(2,1)}, bf16[288,1664]{1,0:T(8,128)(2,1)S(1)}, u32[]{:S(2)}, u32[]{:S(2)}) collective-permute-start(bf16[288,1664]{1,0:T(8,128)(2,1)} %get-tuple-element.38), channel_id=1, source_target_pairs={{2,0},{4,2},{6,4},{8,6},{10,8},{12,10},{14,12},{16,14},{18,16},{20... | collective-permute-start | bytes 2875400 | tf_op jit(solution)/shard_map/ppermute | solution.py:274
  58.4 14.9 %collective-permute-start.6 = (bf16[192,1536]{1,0:T(8,128)(2,1)S(1)}, bf16[192,1536]{1,0:T(8,128)(2,1)S(1)}, u32[]{:S(2)}, u32[]{:S(2)}) collective-permute-start(bf16[192,1536]{1,0:T(8,128)(2,1)S(1)} %pad_maximum_fusion.3), channel_id=1, source_target_pairs={{0,128},{32,160},{64,192},{96,224},{128,256},{160,288},{192,320},{... | collective-permute-start | bytes 1769480 | tf_op jit(solution)/shard_map/ppermute | solution.py:288
  60.3 16.6 %collective-permute-start.7 = (bf16[192,1536]{1,0:T(8,128)(2,1)S(1)}, bf16[192,1536]{1,0:T(8,128)(2,1)}, u32[]{:S(2)}, u32[]{:S(2)}) collective-permute-start(bf16[192,1536]{1,0:T(8,128)(2,1)S(1)} %pad_maximum_fusion.3), channel_id=1, source_target_pairs={{0,384},{32,416},{64,448},{96,480},{128,0},{160,32},{192,64},{224,... | collective-permute-start | bytes 1769480 | tf_op jit(solution)/shard_map/ppermute | solution.py:288
  64.2 22.1 %collective-permute-start.3 = (bf16[288,1664]{1,0:T(8,128)(2,1)}, bf16[288,1664]{1,0:T(8,128)(2,1)S(1)}, u32[]{:S(2)}, u32[]{:S(2)}) collective-permute-start(bf16[288,1664]{1,0:T(8,128)(2,1)} %get-tuple-element.37), channel_id=1, source_target_pairs={{0,2},{2,4},{4,6},{6,8},{8,10},{10,12},{12,14},{14,16},{16,18},{18... | collective-permute-start | bytes 2875400 | tf_op jit(solution)/shard_map/ppermute | solution.py:273
  74.0 9.3 %collective-permute-start.8 = (bf16[96,1536]{1,0:T(8,128)(2,1)}, bf16[96,1536]{1,0:T(8,128)(2,1)S(1)}, u32[]{:S(2)}, u32[]{:S(2)}) collective-permute-start(bf16[96,1536]{1,0:T(8,128)(2,1)} %slice.32), channel_id=1, source_target_pairs={{0,128},{32,160},{64,192},{96,224},{128,256},{160,288},{192,320},{... | collective-permute-start | bytes 884744 | tf_op jit(solution)/shard_map/ppermute | solution.py:288
  77.9 11.9 %collective-permute-start.9 = (bf16[96,1536]{1,0:T(8,128)(2,1)S(1)}, bf16[96,1536]{1,0:T(8,128)(2,1)S(1)}, u32[]{:S(2)}, u32[]{:S(2)}) collective-permute-start(bf16[96,1536]{1,0:T(8,128)(2,1)S(1)} %slice.33), channel_id=1, source_target_pairs={{0,384},{32,416},{64,448},{96,480},{128,0},{160,32},{192,64},{224,... | collective-permute-start | bytes 884744 | tf_op jit(solution)/shard_map/ppermute | solution.py:288
  83.3 10.5 %collective-permute-start.10 = (bf16[576,1536]{1,0:T(8,128)(2,1)}, bf16[576,1536]{1,0:T(8,128)(2,1)}, u32[]{:S(2)}, u32[]{:S(2)}) collective-permute-start(bf16[576,1536]{1,0:T(8,128)(2,1)} %pad_maximum_fusion.rest_0_), channel_id=1, source_target_pairs={{0,32},{32,0},{64,96},{96,64},{128,160},{160,128},{192,224},{224,1... | collective-permute-start | bytes 5308424 | tf_op jit(solution)/shard_map/ppermute | solution.py:284
  85.2 1.0 copy-start.9
  86.3 5.6 %copy-start.13 = (f32[384]{0:T(512)S(1)}, f32[384]{0:T(512)}, u32[]{:S(2)}) copy-start(f32[384]{0:T(512)} %param.11) | copy-start | bytes 4612
  86.3 5.6 %copy-start.14 = (f32[384]{0:T(512)S(1)}, f32[384]{0:T(512)}, u32[]{:S(2)}) copy-start(f32[384]{0:T(512)} %param.12) | copy-start | bytes 4612
  86.3 7.5 %copy-start.8 = (bf16[1,2,144,1536]{3,2,1,0:T(8,128)(2,1)S(1)}, bf16[1,2,144,1536]{3,2,1,0:T(8,128)(2,1)}, u32[]{:S(2)}) copy-start(bf16[1,2,144,1536]{3,2,1,0:T(8,128)(2,1)} %param.8) | copy-start | bytes 2654212
  86.3 3.6 %copy-start.6 = (bf16[288,1664]{1,0:T(8,128)(2,1)}, bf16[288,1664]{1,0:T(8,128)(2,1)S(1)}, u32[]{:S(2)}) copy-start(bf16[288,1664]{1,0:T(8,128)(2,1)S(1)} %collective-permute-done.3.left) | copy-start | bytes 2875396
  87.4 6.4 %collective-permute-start.5 = (bf16[288,1664]{1,0:T(8,128)(2,1)}, bf16[288,1664]{1,0:T(8,128)(2,1)}, u32[]{:S(2)}, u32[]{:S(2)}) collective-permute-start(bf16[288,1664]{1,0:T(8,128)(2,1)} %pad_maximum_fusion.2), channel_id=1, source_target_pairs={{0,32},{32,0},{64,96},{96,64},{128,160},{160,128},{192,224},{224,1... | collective-permute-start | bytes 2875400 | tf_op jit(solution)/shard_map/ppermute | solution.py:284
  89.9 3.9 %collective-permute-start.11 = (bf16[192,1536]{1,0:T(8,128)(2,1)S(1)}, bf16[192,1536]{1,0:T(8,128)(2,1)S(1)}, u32[]{:S(2)}, u32[]{:S(2)}) collective-permute-start(bf16[192,1536]{1,0:T(8,128)(2,1)S(1)} %constant_dynamic-update-slice_fusion.rest_1_), channel_id=1, source_target_pairs={{0,32},{32,0},{64,96},{96,64},{128,160},{160,128},{192,224},{224,1... | collective-permute-start | bytes 1769480 | tf_op jit(solution)/shard_map/ppermute | solution.py:284
  109.5 9.0 %collective-permute-start.12 = (bf16[288,512]{1,0:T(8,128)(2,1)S(1)}, bf16[288,512]{1,0:T(8,128)(2,1)S(1)}, u32[]{:S(2)}, u32[]{:S(2)}) collective-permute-start(bf16[288,512]{1,0:T(8,128)(2,1)S(1)} %get-tuple-element.44.own), channel_id=1, source_target_pairs={{0,32},{32,64},{64,96},{96,128},{128,160},{160,192},{192,224},{224... | collective-permute-start | bytes 884744 | tf_op jit(solution)/shard_map/ppermute | solution.py:267
  111.6 8.6 %collective-permute-start.13 = (bf16[288,512]{1,0:T(8,128)(2,1)S(1)}, bf16[288,512]{1,0:T(8,128)(2,1)S(1)}, u32[]{:S(2)}, u32[]{:S(2)}) collective-permute-start(bf16[288,512]{1,0:T(8,128)(2,1)S(1)} %get-tuple-element.44.own), channel_id=1, source_target_pairs={{32,0},{64,32},{96,64},{128,96},{160,128},{192,160},{224,192},{256... | collective-permute-start | bytes 884744 | tf_op jit(solution)/shard_map/ppermute | solution.py:268
  116.2 15.4 %copy-start.1 = (bf16[288,1664]{1,0:T(8,128)(2,1)S(1)}, bf16[288,1664]{1,0:T(8,128)(2,1)}, u32[]{:S(2)}) copy-start(bf16[288,1664]{1,0:T(8,128)(2,1)} %copy-done) | copy-start | bytes 2875396
  116.2 15.4 %copy-start.3 = (bf16[288,1664]{1,0:T(8,128)(2,1)S(1)}, bf16[288,1664]{1,0:T(8,128)(2,1)}, u32[]{:S(2)}) copy-start(bf16[288,1664]{1,0:T(8,128)(2,1)} %copy-done.2) | copy-start | bytes 2875396
  116.3 15.4 %copy-start.5 = (bf16[288,1664]{1,0:T(8,128)(2,1)S(1)}, bf16[288,1664]{1,0:T(8,128)(2,1)}, u32[]{:S(2)}) copy-start(bf16[288,1664]{1,0:T(8,128)(2,1)} %copy-done.4) | copy-start | bytes 2875396
  116.3 15.4 %copy-start.7 = (bf16[288,1664]{1,0:T(8,128)(2,1)S(1)}, bf16[288,1664]{1,0:T(8,128)(2,1)}, u32[]{:S(2)}) copy-start(bf16[288,1664]{1,0:T(8,128)(2,1)} %copy-done.6) | copy-start | bytes 2875396
  120.3 18.9 %collective-permute-start.16 = (bf16[432,512]{1,0:T(8,128)(2,1)S(1)}, bf16[432,512]{1,0:T(8,128)(2,1)S(1)}, u32[]{:S(2)}, u32[]{:S(2)}) collective-permute-start(bf16[432,512]{1,0:T(8,128)(2,1)S(1)} %pad_maximum_fusion.5), channel_id=1, source_target_pairs={{2,0},{4,2},{6,4},{8,6},{10,8},{12,10},{14,12},{16,14},{18,16},{20... | collective-permute-start | bytes 1327112 | tf_op jit(solution)/shard_map/ppermute | solution.py:274
  121.7 17.6 %collective-permute-start.15 = (bf16[432,512]{1,0:T(8,128)(2,1)S(1)}, bf16[432,512]{1,0:T(8,128)(2,1)S(1)}, u32[]{:S(2)}, u32[]{:S(2)}) collective-permute-start(bf16[432,512]{1,0:T(8,128)(2,1)S(1)} %pad_maximum_fusion.4), channel_id=1, source_target_pairs={{0,2},{2,4},{4,6},{6,8},{8,10},{10,12},{12,14},{14,16},{16,18},{18... | collective-permute-start | bytes 1327112 | tf_op jit(solution)/shard_map/ppermute | solution.py:273
  126.9 23.2 %collective-permute-start.14 = (bf16[288,768]{1,0:T(8,128)(2,1)S(1)}, bf16[288,768]{1,0:T(8,128)(2,1)S(1)}, u32[]{:S(2)}, u32[]{:S(2)}) collective-permute-start(bf16[288,768]{1,0:T(8,128)(2,1)S(1)} %convolution_convert_fusion), channel_id=1, source_target_pairs={{0,1},{1,0},{2,3},{3,2},{4,5},{5,4},{6,7},{7,6},{8,9},{9,8},{10,11... | collective-permute-start | bytes 1327112 | tf_op jit(solution)/shard_map/ppermute | solution.py:394
  147.4 16.1 %collective-permute-start.17 = (bf16[288,768]{1,0:T(8,128)(2,1)S(1)}, bf16[288,768]{1,0:T(8,128)(2,1)S(1)}, u32[]{:S(2)}, u32[]{:S(2)}) collective-permute-start(bf16[288,768]{1,0:T(8,128)(2,1)S(1)} %get-tuple-element.61), channel_id=1, source_target_pairs={{0,1},{1,0},{2,3},{3,2},{4,5},{5,4},{6,7},{7,6},{8,9},{9,8},{10,11... | collective-permute-start | bytes 1327112 | tf_op jit(solution)/shard_map/ppermute | solution.py:394

commit v6 on v5

--- a/solution.py
+++ b/solution.py
@@ -129,7 +129,7 @@
     grad_copy = pltpu.make_async_copy(upstream, grad, grad_sem.at[0])
     token_copies = token_copies_of(lax.rem(here, 2), own, up, down, left, right, shared, tok, token_sems)
     whole_copy = pltpu.make_async_copy(whole, whole_out, whole_sem.at[0])
-    for copy in block_copies + [grad_copy] + token_copies:
+    for copy in block_copies + [grad_copy] + token_copies[3:7] + token_copies[:3] + token_copies[7:]:
         copy.start()
     for copy in block_copies + [grad_copy]:
         copy.wait()
@@ -138,10 +138,9 @@
     heads = range(inner // HEAD_DIM)
     model = whole.shape[0]
     message[:, :inner] = dot_plain(grad[...], whole[:, 3 * inner :]).astype(jnp.bfloat16)
-    for copy in token_copies:
+    for copy in token_copies[3:7]:
         copy.wait()
-    chunk = 2 * TILE
-
+    chunk = 4 * TILE
     for tile, at in enumerate(OWN_TILES):
         mine = slice(tile * TILE, (tile + 1) * TILE)
         own_queries[mine, :] = tok[at * TILE : (at + 1) * TILE, :model]
@@ -151,8 +150,10 @@
         lanes = slice(head * HEAD_DIM, (head + 1) * HEAD_DIM)
         own_queries[:, lanes] = (result[:, lanes] * norm_inverse(result[:, lanes]) * q_gain[:, lanes]).astype(jnp.bfloat16)
 
-    def project(step, carry):
-        rows = pl.ds(pl.multiple_of(step * chunk, chunk), chunk)
+    for step, arrived in ((1, []), (0, token_copies[:3]), (2, token_copies[7:])):
+        for copy in arrived:
+            copy.wait()
+        rows = slice(step * chunk, (step + 1) * chunk)
         result = dot_plain(tok[rows, :model], whole[:, inner : 3 * inner])
         for head in heads:
             lanes = slice(head * HEAD_DIM, (head + 1) * HEAD_DIM)
@@ -163,15 +164,10 @@
         deep = jnp.where(lane_index(chunk) == MASK_LANE, MASK_DEPTH, 0.0)
         marks[rows, :] = (valid * deep - deep + side_marks(step * chunk, chunk)).astype(jnp.bfloat16)
         for tile, at in enumerate(OWN_TILES):
-            offset = at * TILE % chunk
-
-            @pl.when(step == at * TILE // chunk)
-            def keep():
+            if at * TILE // chunk == step:
+                offset = at * TILE % chunk
                 own_k_raw[tile * TILE : (tile + 1) * TILE, :] = result[offset : offset + TILE, :inner]
 
-        return carry
-
-    lax.fori_loop(0, EXTENDED // chunk, project, 0, unroll=True)
     count = own_keys.shape[0]
     lane = lane_index(count)
     stats = jnp.where(lane == MASK_LANE, 1.0, 0.0)
@@ -289,12 +285,12 @@
     rows = block.shape[0]
     pair = jnp.concatenate([block, flip(block, 2)], axis=0)
     pair, first, last = lax.optimization_barrier((pair, *columns(place, up, own, down)))
+    north, south = shift(pair, 4), shift(pair, -4)
+    far, far_beside = shift(north[:rows], 4), shift(south[rows:], -4)
     left, right = spread_width(first, last)
     core = place[0] & 1
     give = lambda part: lax.dynamic_slice(part, ((1 - core) * TILE, 0), (TILE, part.shape[1]))
     shared = flip(jnp.concatenate([give(left), give(right)], axis=0), 1)
-    north, south = shift(pair, 4), shift(pair, -4)
-    far, far_beside = shift(north[:rows], 4), shift(south[rows:], -4)
     near = jnp.concatenate([pair, north, south], axis=0)
     near, far = lax.optimization_barrier((near, far))
     far = jnp.concatenate([far, far_beside], axis=0)

time: 165 us -> 164 us (level)
  transfers between devices with their start and end apart: 18 -> 18, of which waited for: 6 -> 6; matrix products, arithmetic and copies ran while one was open for 6% -> 6% of each run, Pallas kernels for 11% -> 12%
where the time goes in v6:
time: 164 us; the launch traced here: 163 us
  starting transfers between devices  53.1 us (32%)
  blocking collectives  37.9 us (23%)
  Pallas kernels  32.9 us (20%)
  waiting for transfers between devices  23.6 us (14%)
  other arithmetic  6.44 us (4%)
  local copies, waits for them, and re-layouts  3.96 us (2%)
  matrix products  3.88 us (2%)
    all_gather x1, blocking collectives, on_device(): along_width = lax.all_gather(joined, 'width', axis=0, tiled=True)  37.9 us
    pallas_call x1, Pallas kernels, on_device(): pl.pallas_call(front_kernel, out_shape=(shape((model, 4 * inner), half),...  14.2 us
    ppermute x4, starting transfers between devices, gather_height(): shift = lambda x, by: lax.ppermute(x, 'height', steps('height', by, True))  11.7 us
    ppermute x2, waiting for transfers between devices, on_device(): swap = lambda x: lax.ppermute(x, 'head', [(0, 1), (1, 0)])  11.2 us
    ppermute x2, starting transfers between devices, spread_width(): left = lax.ppermute(last, 'width', steps('width', 1))  9.81 us
    ppermute x2, starting transfers between devices, spread_height(): down = lax.ppermute(own, 'height', steps('height', -1))  8.96 us
    ppermute x4, starting transfers between devices, flip(): return lax.ppermute(x, 'height', [(i, i ^ bit) for i in range(count)])  8.62 us
    pallas_call x1, Pallas kernels, on_device(): pl.pallas_call(back_kernel, out_shape=(shape((count, width), half), shape...  8.14 us
  transfers between devices with their start and end apart: 18, of which 6 were waited for; matrix products, arithmetic and copies ran while one was open for 6% of the time, Pallas kernels for 12%

profile of v6, /device:TPU:6, one launch (start us, length us, event | category | flops | bytes accessed | tf_op | source)
XLA Modules:
  0.0 163.0 jit_solution(5081588146078467736)
XLA Ops:
  0.7 0.7 convert_element_type.35
  1.3 0.1 convert_element_type.36
  1.4 0.1 broadcast_in_dim.2
  1.5 1.2 pad_maximum_fusion.1.own
  2.8 1.9 %collective-permute-start = (bf16[288,1664]{1,0:T(8,128)(2,1)S(1)}, bf16[288,1664]{1,0:T(8,128)(2,1)S(1)}, u32[]{:S(2)}, u32[]{:S(2)}) collective-permute-start(bf16[288,1664]{1,0:T(8,128)(2,1)S(1)} %pad_maximum_fusion.1.own), channel_id=1, source_target_pairs={{0,32},{32,64},{64,96},{96,128},{128,160},{160,192},{192,224},{224... | collective-permute-start | bytes 2875400 | tf_op jit(solution)/shard_map/ppermute | solution.py:263
  4.7 4.5 %collective-permute-start.1 = (bf16[288,1664]{1,0:T(8,128)(2,1)S(1)}, bf16[288,1664]{1,0:T(8,128)(2,1)S(1)}, u32[]{:S(2)}, u32[]{:S(2)}) collective-permute-start(bf16[288,1664]{1,0:T(8,128)(2,1)S(1)} %pad_maximum_fusion.1.own), channel_id=1, source_target_pairs={{32,0},{64,32},{96,64},{128,96},{160,128},{192,160},{224,192},{256... | collective-permute-start | bytes 2875400 | tf_op jit(solution)/shard_map/ppermute | solution.py:264
  9.3 0.0 copy-done.12
  9.3 37.9 %all-gather = bf16[16,6,1536]{2,1,0:T(8,128)(2,1)S(1)} all-gather(bf16[1,6,1536]{2,1,0:T(8,128)(2,1)S(1)} %maximum_bitcast_fusion), channel_id=1, replica_groups=mesh['height'=16,'width'=16,'head'=2] {'width'}, dimensions={0}, use_global_device_ids=true | all-gather | bytes 313344 | tf_op jit(solution)/shard_map/all_gather | solution.py:349
  47.2 0.8 reshape.42
  48.0 0.0 collective-permute-done.up
  48.0 0.0 collective-permute-done.1.down
  48.0 0.0 copy-start.4
  48.0 2.4 %collective-permute-start.2 = (bf16[96,1536]{1,0:T(8,128)(2,1)}, bf16[96,1536]{1,0:T(8,128)(2,1)S(1)}, u32[]{:S(2)}, u32[]{:S(2)}) collective-permute-start(bf16[96,1536]{1,0:T(8,128)(2,1)} %reshape.42), channel_id=1, source_target_pairs={{0,64},{32,96},{64,0},{96,32},{128,192},{160,224},{192,128},{224,1... | collective-permute-start | bytes 884744 | tf_op jit(solution)/shard_map/ppermute | solution.py:280
  50.5 0.1 pad_add_fusion.place
  50.5 0.0 copy-done.4
  50.5 3.0 %columns.1 = (bf16[288,1664]{1,0:T(8,128)(2,1)}, bf16[288,1664]{1,0:T(8,128)(2,1)}) custom-call(s32[2]{0:T(128)S(1)} %pad_add_fusion.place, bf16[288,1664]{1,0:T(8,128)(2,1)S(1)} %collective-permute-done.up, bf16[288,1664]{1,0:T(8,128)(2,1)S(1)} %pad_maximum_fusion.1.own, bf16[288,1664]{1,0:T(8,128)(2,1)} %copy-done.4), custom_call_target="tpu_custom_call" | custom-call | tf_op jit(solution)/shard_map/columns/pallas_call | solution.py:324
  53.6 3.4 %collective-permute-done.2 = bf16[96,1536]{1,0:T(8,128)(2,1)S(1)} collective-permute-done((bf16[96,1536]{1,0:T(8,128)(2,1)}, bf16[96,1536]{1,0:T(8,128)(2,1)S(1)}, u32[]{:S(2)}, u32[]{:S(2)}) %collective-permute-start.2) | collective-permute-done | bytes 294944 | tf_op jit(solution)/shard_map/ppermute | solution.py:280
  57.1 0.0 copy-done.2
  57.1 1.3 collective-permute-start.4
  58.4 1.9 %collective-permute-start.6 = (bf16[192,1536]{1,0:T(8,128)(2,1)S(1)}, bf16[192,1536]{1,0:T(8,128)(2,1)S(1)}, u32[]{:S(2)}, u32[]{:S(2)}) collective-permute-start(bf16[192,1536]{1,0:T(8,128)(2,1)S(1)} %pad_maximum_fusion.3), channel_id=1, source_target_pairs={{0,128},{32,160},{64,192},{96,224},{128,256},{160,288},{192,320},{... | collective-permute-start | bytes 1769480 | tf_op jit(solution)/shard_map/ppermute | solution.py:284
  60.3 3.9 %collective-permute-start.7 = (bf16[192,1536]{1,0:T(8,128)(2,1)S(1)}, bf16[192,1536]{1,0:T(8,128)(2,1)}, u32[]{:S(2)}, u32[]{:S(2)}) collective-permute-start(bf16[192,1536]{1,0:T(8,128)(2,1)S(1)} %pad_maximum_fusion.3), channel_id=1, source_target_pairs={{0,384},{32,416},{64,448},{96,480},{128,0},{160,32},{192,64},{224,... | collective-permute-start | bytes 1769480 | tf_op jit(solution)/shard_map/ppermute | solution.py:284
  64.2 4.6 %collective-permute-start.3 = (bf16[288,1664]{1,0:T(8,128)(2,1)}, bf16[288,1664]{1,0:T(8,128)(2,1)S(1)}, u32[]{:S(2)}, u32[]{:S(2)}) collective-permute-start(bf16[288,1664]{1,0:T(8,128)(2,1)} %get-tuple-element.37), channel_id=1, source_target_pairs={{0,2},{2,4},{4,6},{6,8},{8,10},{10,12},{12,14},{14,16},{16,18},{18... | collective-permute-start | bytes 2875400 | tf_op jit(solution)/shard_map/ppermute | solution.py:269
  68.8 4.5 %collective-permute-done.6 = bf16[192,1536]{1,0:T(8,128)(2,1)S(1)} collective-permute-done((bf16[192,1536]{1,0:T(8,128)(2,1)S(1)}, bf16[192,1536]{1,0:T(8,128)(2,1)S(1)}, u32[]{:S(2)}, u32[]{:S(2)}) %collective-permute-start.6) | collective-permute-done | bytes 589856 | tf_op jit(solution)/shard_map/ppermute | solution.py:284
  73.3 0.7 slice.32
  74.0 2.9 %collective-permute-start.8 = (bf16[96,1536]{1,0:T(8,128)(2,1)}, bf16[96,1536]{1,0:T(8,128)(2,1)S(1)}, u32[]{:S(2)}, u32[]{:S(2)}) collective-permute-start(bf16[96,1536]{1,0:T(8,128)(2,1)} %slice.32), channel_id=1, source_target_pairs={{0,128},{32,160},{64,192},{96,224},{128,256},{160,288},{192,320},{... | collective-permute-start | bytes 884744 | tf_op jit(solution)/shard_map/ppermute | solution.py:284
  76.9 0.0 collective-permute-done.7
  76.9 1.0 slice.33
  77.9 3.0 %collective-permute-start.9 = (bf16[96,1536]{1,0:T(8,128)(2,1)S(1)}, bf16[96,1536]{1,0:T(8,128)(2,1)S(1)}, u32[]{:S(2)}, u32[]{:S(2)}) collective-permute-start(bf16[96,1536]{1,0:T(8,128)(2,1)S(1)} %slice.33), channel_id=1, source_target_pairs={{0,384},{32,416},{64,448},{96,480},{128,0},{160,32},{192,64},{224,... | collective-permute-start | bytes 884744 | tf_op jit(solution)/shard_map/ppermute | solution.py:284
  80.9 2.4 %pad_maximum_fusion.rest_0_ = bf16[576,1536]{1,0:T(8,128)(2,1)} fusion(bf16[192,1536]{1,0:T(8,128)(2,1)} %collective-permute-done.7, bf16[192,1536]{1,0:T(8,128)(2,1)S(1)} %collective-permute-done.6, bf16[192,1536]{1,0:T(8,128)(2,1)S(1)} %pad_maximum_fusion.3), kind=kLoop, calls=%fused_computation | loop fusion | flops 5308416 | bytes 3538944 | tf_op jit(solution)/shard_map/concatenate | solution.py:294
  83.3 0.0 collective-permute-done.8
  83.3 1.9 %collective-permute-start.10 = (bf16[576,1536]{1,0:T(8,128)(2,1)}, bf16[576,1536]{1,0:T(8,128)(2,1)}, u32[]{:S(2)}, u32[]{:S(2)}) collective-permute-start(bf16[576,1536]{1,0:T(8,128)(2,1)} %pad_maximum_fusion.rest_0_), channel_id=1, source_target_pairs={{0,32},{32,0},{64,96},{96,64},{128,160},{160,128},{192,224},{224,1... | collective-permute-start | bytes 5308424 | tf_op jit(solution)/shard_map/ppermute | solution.py:280
  85.2 0.0 collective-permute-done.4.right
  85.3 1.0 copy-done.9
  86.3 0.0 copy-start.13
  86.3 0.0 copy-start.14
  86.3 0.0 copy-start.8
  86.3 0.0 collective-permute-done.3.left
  86.4 1.0 pad_maximum_fusion.2
  87.4 2.4 %collective-permute-start.5 = (bf16[288,1664]{1,0:T(8,128)(2,1)}, bf16[288,1664]{1,0:T(8,128)(2,1)}, u32[]{:S(2)}, u32[]{:S(2)}) collective-permute-start(bf16[288,1664]{1,0:T(8,128)(2,1)} %pad_maximum_fusion.2), channel_id=1, source_target_pairs={{0,32},{32,0},{64,96},{96,64},{128,160},{160,128},{192,224},{224,1... | collective-permute-start | bytes 2875400 | tf_op jit(solution)/shard_map/ppermute | solution.py:280
  89.8 0.0 collective-permute-done.9
  89.9 1.9 %collective-permute-start.11 = (bf16[192,1536]{1,0:T(8,128)(2,1)S(1)}, bf16[192,1536]{1,0:T(8,128)(2,1)S(1)}, u32[]{:S(2)}, u32[]{:S(2)}) collective-permute-start(bf16[192,1536]{1,0:T(8,128)(2,1)S(1)} %constant_dynamic-update-slice_fusion.rest_1_), channel_id=1, source_target_pairs={{0,32},{32,0},{64,96},{96,64},{128,160},{160,128},{192,224},{224,1... | collective-permute-start | bytes 1769480 | tf_op jit(solution)/shard_map/ppermute | solution.py:280
  91.8 0.0 copy-done.13
  91.9 1.9 %collective-permute-done.11.rest_3_ = bf16[192,1536]{1,0:T(8,128)(2,1)S(1)} collective-permute-done((bf16[192,1536]{1,0:T(8,128)(2,1)S(1)}, bf16[192,1536]{1,0:T(8,128)(2,1)S(1)}, u32[]{:S(2)}, u32[]{:S(2)}) %collective-permute-start.11) | collective-permute-done | bytes 589856 | tf_op jit(solution)/shard_map/ppermute | solution.py:280
  93.8 0.0 collective-permute-done.5.shared
  93.8 0.0 collective-permute-done.10.rest_2_
  93.8 14.2 %front.1 = (bf16[1536,1536]{1,0:T(8,128)(2,1)}, bf16[288,384]{1,0:T(8,128)(2,1)S(1)}, bf16[288,384]{1,0:T(8,128)(2,1)S(1)}, bf16[288,128]{1,0:T(8,128)(2,1)S(1)}...) custom-call(s32[2]{0:T(128)S(1)} %pad_add_fusion.place, ...), custom_call_target="tpu_custom_call" | custom-call | tf_op jit(solution)/shard_map/front/pallas_call | solution.py:356
  108.0 2.2 %collective-permute-start.12 = (bf16[288,512]{1,0:T(8,128)(2,1)S(1)}, bf16[288,512]{1,0:T(8,128)(2,1)S(1)}, u32[]{:S(2)}, u32[]{:S(2)}) collective-permute-start(bf16[288,512]{1,0:T(8,128)(2,1)S(1)} %get-tuple-element.44.own), channel_id=1, source_target_pairs={{0,32},{32,64},{64,96},{96,128},{128,160},{160,192},{192,224},{224... | collective-permute-start | bytes 884744 | tf_op jit(solution)/shard_map/ppermute | solution.py:263
  110.2 4.4 %collective-permute-start.13 = (bf16[288,512]{1,0:T(8,128)(2,1)S(1)}, bf16[288,512]{1,0:T(8,128)(2,1)S(1)}, u32[]{:S(2)}, u32[]{:S(2)}) collective-permute-start(bf16[288,512]{1,0:T(8,128)(2,1)S(1)} %get-tuple-element.44.own), channel_id=1, source_target_pairs={{32,0},{64,32},{96,64},{128,96},{160,128},{192,160},{224,192},{256... | collective-permute-start | bytes 884744 | tf_op jit(solution)/shard_map/ppermute | solution.py:264
  114.7 1.6 %convolution_convert_fusion = bf16[288,768]{1,0:T(8,128)(2,1)S(1)} fusion(bf16[288,384]{1,0:T(8,128)(2,1)S(1)} %get-tuple-element.42, bf16[1536,1536]{1,0:T(8,128)(2,1)} %get-tuple-element.43.whole, s32[]{:T(128)S(6)} %select_n.12), kind=kOutput, calls=%fused_computation.1 | convolution fusion | flops 170090496 | bytes 1253380 | tf_op jit(solution)/shard_map/dot_general | solution.py:26
  116.4 0.9 collective-permute-done.12.up
  117.2 1.7 %collective-permute-done.13.down = bf16[288,512]{1,0:T(8,128)(2,1)S(1)} collective-permute-done((bf16[288,512]{1,0:T(8,128)(2,1)S(1)}, bf16[288,512]{1,0:T(8,128)(2,1)S(1)}, u32[]{:S(2)}, u32[]{:S(2)}) %collective-permute-start.13) | collective-permute-done | bytes 294944 | tf_op jit(solution)/shard_map/ppermute | solution.py:264
  118.9 1.3 collective-permute-start.16
  120.3 5.2 %collective-permute-start.15 = (bf16[432,512]{1,0:T(8,128)(2,1)S(1)}, bf16[432,512]{1,0:T(8,128)(2,1)S(1)}, u32[]{:S(2)}, u32[]{:S(2)}) collective-permute-start(bf16[432,512]{1,0:T(8,128)(2,1)S(1)} %pad_maximum_fusion.4), channel_id=1, source_target_pairs={{0,2},{2,4},{4,6},{6,8},{8,10},{10,12},{12,14},{14,16},{16,18},{18... | collective-permute-start | bytes 1327112 | tf_op jit(solution)/shard_map/ppermute | solution.py:269
  125.5 4.7 %collective-permute-start.14 = (bf16[288,768]{1,0:T(8,128)(2,1)S(1)}, bf16[288,768]{1,0:T(8,128)(2,1)S(1)}, u32[]{:S(2)}, u32[]{:S(2)}) collective-permute-start(bf16[288,768]{1,0:T(8,128)(2,1)S(1)} %convolution_convert_fusion), channel_id=1, source_target_pairs={{0,1},{1,0},{2,3},{3,2},{4,5},{5,4},{6,7},{7,6},{8,9},{9,8},{10,11... | collective-permute-start | bytes 1327112 | tf_op jit(solution)/shard_map/ppermute | solution.py:390
  130.2 0.0 copy-done.1
  130.3 7.6 %queries.1 = bf16[1728,384]{1,0:T(8,128)(2,1)} custom-call(s32[2]{0:T(128)S(1)} %pad_add_fusion.place, bf16[288,1664]{1,0:T(8,128)(2,1)S(1)} %copy-done.1, bf16[288,1664]{1,0:T(8,128)(2,1)S(1)} %copy-done.3, bf16[288,1664]{1,0:T(8,128)(2,1)S(1)} %copy-done.5, bf16[288,1664]{1,0:T(8,128)(2,1)S(1)} %copy-done.7, bf16[288,1664]{1,0:T(8,128)(2,1)} %copy-done.9, ...), custom_call_target="tpu_custom_call" | custom-call | flops 2038431744 | bytes 8388608 | tf_op jit(solution)/shard_map/queries/pallas_call | solution.py:400
  137.8 0.0 collective-permute-done.16.right
  137.8 0.0 collective-permute-done.15.left
  137.9 8.1 %back.1 = (bf16[288,768]{1,0:T(8,128)(2,1)S(1)}, bf16[288,768]{1,0:T(8,128)(2,1)S(1)}) custom-call(s32[2]{0:T(128)S(1)} %pad_add_fusion.place, bf16[288,512]{1,0:T(8,128)(2,1)S(1)} %get-tuple-element.44.own, bf16[288,512]{1,0:T(8,128)(2,1)S(1)} %collective-permute-done.12.up, bf16[288,512]{1,0:T(8,128)(2,1)S(1)} %collective-permute-done.13.down, ...), custom_call_target="tpu_custom_call" | custom-call | tf_op jit(solution)/shard_map/back/pallas_call | solution.py:415
  146.0 2.6 %collective-permute-start.17 = (bf16[288,768]{1,0:T(8,128)(2,1)S(1)}, bf16[288,768]{1,0:T(8,128)(2,1)S(1)}, u32[]{:S(2)}, u32[]{:S(2)}) collective-permute-start(bf16[288,768]{1,0:T(8,128)(2,1)S(1)} %get-tuple-element.61), channel_id=1, source_target_pairs={{0,1},{1,0},{2,3},{3,2},{4,5},{5,4},{6,7},{7,6},{8,9},{9,8},{10,11... | collective-permute-start | bytes 1327112 | tf_op jit(solution)/shard_map/ppermute | solution.py:390
  148.6 0.0 collective-permute-done.14
  148.6 2.3 %fusion.2 = bf16[288,768]{1,0:T(8,128)(2,1)} fusion(bf16[288,384]{1,0:T(8,128)(2,1)S(1)} %get-tuple-element.42, bf16[288,768]{1,0:T(8,128)(2,1)S(1)} %collective-permute-done.14, bf16[1536,1536]{1,0:T(8,128)(2,1)} %get-tuple-element.43.whole, s32[]{:T(128)S(6)} %select_n.11), kind=kOutput, calls=%fused_computation.5 | convolution fusion | flops 170975232 | bytes 1695748 | tf_op jit(solution)/shard_map/dot_general | solution.py:26
  150.9 11.2 %collective-permute-done.17 = bf16[288,768]{1,0:T(8,128)(2,1)S(1)} collective-permute-done((bf16[288,768]{1,0:T(8,128)(2,1)S(1)}, bf16[288,768]{1,0:T(8,128)(2,1)S(1)}, u32[]{:S(2)}, u32[]{:S(2)}) %collective-permute-start.17) | collective-permute-done | bytes 442400 | tf_op jit(solution)/shard_map/ppermute | solution.py:390
  162.1 0.9 add_convert_fusion
  (33 shorter events, 0.3 us)
Async XLA Ops:
  0.6 8.7 %copy-start.11 = (bf16[6,3,384]{2,1,0:T(4,128)(2,1)S(1)}, bf16[6,3,384]{2,1,0:T(4,128)(2,1)}, u32[]{:S(2)}) copy-start(bf16[6,3,384]{2,1,0:T(4,128)(2,1)} %param.9) | copy-start | bytes 41476
  0.6 8.7 %copy-start.12 = (bf16[6,384]{1,0:T(8,128)(2,1)S(1)}, bf16[6,384]{1,0:T(8,128)(2,1)}, u32[]{:S(2)}) copy-start(bf16[6,384]{1,0:T(8,128)(2,1)} %param.10) | copy-start | bytes 13828
  2.8 50.8 %copy-start = (bf16[288,1664]{1,0:T(8,128)(2,1)}, bf16[288,1664]{1,0:T(8,128)(2,1)S(1)}, u32[]{:S(2)}) copy-start(bf16[288,1664]{1,0:T(8,128)(2,1)S(1)} %pad_maximum_fusion.1.own) | copy-start | bytes 2875396
  2.8 45.2 %collective-permute-start = (bf16[288,1664]{1,0:T(8,128)(2,1)S(1)}, bf16[288,1664]{1,0:T(8,128)(2,1)S(1)}, u32[]{:S(2)}, u32[]{:S(2)}) collective-permute-start(bf16[288,1664]{1,0:T(8,128)(2,1)S(1)} %pad_maximum_fusion.1.own), channel_id=1, source_target_pairs={{0,32},{32,64},{64,96},{96,128},{128,160},{160,192},{192,224},{224... | collective-permute-start | bytes 2875400 | tf_op jit(solution)/shard_map/ppermute | solution.py:263
  4.7 43.3 %collective-permute-start.1 = (bf16[288,1664]{1,0:T(8,128)(2,1)S(1)}, bf16[288,1664]{1,0:T(8,128)(2,1)S(1)}, u32[]{:S(2)}, u32[]{:S(2)}) collective-permute-start(bf16[288,1664]{1,0:T(8,128)(2,1)S(1)} %pad_maximum_fusion.1.own), channel_id=1, source_target_pairs={{32,0},{64,32},{96,64},{128,96},{160,128},{192,160},{224,192},{256... | collective-permute-start | bytes 2875400 | tf_op jit(solution)/shard_map/ppermute | solution.py:264
  48.0 9.0 %copy-start.10 = (bf16[96,1536]{1,0:T(8,128)(2,1)S(1)}, bf16[96,1536]{1,0:T(8,128)(2,1)}, u32[]{:S(2)}) copy-start(bf16[96,1536]{1,0:T(8,128)(2,1)} %reshape.42) | copy-start | bytes 884740
  48.0 9.0 %copy-start.2 = (bf16[288,1664]{1,0:T(8,128)(2,1)}, bf16[288,1664]{1,0:T(8,128)(2,1)S(1)}, u32[]{:S(2)}) copy-start(bf16[288,1664]{1,0:T(8,128)(2,1)S(1)} %collective-permute-done.up) | copy-start | bytes 2875396
  48.0 2.5 %copy-start.4 = (bf16[288,1664]{1,0:T(8,128)(2,1)}, bf16[288,1664]{1,0:T(8,128)(2,1)S(1)}, u32[]{:S(2)}) copy-start(bf16[288,1664]{1,0:T(8,128)(2,1)S(1)} %collective-permute-done.1.down) | copy-start | bytes 2875396
  48.0 9.0 %collective-permute-start.2 = (bf16[96,1536]{1,0:T(8,128)(2,1)}, bf16[96,1536]{1,0:T(8,128)(2,1)S(1)}, u32[]{:S(2)}, u32[]{:S(2)}) collective-permute-start(bf16[96,1536]{1,0:T(8,128)(2,1)} %reshape.42), channel_id=1, source_target_pairs={{0,64},{32,96},{64,0},{96,32},{128,192},{160,224},{192,128},{224,1... | collective-permute-start | bytes 884744 | tf_op jit(solution)/shard_map/ppermute | solution.py:280
  57.1 28.2 %collective-permute-start.4 = (bf16[288,1664]{1,0:T(8,128)(2,1)}, bf16[288,1664]{1,0:T(8,128)(2,1)S(1)}, u32[]{:S(2)}, u32[]{:S(2)}) collective-permute-start(bf16[288,1664]{1,0:T(8,128)(2,1)} %get-tuple-element.38), channel_id=1, source_target_pairs={{2,0},{4,2},{6,4},{8,6},{10,8},{12,10},{14,12},{16,14},{18,16},{20... | collective-permute-start | bytes 2875400 | tf_op jit(solution)/shard_map/ppermute | solution.py:270
  58.4 14.9 %collective-permute-start.6 = (bf16[192,1536]{1,0:T(8,128)(2,1)S(1)}, bf16[192,1536]{1,0:T(8,128)(2,1)S(1)}, u32[]{:S(2)}, u32[]{:S(2)}) collective-permute-start(bf16[192,1536]{1,0:T(8,128)(2,1)S(1)} %pad_maximum_fusion.3), channel_id=1, source_target_pairs={{0,128},{32,160},{64,192},{96,224},{128,256},{160,288},{192,320},{... | collective-permute-start | bytes 1769480 | tf_op jit(solution)/shard_map/ppermute | solution.py:284
  60.3 16.6 %collective-permute-start.7 = (bf16[192,1536]{1,0:T(8,128)(2,1)S(1)}, bf16[192,1536]{1,0:T(8,128)(2,1)}, u32[]{:S(2)}, u32[]{:S(2)}) collective-permute-start(bf16[192,1536]{1,0:T(8,128)(2,1)S(1)} %pad_maximum_fusion.3), channel_id=1, source_target_pairs={{0,384},{32,416},{64,448},{96,480},{128,0},{160,32},{192,64},{224,... | collective-permute-start | bytes 1769480 | tf_op jit(solution)/shard_map/ppermute | solution.py:284
  64.2 22.1 %collective-permute-start.3 = (bf16[288,1664]{1,0:T(8,128)(2,1)}, bf16[288,1664]{1,0:T(8,128)(2,1)S(1)}, u32[]{:S(2)}, u32[]{:S(2)}) collective-permute-start(bf16[288,1664]{1,0:T(8,128)(2,1)} %get-tuple-element.37), channel_id=1, source_target_pairs={{0,2},{2,4},{4,6},{6,8},{8,10},{10,12},{12,14},{14,16},{16,18},{18... | collective-permute-start | bytes 2875400 | tf_op jit(solution)/shard_map/ppermute | solution.py:269
  74.0 9.3 %collective-permute-start.8 = (bf16[96,1536]{1,0:T(8,128)(2,1)}, bf16[96,1536]{1,0:T(8,128)(2,1)S(1)}, u32[]{:S(2)}, u32[]{:S(2)}) collective-permute-start(bf16[96,1536]{1,0:T(8,128)(2,1)} %slice.32), channel_id=1, source_target_pairs={{0,128},{32,160},{64,192},{96,224},{128,256},{160,288},{192,320},{... | collective-permute-start | bytes 884744 | tf_op jit(solution)/shard_map/ppermute | solution.py:284
  77.9 11.9 %collective-permute-start.9 = (bf16[96,1536]{1,0:T(8,128)(2,1)S(1)}, bf16[96,1536]{1,0:T(8,128)(2,1)S(1)}, u32[]{:S(2)}, u32[]{:S(2)}) collective-permute-start(bf16[96,1536]{1,0:T(8,128)(2,1)S(1)} %slice.33), channel_id=1, source_target_pairs={{0,384},{32,416},{64,448},{96,480},{128,0},{160,32},{192,64},{224,... | collective-permute-start | bytes 884744 | tf_op jit(solution)/shard_map/ppermute | solution.py:284
  83.3 10.5 %collective-permute-start.10 = (bf16[576,1536]{1,0:T(8,128)(2,1)}, bf16[576,1536]{1,0:T(8,128)(2,1)}, u32[]{:S(2)}, u32[]{:S(2)}) collective-permute-start(bf16[576,1536]{1,0:T(8,128)(2,1)} %pad_maximum_fusion.rest_0_), channel_id=1, source_target_pairs={{0,32},{32,0},{64,96},{96,64},{128,160},{160,128},{192,224},{224,1... | collective-permute-start | bytes 5308424 | tf_op jit(solution)/shard_map/ppermute | solution.py:280
  85.2 1.0 copy-start.9
  86.3 5.6 %copy-start.13 = (f32[384]{0:T(512)S(1)}, f32[384]{0:T(512)}, u32[]{:S(2)}) copy-start(f32[384]{0:T(512)} %param.11) | copy-start | bytes 4612
  86.3 5.6 %copy-start.14 = (f32[384]{0:T(512)S(1)}, f32[384]{0:T(512)}, u32[]{:S(2)}) copy-start(f32[384]{0:T(512)} %param.12) | copy-start | bytes 4612
  86.3 7.5 %copy-start.8 = (bf16[1,2,144,1536]{3,2,1,0:T(8,128)(2,1)S(1)}, bf16[1,2,144,1536]{3,2,1,0:T(8,128)(2,1)}, u32[]{:S(2)}) copy-start(bf16[1,2,144,1536]{3,2,1,0:T(8,128)(2,1)} %param.8) | copy-start | bytes 2654212
  86.3 3.6 %copy-start.6 = (bf16[288,1664]{1,0:T(8,128)(2,1)}, bf16[288,1664]{1,0:T(8,128)(2,1)S(1)}, u32[]{:S(2)}) copy-start(bf16[288,1664]{1,0:T(8,128)(2,1)S(1)} %collective-permute-done.3.left) | copy-start | bytes 2875396
  87.4 6.4 %collective-permute-start.5 = (bf16[288,1664]{1,0:T(8,128)(2,1)}, bf16[288,1664]{1,0:T(8,128)(2,1)}, u32[]{:S(2)}, u32[]{:S(2)}) collective-permute-start(bf16[288,1664]{1,0:T(8,128)(2,1)} %pad_maximum_fusion.2), channel_id=1, source_target_pairs={{0,32},{32,0},{64,96},{96,64},{128,160},{160,128},{192,224},{224,1... | collective-permute-start | bytes 2875400 | tf_op jit(solution)/shard_map/ppermute | solution.py:280
  89.9 3.9 %collective-permute-start.11 = (bf16[192,1536]{1,0:T(8,128)(2,1)S(1)}, bf16[192,1536]{1,0:T(8,128)(2,1)S(1)}, u32[]{:S(2)}, u32[]{:S(2)}) collective-permute-start(bf16[192,1536]{1,0:T(8,128)(2,1)S(1)} %constant_dynamic-update-slice_fusion.rest_1_), channel_id=1, source_target_pairs={{0,32},{32,0},{64,96},{96,64},{128,160},{160,128},{192,224},{224,1... | collective-permute-start | bytes 1769480 | tf_op jit(solution)/shard_map/ppermute | solution.py:280
  108.0 9.2 %collective-permute-start.12 = (bf16[288,512]{1,0:T(8,128)(2,1)S(1)}, bf16[288,512]{1,0:T(8,128)(2,1)S(1)}, u32[]{:S(2)}, u32[]{:S(2)}) collective-permute-start(bf16[288,512]{1,0:T(8,128)(2,1)S(1)} %get-tuple-element.44.own), channel_id=1, source_target_pairs={{0,32},{32,64},{64,96},{96,128},{128,160},{160,192},{192,224},{224... | collective-permute-start | bytes 884744 | tf_op jit(solution)/shard_map/ppermute | solution.py:263
  110.2 8.6 %collective-permute-start.13 = (bf16[288,512]{1,0:T(8,128)(2,1)S(1)}, bf16[288,512]{1,0:T(8,128)(2,1)S(1)}, u32[]{:S(2)}, u32[]{:S(2)}) collective-permute-start(bf16[288,512]{1,0:T(8,128)(2,1)S(1)} %get-tuple-element.44.own), channel_id=1, source_target_pairs={{32,0},{64,32},{96,64},{128,96},{160,128},{192,160},{224,192},{256... | collective-permute-start | bytes 884744 | tf_op jit(solution)/shard_map/ppermute | solution.py:264
  114.7 15.5 %copy-start.1 = (bf16[288,1664]{1,0:T(8,128)(2,1)S(1)}, bf16[288,1664]{1,0:T(8,128)(2,1)}, u32[]{:S(2)}) copy-start(bf16[288,1664]{1,0:T(8,128)(2,1)} %copy-done) | copy-start | bytes 2875396
  114.7 15.5 %copy-start.3 = (bf16[288,1664]{1,0:T(8,128)(2,1)S(1)}, bf16[288,1664]{1,0:T(8,128)(2,1)}, u32[]{:S(2)}) copy-start(bf16[288,1664]{1,0:T(8,128)(2,1)} %copy-done.2) | copy-start | bytes 2875396
  114.7 15.5 %copy-start.5 = (bf16[288,1664]{1,0:T(8,128)(2,1)S(1)}, bf16[288,1664]{1,0:T(8,128)(2,1)}, u32[]{:S(2)}) copy-start(bf16[288,1664]{1,0:T(8,128)(2,1)} %copy-done.4) | copy-start | bytes 2875396
  114.7 15.5 %copy-start.7 = (bf16[288,1664]{1,0:T(8,128)(2,1)S(1)}, bf16[288,1664]{1,0:T(8,128)(2,1)}, u32[]{:S(2)}) copy-start(bf16[288,1664]{1,0:T(8,128)(2,1)} %copy-done.6) | copy-start | bytes 2875396
  118.9 18.9 %collective-permute-start.16 = (bf16[432,512]{1,0:T(8,128)(2,1)S(1)}, bf16[432,512]{1,0:T(8,128)(2,1)S(1)}, u32[]{:S(2)}, u32[]{:S(2)}) collective-permute-start(bf16[432,512]{1,0:T(8,128)(2,1)S(1)} %pad_maximum_fusion.5), channel_id=1, source_target_pairs={{2,0},{4,2},{6,4},{8,6},{10,8},{12,10},{14,12},{16,14},{18,16},{20... | collective-permute-start | bytes 1327112 | tf_op jit(solution)/shard_map/ppermute | solution.py:270
  120.3 17.6 %collective-permute-start.15 = (bf16[432,512]{1,0:T(8,128)(2,1)S(1)}, bf16[432,512]{1,0:T(8,128)(2,1)S(1)}, u32[]{:S(2)}, u32[]{:S(2)}) collective-permute-start(bf16[432,512]{1,0:T(8,128)(2,1)S(1)} %pad_maximum_fusion.4), channel_id=1, source_target_pairs={{0,2},{2,4},{4,6},{6,8},{8,10},{10,12},{12,14},{14,16},{16,18},{18... | collective-permute-start | bytes 1327112 | tf_op jit(solution)/shard_map/ppermute | solution.py:269
  125.5 23.1 %collective-permute-start.14 = (bf16[288,768]{1,0:T(8,128)(2,1)S(1)}, bf16[288,768]{1,0:T(8,128)(2,1)S(1)}, u32[]{:S(2)}, u32[]{:S(2)}) collective-permute-start(bf16[288,768]{1,0:T(8,128)(2,1)S(1)} %convolution_convert_fusion), channel_id=1, source_target_pairs={{0,1},{1,0},{2,3},{3,2},{4,5},{5,4},{6,7},{7,6},{8,9},{9,8},{10,11... | collective-permute-start | bytes 1327112 | tf_op jit(solution)/shard_map/ppermute | solution.py:390
  146.0 16.1 %collective-permute-start.17 = (bf16[288,768]{1,0:T(8,128)(2,1)S(1)}, bf16[288,768]{1,0:T(8,128)(2,1)S(1)}, u32[]{:S(2)}, u32[]{:S(2)}) collective-permute-start(bf16[288,768]{1,0:T(8,128)(2,1)S(1)} %get-tuple-element.61), channel_id=1, source_target_pairs={{0,1},{1,0},{2,3},{3,2},{4,5},{5,4},{6,7},{7,6},{8,9},{9,8},{10,11... | collective-permute-start | bytes 1327112 | tf_op jit(solution)/shard_map/ppermute | solution.py:390

commit v7 on v6

--- a/solution.py
+++ b/solution.py
@@ -220,10 +220,12 @@
 
 
 def back_kernel(place, own, up, down, left, right, queries, keys, values, marks, k_raw, grad_q, whole, k_gain,
-                kept, sent, ext, grad_qkv, weight, sems, weight_sem):
+                grad_qkv, sent, ext, weight, sems, weight_sem):
     inner = queries.shape[1]
     copies = extended_copies(own, up, down, left, right, ext, sems)
-    weight_copy = pltpu.make_async_copy(whole.at[:, pl.ds(0, 3 * inner)], weight, weight_sem.at[0])
+    half = sent.shape[1]
+    other = pl.ds(pl.multiple_of((1 - place[1]) * half, half), half)
+    weight_copy = pltpu.make_async_copy(whole.at[other, pl.ds(0, 3 * inner)], weight, weight_sem.at[0])
     for copy in copies + [weight_copy]:
         copy.start()
     for copy in copies:
@@ -248,10 +250,7 @@
         grad_qkv[:, inner + head * HEAD_DIM : inner + (head + 1) * HEAD_DIM] = grad_k.astype(jnp.bfloat16)
         grad_qkv[:, 2 * inner + head * HEAD_DIM : 2 * inner + (head + 1) * HEAD_DIM] = grad_v.astype(jnp.bfloat16)
     weight_copy.wait()
-    half = kept.shape[1]
-    for target, group in ((sent, 1 - place[1]), (kept, place[1])):
-        rows = pl.ds(pl.multiple_of(group * half, half), half)
-        target[...] = dot_rows(grad_qkv[...], weight[rows, :]).astype(jnp.bfloat16)
+    sent[...] = dot_rows(grad_qkv[...], weight[...]).astype(jnp.bfloat16)
 
 
 def steps(axis, shift, wrap=False):
@@ -412,15 +411,14 @@
         cost_estimate=pl.CostEstimate(flops=2 * EXTENDED * model * inner, bytes_accessed=8 * 2**20, transcendentals=0),
         name="queries",
     )(place, *beyond, whole, q_gains)
-    kept, sent = pl.pallas_call(
+    grad_qkv, sent = pl.pallas_call(
         back_kernel,
-        out_shape=(shape((count, width), half), shape((count, width), half)),
+        out_shape=(shape((count, 3 * inner), half), shape((count, width), half)),
         in_specs=[pl.BlockSpec(memory_space=pltpu.SMEM)] + [anywhere] * 5 + [whole_spec()] * 6 + [anywhere, whole_spec()],
         out_specs=(whole_spec(), whole_spec()),
         scratch_shapes=[
             pltpu.VMEM((EXTENDED, inner + LANES), half),
-            pltpu.VMEM((count, 3 * inner), half),
-            pltpu.VMEM((model, 3 * inner), half),
+            pltpu.VMEM((width, 3 * inner), half),
             pltpu.SemaphoreType.DMA((8,)),
             pltpu.SemaphoreType.DMA((1,)),
         ],
@@ -429,6 +427,8 @@
     )(place, message, up, down, left, right, queries, keys, values, marks, k_raw, grad_q, whole, k_gains)
     total = lambda a, b: (a.astype(jnp.float32) + b.astype(jnp.float32)).astype(half)
     mixed = total(mixed_kept, mixed_got)
+    own_rows = lax.dynamic_slice(whole, (group * width, 0), (width, 3 * inner))
+    kept = lax.optimization_barrier(dot_rows(grad_qkv, own_rows).astype(half))
     grad_in = total(kept, swap(sent))
     out_shape = tokens.shape[:3] + (width,)
     return (mixed.reshape(out_shape), grad_in.reshape(out_shape))

time: 164 us -> 171 us (1.043)
  local copies, waits for them, and re-layouts: 3.96 us -> 8.61 us
    unnamed x32 -> x62, local copies, waits for them, and re-layouts: 1.07 us -> 5.71 us
    dot_general x2 -> x3, matrix products: 3.88 us -> 4.37 us  [dot_rows(): lax.dot_general(left, right, (((1,), (1,)), ((), ())), preferred_element_...]
  transfers between devices with their start and end apart: 18 -> 18, of which waited for: 6 -> 6; matrix products, arithmetic and copies ran while one was open for 6% -> 7% of each run, Pallas kernels for 12% -> 11%
where the time goes in v7:
time: 171 us
  starting transfers between devices  54.1 us (32%)
  blocking collectives  37.9 us (22%)
  Pallas kernels  33.5 us (20%)
  waiting for transfers between devices  22.7 us (13%)
  local copies, waits for them, and re-layouts  8.61 us (5%)
  other arithmetic  8.04 us (5%)
  matrix products  4.37 us (3%)
    all_gather x1, blocking collectives, on_device(): along_width = lax.all_gather(joined, 'width', axis=0, tiled=True)  37.9 us
    pallas_call x1, Pallas kernels, on_device(): pl.pallas_call(front_kernel, out_shape=(shape((model, 4 * inner), half),...  14.2 us
    ppermute x4, starting transfers between devices, gather_height(): shift = lambda x, by: lax.ppermute(x, 'height', steps('height', by, True))  11.7 us
    ppermute x2, waiting for transfers between devices, on_device(): swap = lambda x: lax.ppermute(x, 'head', [(0, 1), (1, 0)])  11.4 us
    ppermute x2, starting transfers between devices, spread_width(): left = lax.ppermute(last, 'width', steps('width', 1))  10.6 us
    ppermute x2, starting transfers between devices, spread_height(): down = lax.ppermute(own, 'height', steps('height', -1))  8.95 us
    ppermute x4, starting transfers between devices, flip(): return lax.ppermute(x, 'height', [(i, i ^ bit) for i in range(count)])  8.8 us
    pallas_call x1, Pallas kernels, on_device(): pl.pallas_call(back_kernel, out_shape=(shape((count, 3 * inner), half), s...  8.68 us
  transfers between devices with their start and end apart: 18, of which 6 were waited for; matrix products, arithmetic and copies ran while one was open for 7% of the time, Pallas kernels for 11%

profile of v7, /device:TPU:6, one launch (start us, length us, event | category | flops | bytes accessed | tf_op | source)
XLA Modules:
  0.0 170.5 jit_solution(11497748652140887995)
XLA Ops:
  0.7 0.7 convert_element_type.38
  1.3 0.1 convert_element_type.39
  1.4 0.1 broadcast_in_dim.2
  1.5 1.2 pad_maximum_fusion.1.own
  2.8 1.9 %collective-permute-start = (bf16[288,1664]{1,0:T(8,128)(2,1)S(1)}, bf16[288,1664]{1,0:T(8,128)(2,1)S(1)}, u32[]{:S(2)}, u32[]{:S(2)}) collective-permute-start(bf16[288,1664]{1,0:T(8,128)(2,1)S(1)} %pad_maximum_fusion.1.own), channel_id=1, source_target_pairs={{0,32},{32,64},{64,96},{96,128},{128,160},{160,192},{192,224},{224... | collective-permute-start | bytes 2875400 | tf_op jit(solution)/shard_map/ppermute | solution.py:262
  4.7 4.5 %collective-permute-start.1 = (bf16[288,1664]{1,0:T(8,128)(2,1)S(1)}, bf16[288,1664]{1,0:T(8,128)(2,1)S(1)}, u32[]{:S(2)}, u32[]{:S(2)}) collective-permute-start(bf16[288,1664]{1,0:T(8,128)(2,1)S(1)} %pad_maximum_fusion.1.own), channel_id=1, source_target_pairs={{32,0},{64,32},{96,64},{128,96},{160,128},{192,160},{224,192},{256... | collective-permute-start | bytes 2875400 | tf_op jit(solution)/shard_map/ppermute | solution.py:263
  9.3 37.9 %all-gather = bf16[16,6,1536]{2,1,0:T(8,128)(2,1)S(1)} all-gather(bf16[1,6,1536]{2,1,0:T(8,128)(2,1)S(1)} %maximum_bitcast_fusion), channel_id=1, replica_groups=mesh['height'=16,'width'=16,'head'=2] {'width'}, dimensions={0}, use_global_device_ids=true | all-gather | bytes 313344 | tf_op jit(solution)/shard_map/all_gather | solution.py:348
  47.2 0.8 reshape.42
  48.0 0.0 collective-permute-done.up
  48.0 0.0 collective-permute-done.1.down
  48.0 2.4 %collective-permute-start.2 = (bf16[96,1536]{1,0:T(8,128)(2,1)}, bf16[96,1536]{1,0:T(8,128)(2,1)S(1)}, u32[]{:S(2)}, u32[]{:S(2)}) collective-permute-start(bf16[96,1536]{1,0:T(8,128)(2,1)} %reshape.42), channel_id=1, source_target_pairs={{0,64},{32,96},{64,0},{96,32},{128,192},{160,224},{192,128},{224,1... | collective-permute-start | bytes 884744 | tf_op jit(solution)/shard_map/ppermute | solution.py:279
  50.5 0.1 pad_add_fusion.place
  50.5 3.1 %columns.1 = (bf16[288,1664]{1,0:T(8,128)(2,1)}, bf16[288,1664]{1,0:T(8,128)(2,1)}) custom-call(s32[2]{0:T(128)S(1)} %pad_add_fusion.place, bf16[288,1664]{1,0:T(8,128)(2,1)S(1)} %collective-permute-done.up, bf16[288,1664]{1,0:T(8,128)(2,1)S(1)} %pad_maximum_fusion.1.own, bf16[288,1664]{1,0:T(8,128)(2,1)} %copy-done.4), custom_call_target="tpu_custom_call" | custom-call | tf_op jit(solution)/shard_map/columns/pallas_call | solution.py:323
  53.6 3.4 %collective-permute-done.2 = bf16[96,1536]{1,0:T(8,128)(2,1)S(1)} collective-permute-done((bf16[96,1536]{1,0:T(8,128)(2,1)}, bf16[96,1536]{1,0:T(8,128)(2,1)S(1)}, u32[]{:S(2)}, u32[]{:S(2)}) %collective-permute-start.2) | collective-permute-done | bytes 294944 | tf_op jit(solution)/shard_map/ppermute | solution.py:279
  57.1 1.3 collective-permute-start.4
  58.4 1.9 %collective-permute-start.6 = (bf16[192,1536]{1,0:T(8,128)(2,1)S(1)}, bf16[192,1536]{1,0:T(8,128)(2,1)S(1)}, u32[]{:S(2)}, u32[]{:S(2)}) collective-permute-start(bf16[192,1536]{1,0:T(8,128)(2,1)S(1)} %pad_maximum_fusion.3), channel_id=1, source_target_pairs={{0,128},{32,160},{64,192},{96,224},{128,256},{160,288},{192,320},{... | collective-permute-start | bytes 1769480 | tf_op jit(solution)/shard_map/ppermute | solution.py:283
  60.3 3.9 %collective-permute-start.7 = (bf16[192,1536]{1,0:T(8,128)(2,1)S(1)}, bf16[192,1536]{1,0:T(8,128)(2,1)}, u32[]{:S(2)}, u32[]{:S(2)}) collective-permute-start(bf16[192,1536]{1,0:T(8,128)(2,1)S(1)} %pad_maximum_fusion.3), channel_id=1, source_target_pairs={{0,384},{32,416},{64,448},{96,480},{128,0},{160,32},{192,64},{224,... | collective-permute-start | bytes 1769480 | tf_op jit(solution)/shard_map/ppermute | solution.py:283
  64.2 4.6 %collective-permute-start.3 = (bf16[288,1664]{1,0:T(8,128)(2,1)}, bf16[288,1664]{1,0:T(8,128)(2,1)S(1)}, u32[]{:S(2)}, u32[]{:S(2)}) collective-permute-start(bf16[288,1664]{1,0:T(8,128)(2,1)} %get-tuple-element.37), channel_id=1, source_target_pairs={{0,2},{2,4},{4,6},{6,8},{8,10},{10,12},{12,14},{14,16},{16,18},{18... | collective-permute-start | bytes 2875400 | tf_op jit(solution)/shard_map/ppermute | solution.py:268
  68.8 4.5 %collective-permute-done.6 = bf16[192,1536]{1,0:T(8,128)(2,1)S(1)} collective-permute-done((bf16[192,1536]{1,0:T(8,128)(2,1)S(1)}, bf16[192,1536]{1,0:T(8,128)(2,1)S(1)}, u32[]{:S(2)}, u32[]{:S(2)}) %collective-permute-start.6) | collective-permute-done | bytes 589856 | tf_op jit(solution)/shard_map/ppermute | solution.py:283
  73.3 0.7 slice.32
  74.0 2.9 %collective-permute-start.8 = (bf16[96,1536]{1,0:T(8,128)(2,1)}, bf16[96,1536]{1,0:T(8,128)(2,1)S(1)}, u32[]{:S(2)}, u32[]{:S(2)}) collective-permute-start(bf16[96,1536]{1,0:T(8,128)(2,1)} %slice.32), channel_id=1, source_target_pairs={{0,128},{32,160},{64,192},{96,224},{128,256},{160,288},{192,320},{... | collective-permute-start | bytes 884744 | tf_op jit(solution)/shard_map/ppermute | solution.py:283
  76.9 0.0 collective-permute-done.7
  76.9 1.0 slice.33
  77.9 3.0 %collective-permute-start.9 = (bf16[96,1536]{1,0:T(8,128)(2,1)S(1)}, bf16[96,1536]{1,0:T(8,128)(2,1)S(1)}, u32[]{:S(2)}, u32[]{:S(2)}) collective-permute-start(bf16[96,1536]{1,0:T(8,128)(2,1)S(1)} %slice.33), channel_id=1, source_target_pairs={{0,384},{32,416},{64,448},{96,480},{128,0},{160,32},{192,64},{224,... | collective-permute-start | bytes 884744 | tf_op jit(solution)/shard_map/ppermute | solution.py:283
  80.9 2.5 %pad_maximum_fusion.rest_0_ = bf16[576,1536]{1,0:T(8,128)(2,1)} fusion(bf16[192,1536]{1,0:T(8,128)(2,1)} %collective-permute-done.7, bf16[192,1536]{1,0:T(8,128)(2,1)S(1)} %collective-permute-done.6, bf16[192,1536]{1,0:T(8,128)(2,1)S(1)} %pad_maximum_fusion.3), kind=kLoop, calls=%fused_computation | loop fusion | flops 5308416 | bytes 3538944 | tf_op jit(solution)/shard_map/concatenate | solution.py:293
  83.4 0.0 collective-permute-done.8
  83.4 1.9 %collective-permute-start.10 = (bf16[576,1536]{1,0:T(8,128)(2,1)}, bf16[576,1536]{1,0:T(8,128)(2,1)}, u32[]{:S(2)}, u32[]{:S(2)}) collective-permute-start(bf16[576,1536]{1,0:T(8,128)(2,1)} %pad_maximum_fusion.rest_0_), channel_id=1, source_target_pairs={{0,32},{32,0},{64,96},{96,64},{128,160},{160,128},{192,224},{224,1... | collective-permute-start | bytes 5308424 | tf_op jit(solution)/shard_map/ppermute | solution.py:279
  85.3 0.0 collective-permute-done.4.right
  85.3 1.0 copy-done.24
  86.4 0.0 copy-start.28
  86.4 0.0 copy-start.29
  86.4 0.0 copy-start.10
  86.5 1.0 pad_maximum_fusion.2
  87.5 2.4 %collective-permute-start.5 = (bf16[288,1664]{1,0:T(8,128)(2,1)}, bf16[288,1664]{1,0:T(8,128)(2,1)}, u32[]{:S(2)}, u32[]{:S(2)}) collective-permute-start(bf16[288,1664]{1,0:T(8,128)(2,1)} %pad_maximum_fusion.2), channel_id=1, source_target_pairs={{0,32},{32,0},{64,96},{96,64},{128,160},{160,128},{192,224},{224,1... | collective-permute-start | bytes 2875400 | tf_op jit(solution)/shard_map/ppermute | solution.py:279
  89.9 0.0 collective-permute-done.9
  90.0 2.1 %collective-permute-start.11 = (bf16[192,1536]{1,0:T(8,128)(2,1)S(1)}, bf16[192,1536]{1,0:T(8,128)(2,1)S(1)}, u32[]{:S(2)}, u32[]{:S(2)}) collective-permute-start(bf16[192,1536]{1,0:T(8,128)(2,1)S(1)} %constant_dynamic-update-slice_fusion.rest_1_), channel_id=1, source_target_pairs={{0,32},{32,0},{64,96},{96,64},{128,160},{160,128},{192,224},{224,1... | collective-permute-start | bytes 1769480 | tf_op jit(solution)/shard_map/ppermute | solution.py:279
  92.1 1.7 %collective-permute-done.11.rest_3_ = bf16[192,1536]{1,0:T(8,128)(2,1)S(1)} collective-permute-done((bf16[192,1536]{1,0:T(8,128)(2,1)S(1)}, bf16[192,1536]{1,0:T(8,128)(2,1)S(1)}, u32[]{:S(2)}, u32[]{:S(2)}) %collective-permute-start.11) | collective-permute-done | bytes 589856 | tf_op jit(solution)/shard_map/ppermute | solution.py:279
  93.9 0.8 copy-done.13
  94.7 0.0 collective-permute-done.5.shared
  94.7 0.0 collective-permute-done.10.rest_2_
  94.7 1.1 copy-done.14
  95.8 14.2 %front.1 = (bf16[1536,1536]{1,0:T(8,128)(2,1)}, bf16[288,384]{1,0:T(8,128)(2,1)S(1)}, bf16[288,384]{1,0:T(8,128)(2,1)S(1)}, bf16[288,128]{1,0:T(8,128)(2,1)S(1)}...) custom-call(s32[2]{0:T(128)S(1)} %pad_add_fusion.place, ...), custom_call_target="tpu_custom_call" | custom-call | tf_op jit(solution)/shard_map/front/pallas_call | solution.py:355
  110.0 0.7 copy-done.21
  110.6 2.0 %collective-permute-start.12 = (bf16[288,512]{1,0:T(8,128)(2,1)S(1)}, bf16[288,512]{1,0:T(8,128)(2,1)S(1)}, u32[]{:S(2)}, u32[]{:S(2)}) collective-permute-start(bf16[288,512]{1,0:T(8,128)(2,1)S(1)} %get-tuple-element.44.own), channel_id=1, source_target_pairs={{0,32},{32,64},{64,96},{96,128},{128,160},{160,192},{192,224},{224... | collective-permute-start | bytes 884744 | tf_op jit(solution)/shard_map/ppermute | solution.py:262
  112.7 4.4 %collective-permute-start.13 = (bf16[288,512]{1,0:T(8,128)(2,1)S(1)}, bf16[288,512]{1,0:T(8,128)(2,1)S(1)}, u32[]{:S(2)}, u32[]{:S(2)}) collective-permute-start(bf16[288,512]{1,0:T(8,128)(2,1)S(1)} %get-tuple-element.44.own), channel_id=1, source_target_pairs={{32,0},{64,32},{96,64},{128,96},{160,128},{192,160},{224,192},{256... | collective-permute-start | bytes 884744 | tf_op jit(solution)/shard_map/ppermute | solution.py:263
  117.2 2.4 %convolution_convert_fusion = bf16[288,768]{1,0:T(8,128)(2,1)} fusion(bf16[288,384]{1,0:T(8,128)(2,1)S(1)} %get-tuple-element.42, bf16[1536,1536]{1,0:T(8,128)(2,1)} %get-tuple-element.43.whole, s32[]{:T(128)S(6)} %select_n.13), kind=kOutput, calls=%fused_computation.4 | convolution fusion | flops 170090496 | bytes 1253380 | tf_op jit(solution)/shard_map/dot_general | solution.py:26
  119.6 0.1 collective-permute-done.12.up
  119.7 1.7 collective-permute-done.13.down
  121.4 0.7 copy-done.8
  122.1 0.8 pad_maximum_fusion.5
  122.9 1.3 collective-permute-start.16
  124.2 0.8 pad_maximum_fusion.4
  125.0 6.0 %collective-permute-start.15 = (bf16[432,512]{1,0:T(8,128)(2,1)}, bf16[432,512]{1,0:T(8,128)(2,1)}, u32[]{:S(2)}, u32[]{:S(2)}) collective-permute-start(bf16[432,512]{1,0:T(8,128)(2,1)} %pad_maximum_fusion.4), channel_id=1, source_target_pairs={{0,2},{2,4},{4,6},{6,8},{8,10},{10,12},{12,14},{14,16},{16,18},{18... | collective-permute-start | bytes 1327112 | tf_op jit(solution)/shard_map/ppermute | solution.py:268
  131.0 4.9 %collective-permute-start.14 = (bf16[288,768]{1,0:T(8,128)(2,1)}, bf16[288,768]{1,0:T(8,128)(2,1)S(1)}, u32[]{:S(2)}, u32[]{:S(2)}) collective-permute-start(bf16[288,768]{1,0:T(8,128)(2,1)} %convolution_convert_fusion), channel_id=1, source_target_pairs={{0,1},{1,0},{2,3},{3,2},{4,5},{5,4},{6,7},{7,6},{8,9},{9,8},{10,11... | collective-permute-start | bytes 1327112 | tf_op jit(solution)/shard_map/ppermute | solution.py:389
  135.9 1.2 copy-done.7
  137.2 7.6 %queries.1 = bf16[1728,384]{1,0:T(8,128)(2,1)} custom-call(s32[2]{0:T(128)S(1)} %pad_add_fusion.place, bf16[288,1664]{1,0:T(8,128)(2,1)S(1)} %copy-done.1, bf16[288,1664]{1,0:T(8,128)(2,1)S(1)} %copy-done.3, bf16[288,1664]{1,0:T(8,128)(2,1)S(1)} %copy-done.5, bf16[288,1664]{1,0:T(8,128)(2,1)S(1)} %copy-done.7, bf16[288,1664]{1,0:T(8,128)(2,1)} %copy-done.24, ...), custom_call_target="tpu_custom_call" | custom-call | flops 2038431744 | bytes 8388608 | tf_op jit(solution)/shard_map/queries/pallas_call | solution.py:399
  144.7 0.0 collective-permute-done.16.right
  144.8 8.7 %back.1 = (bf16[288,1152]{1,0:T(8,128)(2,1)S(1)}, bf16[288,768]{1,0:T(8,128)(2,1)S(1)}) custom-call(s32[2]{0:T(128)S(1)} %pad_add_fusion.place, bf16[288,512]{1,0:T(8,128)(2,1)S(1)} %get-tuple-element.44.own, bf16[288,512]{1,0:T(8,128)(2,1)S(1)} %collective-permute-done.12.up, bf16[288,512]{1,0:T(8,128)(2,1)S(1)} %copy-done.9, ...), custom_call_target="tpu_custom_call" | custom-call | tf_op jit(solution)/shard_map/back/pallas_call | solution.py:414
  153.5 2.6 %collective-permute-start.17 = (bf16[288,768]{1,0:T(8,128)(2,1)S(1)}, bf16[288,768]{1,0:T(8,128)(2,1)S(1)}, u32[]{:S(2)}, u32[]{:S(2)}) collective-permute-start(bf16[288,768]{1,0:T(8,128)(2,1)S(1)} %get-tuple-element.61), channel_id=1, source_target_pairs={{0,1},{1,0},{2,3},{3,2},{4,5},{5,4},{6,7},{7,6},{8,9},{9,8},{10,11... | collective-permute-start | bytes 1327112 | tf_op jit(solution)/shard_map/ppermute | solution.py:389
  156.2 0.8 fusion.2
  157.0 0.1 copy-done.12
  157.1 1.2 fusion.7
  158.3 11.4 %collective-permute-done.17 = bf16[288,768]{1,0:T(8,128)(2,1)S(1)} collective-permute-done((bf16[288,768]{1,0:T(8,128)(2,1)S(1)}, bf16[288,768]{1,0:T(8,128)(2,1)S(1)}, u32[]{:S(2)}, u32[]{:S(2)}) %collective-permute-start.17) | collective-permute-done | bytes 442400 | tf_op jit(solution)/shard_map/ppermute | solution.py:389
  169.6 0.9 add_convert_fusion
  (64 shorter events, 0.4 us)
Async XLA Ops:
  0.6 8.7 %copy-start.26 = (bf16[6,3,384]{2,1,0:T(4,128)(2,1)S(1)}, bf16[6,3,384]{2,1,0:T(4,128)(2,1)}, u32[]{:S(2)}) copy-start(bf16[6,3,384]{2,1,0:T(4,128)(2,1)} %param.9) | copy-start | bytes 41476
  0.6 8.7 %copy-start.27 = (bf16[6,384]{1,0:T(8,128)(2,1)S(1)}, bf16[6,384]{1,0:T(8,128)(2,1)}, u32[]{:S(2)}) copy-start(bf16[6,384]{1,0:T(8,128)(2,1)} %param.10) | copy-start | bytes 13828
  2.8 50.8 %copy-start = (bf16[288,1664]{1,0:T(8,128)(2,1)}, bf16[288,1664]{1,0:T(8,128)(2,1)S(1)}, u32[]{:S(2)}) copy-start(bf16[288,1664]{1,0:T(8,128)(2,1)S(1)} %pad_maximum_fusion.1.own) | copy-start | bytes 2875396
  2.8 45.2 %collective-permute-start = (bf16[288,1664]{1,0:T(8,128)(2,1)S(1)}, bf16[288,1664]{1,0:T(8,128)(2,1)S(1)}, u32[]{:S(2)}, u32[]{:S(2)}) collective-permute-start(bf16[288,1664]{1,0:T(8,128)(2,1)S(1)} %pad_maximum_fusion.1.own), channel_id=1, source_target_pairs={{0,32},{32,64},{64,96},{96,128},{128,160},{160,192},{192,224},{224... | collective-permute-start | bytes 2875400 | tf_op jit(solution)/shard_map/ppermute | solution.py:262
  4.7 43.3 %collective-permute-start.1 = (bf16[288,1664]{1,0:T(8,128)(2,1)S(1)}, bf16[288,1664]{1,0:T(8,128)(2,1)S(1)}, u32[]{:S(2)}, u32[]{:S(2)}) collective-permute-start(bf16[288,1664]{1,0:T(8,128)(2,1)S(1)} %pad_maximum_fusion.1.own), channel_id=1, source_target_pairs={{32,0},{64,32},{96,64},{128,96},{160,128},{192,160},{224,192},{256... | collective-permute-start | bytes 2875400 | tf_op jit(solution)/shard_map/ppermute | solution.py:263
  48.0 9.0 %copy-start.25 = (bf16[96,1536]{1,0:T(8,128)(2,1)S(1)}, bf16[96,1536]{1,0:T(8,128)(2,1)}, u32[]{:S(2)}) copy-start(bf16[96,1536]{1,0:T(8,128)(2,1)} %reshape.42) | copy-start | bytes 884740
  48.0 9.0 %copy-start.2 = (bf16[288,1664]{1,0:T(8,128)(2,1)}, bf16[288,1664]{1,0:T(8,128)(2,1)S(1)}, u32[]{:S(2)}) copy-start(bf16[288,1664]{1,0:T(8,128)(2,1)S(1)} %collective-permute-done.up) | copy-start | bytes 2875396
  48.0 2.5 %copy-start.4 = (bf16[288,1664]{1,0:T(8,128)(2,1)}, bf16[288,1664]{1,0:T(8,128)(2,1)S(1)}, u32[]{:S(2)}) copy-start(bf16[288,1664]{1,0:T(8,128)(2,1)S(1)} %collective-permute-done.1.down) | copy-start | bytes 2875396
  48.0 9.0 %collective-permute-start.2 = (bf16[96,1536]{1,0:T(8,128)(2,1)}, bf16[96,1536]{1,0:T(8,128)(2,1)S(1)}, u32[]{:S(2)}, u32[]{:S(2)}) collective-permute-start(bf16[96,1536]{1,0:T(8,128)(2,1)} %reshape.42), channel_id=1, source_target_pairs={{0,64},{32,96},{64,0},{96,32},{128,192},{160,224},{192,128},{224,1... | collective-permute-start | bytes 884744 | tf_op jit(solution)/shard_map/ppermute | solution.py:279
  57.1 28.2 %collective-permute-start.4 = (bf16[288,1664]{1,0:T(8,128)(2,1)}, bf16[288,1664]{1,0:T(8,128)(2,1)S(1)}, u32[]{:S(2)}, u32[]{:S(2)}) collective-permute-start(bf16[288,1664]{1,0:T(8,128)(2,1)} %get-tuple-element.38), channel_id=1, source_target_pairs={{2,0},{4,2},{6,4},{8,6},{10,8},{12,10},{14,12},{16,14},{18,16},{20... | collective-permute-start | bytes 2875400 | tf_op jit(solution)/shard_map/ppermute | solution.py:269
  58.4 14.9 %collective-permute-start.6 = (bf16[192,1536]{1,0:T(8,128)(2,1)S(1)}, bf16[192,1536]{1,0:T(8,128)(2,1)S(1)}, u32[]{:S(2)}, u32[]{:S(2)}) collective-permute-start(bf16[192,1536]{1,0:T(8,128)(2,1)S(1)} %pad_maximum_fusion.3), channel_id=1, source_target_pairs={{0,128},{32,160},{64,192},{96,224},{128,256},{160,288},{192,320},{... | collective-permute-start | bytes 1769480 | tf_op jit(solution)/shard_map/ppermute | solution.py:283
  60.3 16.6 %collective-permute-start.7 = (bf16[192,1536]{1,0:T(8,128)(2,1)S(1)}, bf16[192,1536]{1,0:T(8,128)(2,1)}, u32[]{:S(2)}, u32[]{:S(2)}) collective-permute-start(bf16[192,1536]{1,0:T(8,128)(2,1)S(1)} %pad_maximum_fusion.3), channel_id=1, source_target_pairs={{0,384},{32,416},{64,448},{96,480},{128,0},{160,32},{192,64},{224,... | collective-permute-start | bytes 1769480 | tf_op jit(solution)/shard_map/ppermute | solution.py:283
  64.2 22.2 %collective-permute-start.3 = (bf16[288,1664]{1,0:T(8,128)(2,1)}, bf16[288,1664]{1,0:T(8,128)(2,1)S(1)}, u32[]{:S(2)}, u32[]{:S(2)}) collective-permute-start(bf16[288,1664]{1,0:T(8,128)(2,1)} %get-tuple-element.37), channel_id=1, source_target_pairs={{0,2},{2,4},{4,6},{6,8},{8,10},{10,12},{12,14},{14,16},{16,18},{18... | collective-permute-start | bytes 2875400 | tf_op jit(solution)/shard_map/ppermute | solution.py:268
  74.0 9.3 %collective-permute-start.8 = (bf16[96,1536]{1,0:T(8,128)(2,1)}, bf16[96,1536]{1,0:T(8,128)(2,1)S(1)}, u32[]{:S(2)}, u32[]{:S(2)}) collective-permute-start(bf16[96,1536]{1,0:T(8,128)(2,1)} %slice.32), channel_id=1, source_target_pairs={{0,128},{32,160},{64,192},{96,224},{128,256},{160,288},{192,320},{... | collective-permute-start | bytes 884744 | tf_op jit(solution)/shard_map/ppermute | solution.py:283
  77.9 12.0 %collective-permute-start.9 = (bf16[96,1536]{1,0:T(8,128)(2,1)S(1)}, bf16[96,1536]{1,0:T(8,128)(2,1)S(1)}, u32[]{:S(2)}, u32[]{:S(2)}) collective-permute-start(bf16[96,1536]{1,0:T(8,128)(2,1)S(1)} %slice.33), channel_id=1, source_target_pairs={{0,384},{32,416},{64,448},{96,480},{128,0},{160,32},{192,64},{224,... | collective-permute-start | bytes 884744 | tf_op jit(solution)/shard_map/ppermute | solution.py:283
  83.4 11.3 %collective-permute-start.10 = (bf16[576,1536]{1,0:T(8,128)(2,1)}, bf16[576,1536]{1,0:T(8,128)(2,1)}, u32[]{:S(2)}, u32[]{:S(2)}) collective-permute-start(bf16[576,1536]{1,0:T(8,128)(2,1)} %pad_maximum_fusion.rest_0_), channel_id=1, source_target_pairs={{0,32},{32,0},{64,96},{96,64},{128,160},{160,128},{192,224},{224,1... | collective-permute-start | bytes 5308424 | tf_op jit(solution)/shard_map/ppermute | solution.py:279
  85.3 1.0 copy-start.24
  86.4 5.7 %copy-start.28 = (f32[384]{0:T(512)S(1)}, f32[384]{0:T(512)}, u32[]{:S(2)}) copy-start(f32[384]{0:T(512)} %param.11) | copy-start | bytes 4612
  86.4 5.7 %copy-start.29 = (f32[384]{0:T(512)S(1)}, f32[384]{0:T(512)}, u32[]{:S(2)}) copy-start(f32[384]{0:T(512)} %param.12) | copy-start | bytes 4612
  86.4 8.3 %copy-start.10 = (bf16[1,2,144,1536]{3,2,1,0:T(8,128)(2,1)S(1)}, bf16[1,2,144,1536]{3,2,1,0:T(8,128)(2,1)}, u32[]{:S(2)}) copy-start(bf16[1,2,144,1536]{3,2,1,0:T(8,128)(2,1)} %param.8) | copy-start | bytes 2654212
  86.4 3.6 %copy-start.6 = (bf16[288,1664]{1,0:T(8,128)(2,1)}, bf16[288,1664]{1,0:T(8,128)(2,1)S(1)}, u32[]{:S(2)}) copy-start(bf16[288,1664]{1,0:T(8,128)(2,1)S(1)} %collective-permute-done.3.left) | copy-start | bytes 2875396
  87.5 7.2 %collective-permute-start.5 = (bf16[288,1664]{1,0:T(8,128)(2,1)}, bf16[288,1664]{1,0:T(8,128)(2,1)}, u32[]{:S(2)}, u32[]{:S(2)}) collective-permute-start(bf16[288,1664]{1,0:T(8,128)(2,1)} %pad_maximum_fusion.2), channel_id=1, source_target_pairs={{0,32},{32,0},{64,96},{96,64},{128,160},{160,128},{192,224},{224,1... | collective-permute-start | bytes 2875400 | tf_op jit(solution)/shard_map/ppermute | solution.py:279
  90.0 3.9 %collective-permute-start.11 = (bf16[192,1536]{1,0:T(8,128)(2,1)S(1)}, bf16[192,1536]{1,0:T(8,128)(2,1)S(1)}, u32[]{:S(2)}, u32[]{:S(2)}) collective-permute-start(bf16[192,1536]{1,0:T(8,128)(2,1)S(1)} %constant_dynamic-update-slice_fusion.rest_1_), channel_id=1, source_target_pairs={{0,32},{32,0},{64,96},{96,64},{128,160},{160,128},{192,224},{224,1... | collective-permute-start | bytes 1769480 | tf_op jit(solution)/shard_map/ppermute | solution.py:279
  93.9 0.8 copy-start.13
  94.7 1.1 copy-start.14
  109.9 0.7 copy-start.21
  110.6 12.3 %copy-start.11 = (bf16[288,384]{1,0:T(8,128)(2,1)}, bf16[288,384]{1,0:T(8,128)(2,1)S(1)}, u32[]{:S(2)}) copy-start(bf16[288,384]{1,0:T(8,128)(2,1)S(1)} %get-tuple-element.42) | copy-start | bytes 663556
  110.6 12.3 %copy-start.15 = (f32[288,384]{1,0:T(8,128)}, f32[288,384]{1,0:T(8,128)S(1)}, u32[]{:S(2)}) copy-start(f32[288,384]{1,0:T(8,128)S(1)} %get-tuple-element.58.k_raw) | copy-start | bytes 1327108
  110.6 12.3 %copy-start.17 = (bf16[288,384]{1,0:T(8,128)(2,1)}, bf16[288,384]{1,0:T(8,128)(2,1)S(1)}, u32[]{:S(2)}) copy-start(bf16[288,384]{1,0:T(8,128)(2,1)S(1)} %get-tuple-element.55.keys) | copy-start | bytes 663556
  110.6 12.3 %copy-start.19 = (bf16[288,384]{1,0:T(8,128)(2,1)}, bf16[288,384]{1,0:T(8,128)(2,1)S(1)}, u32[]{:S(2)}) copy-start(bf16[288,384]{1,0:T(8,128)(2,1)S(1)} %get-tuple-element.56.values) | copy-start | bytes 663556
  110.6 9.0 %collective-permute-start.12 = (bf16[288,512]{1,0:T(8,128)(2,1)S(1)}, bf16[288,512]{1,0:T(8,128)(2,1)S(1)}, u32[]{:S(2)}, u32[]{:S(2)}) collective-permute-start(bf16[288,512]{1,0:T(8,128)(2,1)S(1)} %get-tuple-element.44.own), channel_id=1, source_target_pairs={{0,32},{32,64},{64,96},{96,128},{128,160},{160,192},{192,224},{224... | collective-permute-start | bytes 884744 | tf_op jit(solution)/shard_map/ppermute | solution.py:262
  112.7 8.6 %collective-permute-start.13 = (bf16[288,512]{1,0:T(8,128)(2,1)S(1)}, bf16[288,512]{1,0:T(8,128)(2,1)S(1)}, u32[]{:S(2)}, u32[]{:S(2)}) collective-permute-start(bf16[288,512]{1,0:T(8,128)(2,1)S(1)} %get-tuple-element.44.own), channel_id=1, source_target_pairs={{32,0},{64,32},{96,64},{128,96},{160,128},{192,160},{224,192},{256... | collective-permute-start | bytes 884744 | tf_op jit(solution)/shard_map/ppermute | solution.py:263
  117.1 18.8 %copy-start.1 = (bf16[288,1664]{1,0:T(8,128)(2,1)S(1)}, bf16[288,1664]{1,0:T(8,128)(2,1)}, u32[]{:S(2)}) copy-start(bf16[288,1664]{1,0:T(8,128)(2,1)} %copy-done) | copy-start | bytes 2875396
  117.2 18.8 %copy-start.3 = (bf16[288,1664]{1,0:T(8,128)(2,1)S(1)}, bf16[288,1664]{1,0:T(8,128)(2,1)}, u32[]{:S(2)}) copy-start(bf16[288,1664]{1,0:T(8,128)(2,1)} %copy-done.2) | copy-start | bytes 2875396
  117.2 18.8 %copy-start.5 = (bf16[288,1664]{1,0:T(8,128)(2,1)S(1)}, bf16[288,1664]{1,0:T(8,128)(2,1)}, u32[]{:S(2)}) copy-start(bf16[288,1664]{1,0:T(8,128)(2,1)} %copy-done.4) | copy-start | bytes 2875396
  121.4 0.7 copy-start.8
  122.9 21.8 %collective-permute-start.16 = (bf16[432,512]{1,0:T(8,128)(2,1)}, bf16[432,512]{1,0:T(8,128)(2,1)}, u32[]{:S(2)}, u32[]{:S(2)}) collective-permute-start(bf16[432,512]{1,0:T(8,128)(2,1)} %pad_maximum_fusion.5), channel_id=1, source_target_pairs={{2,0},{4,2},{6,4},{8,6},{10,8},{12,10},{14,12},{16,14},{18,16},{20... | collective-permute-start | bytes 1327112 | tf_op jit(solution)/shard_map/ppermute | solution.py:269
  125.0 19.7 %collective-permute-start.15 = (bf16[432,512]{1,0:T(8,128)(2,1)}, bf16[432,512]{1,0:T(8,128)(2,1)}, u32[]{:S(2)}, u32[]{:S(2)}) collective-permute-start(bf16[432,512]{1,0:T(8,128)(2,1)} %pad_maximum_fusion.4), channel_id=1, source_target_pairs={{0,2},{2,4},{4,6},{6,8},{8,10},{10,12},{12,14},{14,16},{16,18},{18... | collective-permute-start | bytes 1327112 | tf_op jit(solution)/shard_map/ppermute | solution.py:268
  131.0 26.0 %collective-permute-start.14 = (bf16[288,768]{1,0:T(8,128)(2,1)}, bf16[288,768]{1,0:T(8,128)(2,1)S(1)}, u32[]{:S(2)}, u32[]{:S(2)}) collective-permute-start(bf16[288,768]{1,0:T(8,128)(2,1)} %convolution_convert_fusion), channel_id=1, source_target_pairs={{0,1},{1,0},{2,3},{3,2},{4,5},{5,4},{6,7},{7,6},{8,9},{9,8},{10,11... | collective-permute-start | bytes 1327112 | tf_op jit(solution)/shard_map/ppermute | solution.py:389
  135.9 1.2 copy-start.7
  137.1 7.6 %copy-start.9 = (bf16[288,512]{1,0:T(8,128)(2,1)S(1)}, bf16[288,512]{1,0:T(8,128)(2,1)}, u32[]{:S(2)}) copy-start(bf16[288,512]{1,0:T(8,128)(2,1)} %copy-done.8) | copy-start | bytes 884740
  137.1 7.6 %copy-start.16 = (f32[288,384]{1,0:T(8,128)S(1)}, f32[288,384]{1,0:T(8,128)}, u32[]{:S(2)}) copy-start(f32[288,384]{1,0:T(8,128)} %copy-done.15) | copy-start | bytes 1327108
  137.1 7.6 %copy-start.18 = (bf16[288,384]{1,0:T(8,128)(2,1)S(1)}, bf16[288,384]{1,0:T(8,128)(2,1)}, u32[]{:S(2)}) copy-start(bf16[288,384]{1,0:T(8,128)(2,1)} %copy-done.17) | copy-start | bytes 663556
  137.1 7.6 %copy-start.20 = (bf16[288,384]{1,0:T(8,128)(2,1)S(1)}, bf16[288,384]{1,0:T(8,128)(2,1)}, u32[]{:S(2)}) copy-start(bf16[288,384]{1,0:T(8,128)(2,1)} %copy-done.19) | copy-start | bytes 663556
  137.1 7.6 %copy-start.22 = (bf16[288,384]{1,0:T(8,128)(2,1)S(1)}, bf16[288,384]{1,0:T(8,128)(2,1)}, u32[]{:S(2)}) copy-start(bf16[288,384]{1,0:T(8,128)(2,1)} %copy-done.21) | copy-start | bytes 663556
  144.8 11.3 %copy-start.23 = (bf16[1536,1536]{1,0:T(8,128)(2,1)S(1)}, bf16[1536,1536]{1,0:T(8,128)(2,1)}, u32[]{:S(2)}) copy-start(bf16[1536,1536]{1,0:T(8,128)(2,1)} %get-tuple-element.43.whole) | copy-start | bytes 14155780
  153.5 16.1 %collective-permute-start.17 = (bf16[288,768]{1,0:T(8,128)(2,1)S(1)}, bf16[288,768]{1,0:T(8,128)(2,1)S(1)}, u32[]{:S(2)}, u32[]{:S(2)}) collective-permute-start(bf16[288,768]{1,0:T(8,128)(2,1)S(1)} %get-tuple-element.61), channel_id=1, source_target_pairs={{0,1},{1,0},{2,3},{3,2},{4,5},{5,4},{6,7},{7,6},{8,9},{9,8},{10,11... | collective-permute-start | bytes 1327112 | tf_op jit(solution)/shard_map/ppermute | solution.py:389
  156.1 0.9 copy-start.12
